TPU v7x, 32 devices: a whole 2x2x4 slice. The times are simulated.
32 devices in a mesh: chain: 8 (over z, core), grp: 4 (over y, x).
Axes of the slice: x: 2, y: 2, z: 4, core: 2. Of those that a mesh axis runs over, the one named last changes fastest.
Arguments:
- query_raw: bfloat16 [4096, 4096], P(('chain', 'grp')), may hold values from -6 to 6
- key_raw: bfloat16 [4096, 4096], P(('chain', 'grp')), may hold values from -6 to 6
- value_raw: bfloat16 [4096, 4096], P(('chain', 'grp')), may hold values from -6 to 6
- grad_out: bfloat16 [4096, 4096], P(('chain', 'grp')), may hold values from -6 to 6
- query_kernel: bfloat16 [4, 4096], replicated, may hold values from -3 to 3
- key_kernel: bfloat16 [4, 4096], replicated, may hold values from -3 to 3
- value_kernel: bfloat16 [4, 4096], replicated, may hold values from -3 to 3
Outputs:
- query_grad: bfloat16 [4096, 4096], P(('chain', 'grp'))
- key_grad: bfloat16 [4096, 4096], P(('chain', 'grp'))
- value_grad: bfloat16 [4096, 4096], P(('chain', 'grp'))
All inputs are finite; a program needn't handle non-finite values.
Results may differ from a plain program's by a relative error of at most 0.011.
Values may be sent and summed in bfloat16 or wider, within the bound.
No kernel may reach another device: no remote copies, remote signals or barrier semaphores. Data moves between devices by JAX's collectives and lax.ppermute only.
A program may use at most 128 MiB of HBM per device.

v0:
```python
import jax
import jax.numpy as jnp
from jax import lax
from jax.sharding import PartitionSpec as P

HEAD = 128
BLOCK = 1024
KERNEL = 4


def entering(value, axis, join, neutral, backward):
    count = lax.axis_size(axis)
    place = lax.axis_index(axis)
    ahead = count - 1 - place if backward else place
    gathered = lax.all_gather(value.astype(jnp.bfloat16), axis)
    state = jnp.zeros_like(value) + jnp.asarray(neutral, value.dtype)

    def one(hop, state):
        source = count - 1 - hop if backward else hop
        return join(state, lax.dynamic_index_in_dim(gathered, source, 0, False).astype(value.dtype))

    return lax.fori_loop(0, ahead, one, state)


def extended_2(value, sides, width):
    for axis, dim in sides:
        peers, length = (lax.axis_size(axis), value.shape[dim])
        up = [(i, (i + 1) % peers) for i in range(peers - 1)]
        down = [(j, i) for i, j in up]
        last = lax.slice_in_dim(value, length - width, length, axis=dim)
        leading = lax.slice_in_dim(value, 0, width, axis=dim)
        before = lax.ppermute(last, axis, up)
        after = lax.ppermute(leading, axis, down)
        value = jnp.concatenate([before, value, after], axis=dim)
    return value


def add_pair(first, second):
    return first + second


def chain_scans(state_own, grad_own):
    zeros = jnp.zeros_like(state_own)
    before = entering(state_own, "chain", add_pair, zeros, False)
    after = entering(grad_own, "chain", add_pair, zeros, True)
    return (before, after)


def local_grads(extended, kernels, scale, sum_states):
    reach = KERNEL - 1
    rows = extended.shape[1] - 2 * reach
    width = extended.shape[2]
    heads = width // HEAD
    inputs = extended[:3].astype(jnp.float32)
    mixed = kernels[:, 0][:, None, :] * inputs[:, reach : reach + rows + reach]
    for offset in range(1, KERNEL):
        mixed = (
            mixed
            + kernels[:, offset][:, None, :]
            * inputs[:, reach - offset : reach - offset + rows + reach]
        )
    features = mixed.astype(jnp.bfloat16)
    upstream = extended[3, reach:]
    span = min(BLOCK, rows)
    blocks = rows // span

    def split(field):
        return field.reshape(blocks, span, heads, HEAD)

    queries = split(features[0, :rows])
    keys = split(features[1, :rows])
    values = split(features[2, :rows])
    cotangent = split(upstream[:rows])
    state_blocks = jnp.einsum("bshd,bshe->bhde", keys, values, preferred_element_type=jnp.float32)
    grad_blocks = jnp.einsum(
        "bshd,bshe->bhde", queries, cotangent, preferred_element_type=jnp.float32
    )
    state_own = jnp.sum(state_blocks, 0)
    grad_own = jnp.sum(grad_blocks, 0)
    before, after = sum_states(state_own, grad_own)
    state_prev = (before[None] + jnp.cumsum(state_blocks, 0) - state_blocks).astype(jnp.bfloat16)
    grad_next = (after[None] + grad_own[None] - jnp.cumsum(grad_blocks, 0)).astype(jnp.bfloat16)
    lower = jnp.arange(span)[:, None] >= jnp.arange(span)[None, :]

    def block_grads(packed):
        query_block, key_block, value_block, cot_block, state_block, next_block = packed
        scores = jnp.einsum(
            "rhe,che->hrc", cot_block, value_block, preferred_element_type=jnp.float32
        )
        masked = jnp.where(lower[None], scores, 0.0).astype(jnp.bfloat16)
        similar = jnp.einsum(
            "rhd,chd->hrc", query_block, key_block, preferred_element_type=jnp.float32
        )
        masked_sim = jnp.where(lower[None], similar, 0.0).astype(jnp.bfloat16)
        query_part = jnp.einsum(
            "hrc,chd->rhd", masked, key_block, preferred_element_type=jnp.float32
        )
        query_part = query_part + jnp.einsum(
            "rhe,hde->rhd", cot_block, state_block, preferred_element_type=jnp.float32
        )
        key_part = jnp.einsum(
            "hrc,rhd->chd", masked, query_block, preferred_element_type=jnp.float32
        )
        key_part = key_part + jnp.einsum(
            "che,hde->chd", value_block, next_block, preferred_element_type=jnp.float32
        )
        value_part = jnp.einsum(
            "hrc,rhe->che", masked_sim, cot_block, preferred_element_type=jnp.float32
        )
        value_part = value_part + jnp.einsum(
            "chd,hde->che", key_block, next_block, preferred_element_type=jnp.float32
        )
        return jnp.stack([query_part, key_part, value_part])

    grads = lax.map(block_grads, (queries, keys, values, cotangent, state_prev, grad_next))
    grads = grads.transpose(1, 0, 2, 3, 4).reshape(3, rows, width)
    highest = lax.Precision.HIGHEST
    edge_query = features[0, rows:].reshape(reach, heads, HEAD).astype(jnp.float32)
    edge_key = features[1, rows:].reshape(reach, heads, HEAD).astype(jnp.float32)
    edge_value = features[2, rows:].reshape(reach, heads, HEAD).astype(jnp.float32)
    edge_cot = upstream[rows:].reshape(reach, heads, HEAD).astype(jnp.float32)
    state_end = before + state_own
    small_lower = (jnp.arange(reach)[:, None] >= jnp.arange(reach)[None, :])[None]
    small_strict = (jnp.arange(reach)[:, None] < jnp.arange(reach)[None, :])[None]
    edge_scores = jnp.einsum("rhe,che->hrc", edge_cot, edge_value, precision=highest)
    edge_similar = jnp.einsum("rhd,chd->hrc", edge_query, edge_key, precision=highest)
    edge_qgrad = jnp.einsum(
        "hrc,chd->rhd", jnp.where(small_lower, edge_scores, 0.0), edge_key, precision=highest
    )
    edge_qgrad = edge_qgrad + jnp.einsum("rhe,hde->rhd", edge_cot, state_end, precision=highest)
    edge_kgrad = jnp.einsum("che,hde->chd", edge_value, after, precision=highest)
    edge_kgrad = edge_kgrad - jnp.einsum(
        "hrc,rhd->chd", jnp.where(small_strict, edge_scores, 0.0), edge_query, precision=highest
    )
    edge_vgrad = jnp.einsum("chd,hde->che", edge_key, after, precision=highest)
    edge_vgrad = edge_vgrad - jnp.einsum(
        "hrc,rhe->che", jnp.where(small_strict, edge_similar, 0.0), edge_cot, precision=highest
    )
    edge_grads = jnp.stack([edge_qgrad, edge_kgrad, edge_vgrad]).reshape(3, reach, width)
    total_grad = jnp.concatenate([grads, edge_grads], 1) * scale
    result = kernels[:, 0][:, None, :] * total_grad[:, :rows]
    for offset in range(1, KERNEL):
        result = result + kernels[:, offset][:, None, :] * total_grad[:, offset : offset + rows]
    result = result.astype(jnp.bfloat16)
    return (result[0], result[1], result[2])


def local(query_raw, key_raw, value_raw, grad_out, query_kernel, key_kernel, value_kernel):
    tok_rows = query_raw.shape[0]
    scale = float(HEAD * tok_rows * lax.axis_size("chain") * lax.axis_size("grp")) ** (-0.5)
    kernels = jnp.stack([query_kernel, key_kernel, value_kernel]).astype(jnp.float32)
    moved = (
        lax.all_to_all(query_raw, "grp", split_axis=1, concat_axis=0, tiled=True),
        lax.all_to_all(key_raw, "grp", split_axis=1, concat_axis=0, tiled=True),
        lax.all_to_all(value_raw, "grp", split_axis=1, concat_axis=0, tiled=True),
        lax.all_to_all(grad_out, "grp", split_axis=1, concat_axis=0, tiled=True),
    )
    width = moved[0].shape[1]
    local_taps = lax.dynamic_slice_in_dim(kernels, lax.axis_index("grp") * width, width, 2)
    extended = extended_2(jnp.stack(moved), (("chain", 1),), KERNEL - 1)
    first, second, third = local_grads(extended, local_taps, scale, chain_scans)
    return (
        lax.all_to_all(first, "grp", split_axis=0, concat_axis=1, tiled=True),
        lax.all_to_all(second, "grp", split_axis=0, concat_axis=1, tiled=True),
        lax.all_to_all(third, "grp", split_axis=0, concat_axis=1, tiled=True),
    )


def solution(mesh):
    placed = (
        P(("chain", "grp"), None),
        P(("chain", "grp"), None),
        P(("chain", "grp"), None),
        P(("chain", "grp"), None),
        P(),
        P(),
        P(),
    )
    return jax.shard_map(
        local,
        mesh=mesh,
        in_specs=placed,
        out_specs=(P(("chain", "grp"), None), P(("chain", "grp"), None), P(("chain", "grp"), None)),
        check_vma=False,
    )
```

profile of v0, /device:TPU:0, one launch (start us, length us, event | category | flops | bytes accessed | tf_op | source)
XLA Modules:
  0.0 268.9 jit_solution(10754607437516045673)
XLA Ops:
  7.2 2.4 copy.193
  9.5 5.2 %all-to-all-start.3 = ((bf16[128,4,1024]{2,0,1:T(8,128)(2,1)}), bf16[128,4,1024]{2,0,1:T(8,128)(2,1)S(1)}, u32[]{:S(2)}, u32[]{:S(2)}) async-start(bf16[128,4,1024]{2,0,1:T(8,128)(2,1)} %bitcast.120), calls=%async_computation.3 | async-start | bytes 2097152 | tf_op jit(solution)/shard_map/all_to_all | solution.py:156
  16.0 12.3 %all-to-all-done.3 = bf16[128,4,1024]{2,0,1:T(8,128)(2,1)S(1)} async-done(((bf16[128,4,1024]{2,0,1:T(8,128)(2,1)}), bf16[128,4,1024]{2,0,1:T(8,128)(2,1)S(1)}, u32[]{:S(2)}, u32[]{:S(2)}) %all-to-all-start.3) | async-done | bytes 1048608 | tf_op jit(solution)/shard_map/all_to_all | solution.py:156
  28.3 3.5 %all-to-all-start.2 = ((bf16[128,4,1024]{0,2,1:T(8,128)(2,1)}), bf16[128,4,1024]{0,2,1:T(8,128)(2,1)S(1)}, u32[]{:S(2)}, u32[]{:S(2)}) async-start(bf16[128,4,1024]{0,2,1:T(8,128)(2,1)} %bitcast.9), calls=%async_computation.2 | async-start | bytes 2097152 | tf_op jit(solution)/shard_map/all_to_all | solution.py:155
  31.9 2.3 copy.108
  34.2 10.8 %all-to-all-done.2 = bf16[128,4,1024]{0,2,1:T(8,128)(2,1)S(1)} async-done(((bf16[128,4,1024]{0,2,1:T(8,128)(2,1)}), bf16[128,4,1024]{0,2,1:T(8,128)(2,1)S(1)}, u32[]{:S(2)}, u32[]{:S(2)}) %all-to-all-start.2) | async-done | bytes 1048608 | tf_op jit(solution)/shard_map/all_to_all | solution.py:155
  44.9 3.5 %all-to-all-start.1 = ((bf16[128,4,1024]{0,2,1:T(8,128)(2,1)}), bf16[128,4,1024]{0,2,1:T(8,128)(2,1)S(1)}, u32[]{:S(2)}, u32[]{:S(2)}) async-start(bf16[128,4,1024]{0,2,1:T(8,128)(2,1)} %bitcast.145), calls=%async_computation.1 | async-start | bytes 2097152 | tf_op jit(solution)/shard_map/all_to_all | solution.py:154
  48.5 2.3 copy.106
  50.7 10.8 %all-to-all-done.1 = bf16[128,4,1024]{0,2,1:T(8,128)(2,1)S(1)} async-done(((bf16[128,4,1024]{0,2,1:T(8,128)(2,1)}), bf16[128,4,1024]{0,2,1:T(8,128)(2,1)S(1)}, u32[]{:S(2)}, u32[]{:S(2)}) %all-to-all-start.1) | async-done | bytes 1048608 | tf_op jit(solution)/shard_map/all_to_all | solution.py:154
  61.5 4.2 %all-to-all-start = ((bf16[128,4,1024]{0,2,1:T(8,128)(2,1)}), bf16[128,4,1024]{0,2,1:T(8,128)(2,1)}, u32[]{:S(2)}, u32[]{:S(2)}) async-start(bf16[128,4,1024]{0,2,1:T(8,128)(2,1)} %bitcast.144), calls=%async_computation | async-start | bytes 2097152 | tf_op jit(solution)/shard_map/all_to_all | solution.py:153
  66.5 1.8 copy.111
  68.3 1.5 stack.61
  69.8 3.0 %copy.109 = bf16[4,128,1024]{1,0,2:T(4,128)(2,1)} copy(bf16[4,128,1024]{1,2,0:T(8,128)(2,1)} %bitcast.143) | data formatting | bytes 2097152 | tf_op jit(solution)/shard_map/all_to_all | solution.py:154
  72.8 2.2 stack.60
  75.0 3.9 %all-to-all-done = bf16[128,4,1024]{0,2,1:T(8,128)(2,1)} async-done(((bf16[128,4,1024]{0,2,1:T(8,128)(2,1)}), bf16[128,4,1024]{0,2,1:T(8,128)(2,1)}, u32[]{:S(2)}, u32[]{:S(2)}) %all-to-all-start) | async-done | bytes 1048608 | tf_op jit(solution)/shard_map/all_to_all | solution.py:153
  78.9 3.0 %copy.107 = bf16[4,128,1024]{1,0,2:T(4,128)(2,1)} copy(bf16[4,128,1024]{1,2,0:T(8,128)(2,1)} %bitcast.6) | data formatting | bytes 2097152 | tf_op jit(solution)/shard_map/all_to_all | solution.py:153
  81.9 2.2 stack.59
  84.2 2.9 %pad_maximum_fusion.8 = (bf16[4,3,1024]{1,2,0:T(8,128)(2,1)}, bf16[4,3,1024]{1,2,0:T(8,128)(2,1)}) fusion(bf16[1,512,1024]{1,2,0:T(8,128)(2,1)S(1)} %copy.171, bf16[1,512,1024]{1,2,0:T(8,128)(2,1)S(1)} %stack.61, bf16[1,512,1024]{1,2,0:T(8,128)(2,1)} %stack.60, bf16[1,512,1024]{1,2,0:T(8,128)(2,1)} %stack.59), kind=kLoop, calls=%fused_computation.46 | loop fusion | flops 196608 | bytes 4243456 | tf_op jit(solution)/shard_map/slice | solution.py:30
  87.1 1.6 copy.115
  90.0 1.6 copy.114
  91.6 3.0 %collective-permute-start = (bf16[4,3,1024]{2,0,1:T(4,128)(2,1)S(1)}, bf16[4,3,1024]{2,0,1:T(4,128)(2,1)S(1)}, u32[]{:S(2)}, u32[]{:S(2)}) collective-permute-start(bf16[4,3,1024]{2,0,1:T(4,128)(2,1)S(1)} %copy.114), channel_id=1, source_target_pairs={{0,4},{4,8},{8,12},{12,16},{16,20},{20,24},{24,28},{1,5},{5,9},{9,... | collective-permute-start | bytes 73736 | tf_op jit(solution)/shard_map/ppermute | solution.py:32
  95.9 2.5 copy.130
  98.4 1.4 copy.117
  99.8 1.4 copy.116
  101.3 5.9 %fusion.12 = f32[3,518,1024]{1,2,0:T(8,128)S(1)} fusion(bf16[4,3,1024]{1,2,0:T(8,128)(2,1)} %copy.117, bf16[4,3,1024]{1,2,0:T(8,128)(2,1)} %copy.116, bf16[1,512,1024]{1,2,0:T(8,128)(2,1)S(1)} %copy.171, bf16[1,512,1024]{1,2,0:T(8,128)(2,1)S(1)} %stack.61, bf16[1,512,1024]{1,2,0:T(8,128)(2,1)S(1)} %copy-done.1, bf16[1,512,1024]{1,2,0:T(8,128)(2,1)} %stack.59), kind=kLoop, calls=%fused_computation.26 | loop fusion | flops 19095552 | bytes 10608640 | tf_op jit(solution)/shard_map/convert_element_type | solution.py:54
  107.2 8.9 %fusion.2 = bf16[3,515,1024]{1,2,0:T(8,128)(2,1)S(1)} fusion(f32[3,518,1024]{1,2,0:T(8,128)S(1)} %fusion.12, f32[3,1024]{1,0:T(4,128)S(1)} %get-tuple-element.149, f32[3,1024]{1,0:T(4,128)S(1)} %get-tuple-element.150, f32[3,1024]{1,0:T(4,128)S(1)} %get-tuple-element.151, f32[3,1024]{1,0:T(4,128)S(1)} %get-tuple-element.152), kind=kLoop, calls=%fused_computation.7 | loop fusion | flops 12656640 | bytes 28526592 | tf_op jit(solution)/shard_map/convert_element_type | solution.py:62
  120.5 2.0 fusion.38
  122.5 2.5 fusion.42
  127.9 2.6 fusion
  130.6 2.8 %fusion.44 = f32[8,128,512]{2,1,0:T(8,128)} fusion(bf16[512,8,128]{0,2,1:T(8,128)(2,1)S(1)} %bitcast.132, bf16[8,512,512]{1,2,0:T(8,128)(2,1)S(1)} %fusion), kind=kOutput, calls=%fused_computation.87 | convolution fusion | flops 536870912 | bytes 7340032 | tf_op jit(solution)/shard_map/while/body/eval_jaxpr/hrc,rhd->chd/dot_general | solution.py:101
  133.4 2.1 fusion.43
  135.5 13.6 %all-gather.7.cloned.1.call-done = bf16[64,128,128]{2,1,0:T(8,128)(2,1)} async-done(((bf16[8,128,128]{2,1,0:T(8,128)(2,1)}), bf16[64,128,128]{2,1,0:T(8,128)(2,1)}) %all-gather.7.cloned.1.call-update) | async-done | bytes 2097168 | tf_op jit(solution)/shard_map/all_gather | solution.py:15
  149.0 7.7 %while.27 = (s32[]{:T(128)}, f32[8,128,128]{2,1,0:T(8,128)S(1)}, s32[]{:T(128)}, bf16[8,8,128,128]{3,2,1,0:T(8,128)(2,1)}, s32[]{:T(128)}, /*index=5*/s32[]{:T(128)}, s32[]{:T(128)}, s32[]{:T(128)}) while((s32[]{:T(128)}, f32[8,128,128]{2,1,0:T(8,128)S(1)}, s32[]{:T(128)}, bf16[8,8,128,128]{3,2,1,0:T(8,128)(2,1)}, s32[]{:T(128)}, ...), condition=%wide.region_3.4_spmd, body=%wide.region_2.3_spmd.sunk | while | flops 262150 | bytes 1310863 | solution.py:22
  158.2 21.0 %all-gather.5.cloned.1.call-done = bf16[64,128,128]{2,1,0:T(8,128)(2,1)} async-done(((bf16[8,128,128]{2,1,0:T(8,128)(2,1)}), bf16[64,128,128]{2,1,0:T(8,128)(2,1)}) %all-gather.5.cloned.1.call-update) | async-done | bytes 2097168 | tf_op jit(solution)/shard_map/all_gather | solution.py:15
  179.5 1.6 fusion.17
  181.1 1.7 copy.148
  183.9 1.9 fusion.45
  185.8 6.0 %bitcast_add_fusion = f32[512,8,128]{0,2,1:T(8,128)} fusion(f32[8,128,512]{2,1,0:T(8,128)} %fusion.45, bf16[512,8,128]{0,2,1:T(8,128)(2,1)} %copy.130, pred[512,512]{0,1:T(8,128)(4,1)} %iota_compare_fusion, bf16[512,8,128]{0,2,1:T(8,128)(2,1)S(1)} %bitcast.133, bf16[512,8,128]{0,2,1:T(8,128)(2,1)S(1)} %bitcast.128), kind=kOutput, calls=%fused_computation.32 | convolution fusion | flops 1078460416 | bytes 7602176 | tf_op jit(solution)/shard_map/while/body/eval_jaxpr/hrc,rhe->che/dot_general | solution.py:107
  191.8 2.5 convolution_add_fusion
  197.7 7.8 %fusion.6 = bf16[3,512,1024]{1,2,0:T(8,128)(2,1)S(1)} fusion(f32[3,515,1024]{1,2,0:T(8,128)S(1)} %maximum_multiply_fusion, f32[3,1024]{1,0:T(4,128)S(1)} %get-tuple-element.149, f32[3,1024]{1,0:T(4,128)S(1)} %get-tuple-element.150, f32[3,1024]{1,0:T(4,128)S(1)} %get-tuple-element.151, f32[3,1024]{1,0:T(4,128)S(1)} %get-tuple-element.152), kind=kLoop, calls=%fused_computation.16 | loop fusion | flops 12582912 | bytes 28360704 | tf_op jit(solution)/shard_map/convert_element_type | solution.py:144
  207.0 3.6 %all-to-all-start.4 = ((bf16[4,128,1024]{2,1,0:T(8,128)(2,1)}), bf16[4,128,1024]{2,1,0:T(8,128)(2,1)S(1)}, u32[]{:S(2)}, u32[]{:S(2)}) async-start(bf16[4,128,1024]{2,1,0:T(8,128)(2,1)} %bitcast.35), calls=%async_computation.4 | async-start | bytes 2097152 | tf_op jit(solution)/shard_map/all_to_all | solution.py:163
  212.0 13.6 %all-to-all-done.4 = bf16[4,128,1024]{2,1,0:T(8,128)(2,1)S(1)} async-done(((bf16[4,128,1024]{2,1,0:T(8,128)(2,1)}), bf16[4,128,1024]{2,1,0:T(8,128)(2,1)S(1)}, u32[]{:S(2)}, u32[]{:S(2)}) %all-to-all-start.4) | async-done | bytes 1048608 | tf_op jit(solution)/shard_map/all_to_all | solution.py:163
  225.5 3.5 %all-to-all-start.5 = ((bf16[4,128,1024]{2,1,0:T(8,128)(2,1)}), bf16[4,128,1024]{2,1,0:T(8,128)(2,1)S(1)}, u32[]{:S(2)}, u32[]{:S(2)}) async-start(bf16[4,128,1024]{2,1,0:T(8,128)(2,1)} %bitcast.38), calls=%async_computation.5 | async-start | bytes 2097152 | tf_op jit(solution)/shard_map/all_to_all | solution.py:164
  229.0 1.4 copy.153
  230.4 12.8 %all-to-all-done.5 = bf16[4,128,1024]{2,1,0:T(8,128)(2,1)S(1)} async-done(((bf16[4,128,1024]{2,1,0:T(8,128)(2,1)}), bf16[4,128,1024]{2,1,0:T(8,128)(2,1)S(1)}, u32[]{:S(2)}, u32[]{:S(2)}) %all-to-all-start.5) | async-done | bytes 1048608 | tf_op jit(solution)/shard_map/all_to_all | solution.py:164
  243.2 3.5 %all-to-all-start.6 = ((bf16[4,128,1024]{2,1,0:T(8,128)(2,1)}), bf16[4,128,1024]{2,1,0:T(8,128)(2,1)S(1)}, u32[]{:S(2)}, u32[]{:S(2)}) async-start(bf16[4,128,1024]{2,1,0:T(8,128)(2,1)} %bitcast.41), calls=%async_computation.6 | async-start | bytes 2097152 | tf_op jit(solution)/shard_map/all_to_all | solution.py:165
  248.0 2.3 copy.155
  252.3 7.8 %all-to-all-done.6 = bf16[4,128,1024]{2,1,0:T(8,128)(2,1)S(1)} async-done(((bf16[4,128,1024]{2,1,0:T(8,128)(2,1)}), bf16[4,128,1024]{2,1,0:T(8,128)(2,1)S(1)}, u32[]{:S(2)}, u32[]{:S(2)}) %all-to-all-start.6) | async-done | bytes 1048608 | tf_op jit(solution)/shard_map/all_to_all | solution.py:165
  (79 shorter events, 33.7 us)
Async XLA Ops:
  7.2 7.5 %copy-start.11 = (bf16[128,4096]{1,0:T(8,128)(2,1)S(1)}, bf16[128,4096]{1,0:T(8,128)(2,1)}, u32[]{:S(2)}) copy-start(bf16[128,4096]{1,0:T(8,128)(2,1)} %param.13) | copy-start | bytes 3145732
  9.5 18.8 %all-to-all-start.3 = ((bf16[128,4,1024]{2,0,1:T(8,128)(2,1)}), bf16[128,4,1024]{2,0,1:T(8,128)(2,1)S(1)}, u32[]{:S(2)}, u32[]{:S(2)}) async-start(bf16[128,4,1024]{2,0,1:T(8,128)(2,1)} %bitcast.120), calls=%async_computation.3 | async-start | bytes 2097152 | tf_op jit(solution)/shard_map/all_to_all | solution.py:156
  28.3 16.6 %all-to-all-start.2 = ((bf16[128,4,1024]{0,2,1:T(8,128)(2,1)}), bf16[128,4,1024]{0,2,1:T(8,128)(2,1)S(1)}, u32[]{:S(2)}, u32[]{:S(2)}) async-start(bf16[128,4,1024]{0,2,1:T(8,128)(2,1)} %bitcast.9), calls=%async_computation.2 | async-start | bytes 2097152 | tf_op jit(solution)/shard_map/all_to_all | solution.py:155
  31.9 34.0 %copy-start.12 = (bf16[4,4096]{1,0:T(4,128)(2,1)S(1)}, bf16[4,4096]{1,0:T(4,128)(2,1)}, u32[]{:S(2)}) copy-start(bf16[4,4096]{1,0:T(4,128)(2,1)} %param.17) | copy-start | bytes 98308
  31.9 33.9 %copy-start.13 = (bf16[4,4096]{1,0:T(4,128)(2,1)S(1)}, bf16[4,4096]{1,0:T(4,128)(2,1)}, u32[]{:S(2)}) copy-start(bf16[4,4096]{1,0:T(4,128)(2,1)} %param.16) | copy-start | bytes 98308
  31.9 33.9 %copy-start.14 = (bf16[4,4096]{1,0:T(4,128)(2,1)S(1)}, bf16[4,4096]{1,0:T(4,128)(2,1)}, u32[]{:S(2)}) copy-start(bf16[4,4096]{1,0:T(4,128)(2,1)} %param.15) | copy-start | bytes 98308
  44.9 16.6 %all-to-all-start.1 = ((bf16[128,4,1024]{0,2,1:T(8,128)(2,1)}), bf16[128,4,1024]{0,2,1:T(8,128)(2,1)S(1)}, u32[]{:S(2)}, u32[]{:S(2)}) async-start(bf16[128,4,1024]{0,2,1:T(8,128)(2,1)} %bitcast.145), calls=%async_computation.1 | async-start | bytes 2097152 | tf_op jit(solution)/shard_map/all_to_all | solution.py:154
  61.5 4.4 %copy-start.7 = (bf16[128,4,1024]{0,2,1:T(8,128)(2,1)}, bf16[128,4,1024]{0,2,1:T(8,128)(2,1)S(1)}, u32[]{:S(2)}) copy-start(bf16[128,4,1024]{0,2,1:T(8,128)(2,1)S(1)} %all-to-all-done.1) | copy-start | bytes 3145732
  61.5 17.4 %all-to-all-start = ((bf16[128,4,1024]{0,2,1:T(8,128)(2,1)}), bf16[128,4,1024]{0,2,1:T(8,128)(2,1)}, u32[]{:S(2)}, u32[]{:S(2)}) async-start(bf16[128,4,1024]{0,2,1:T(8,128)(2,1)} %bitcast.144), calls=%async_computation | async-start | bytes 2097152 | tf_op jit(solution)/shard_map/all_to_all | solution.py:153
  65.8 83.2 %all-gather.7.cloned.1.call-start = ((), (), s32[]{:S(2)}) async-start(), calls=%async_computation.8 | async-start | bytes 2359296 | tf_op jit(solution)/shard_map/all_gather | solution.py:15
  88.7 9.7 %collective-permute-start.1 = (bf16[4,3,1024]{2,0,1:T(4,128)(2,1)S(1)}, bf16[4,3,1024]{2,0,1:T(4,128)(2,1)S(1)}, u32[]{:S(2)}, u32[]{:S(2)}) collective-permute-start(bf16[4,3,1024]{2,0,1:T(4,128)(2,1)S(1)} %copy.115), channel_id=1, source_target_pairs={{4,0},{8,4},{12,8},{16,12},{20,16},{24,20},{28,24},{5,1},{9,5},{13... | collective-permute-start | bytes 73736 | tf_op jit(solution)/shard_map/ppermute | solution.py:33
  91.6 8.2 %collective-permute-start = (bf16[4,3,1024]{2,0,1:T(4,128)(2,1)S(1)}, bf16[4,3,1024]{2,0,1:T(4,128)(2,1)S(1)}, u32[]{:S(2)}, u32[]{:S(2)}) collective-permute-start(bf16[4,3,1024]{2,0,1:T(4,128)(2,1)S(1)} %copy.114), channel_id=1, source_target_pairs={{0,4},{4,8},{8,12},{12,16},{16,20},{20,24},{24,28},{1,5},{5,9},{9,... | collective-permute-start | bytes 73736 | tf_op jit(solution)/shard_map/ppermute | solution.py:32
  95.9 5.4 %copy-start.1 = (bf16[1,512,1024]{1,2,0:T(8,128)(2,1)S(1)}, bf16[1,512,1024]{1,2,0:T(8,128)(2,1)}, u32[]{:S(2)}) copy-start(bf16[1,512,1024]{1,2,0:T(8,128)(2,1)} %stack.60) | copy-start | bytes 3145732
  116.1 3.3 %copy-start = (bf16[3,515,1024]{1,2,0:T(8,128)(2,1)}, bf16[3,515,1024]{1,2,0:T(8,128)(2,1)S(1)}, u32[]{:S(2)}) copy-start(bf16[3,515,1024]{1,2,0:T(8,128)(2,1)S(1)} %fusion.2) | copy-start | bytes 9492484
  116.1 2.0 copy-start.2
  119.4 59.8 %all-gather.5.cloned.1.call-start = ((), (), s32[]{:S(2)}) async-start(), calls=%async_computation.7 | async-start | bytes 2359296 | tf_op jit(solution)/shard_map/all_gather | solution.py:15
  135.4 21.3 %copy-start.9 = (bf16[1,3,1024]{1,2,0:T(8,128)(2,1)S(1)}, bf16[1,3,1024]{1,2,0:T(8,128)(2,1)}, u32[]{:S(2)}) copy-start(bf16[1,3,1024]{1,2,0:T(8,128)(2,1)} %get-tuple-element.135) | copy-start | bytes 18436
  135.5 21.8 %copy-start.8 = (bf16[1,3,1024]{1,2,0:T(8,128)(2,1)S(1)}, bf16[1,3,1024]{1,2,0:T(8,128)(2,1)}, u32[]{:S(2)}) copy-start(bf16[1,3,1024]{1,2,0:T(8,128)(2,1)} %get-tuple-element.136) | copy-start | bytes 18436
  191.8 2.5 copy-start.3
  191.8 2.9 %copy-start.4 = (f32[8,128,512]{2,1,0:T(8,128)S(1)}, f32[8,128,512]{2,1,0:T(8,128)}, u32[]{:S(2)}) copy-start(f32[8,128,512]{2,1,0:T(8,128)} %fusion.43) | copy-start | bytes 6291460
  191.8 2.9 %copy-start.6 = (f32[8,128,128]{2,1,0:T(8,128)S(1)}, f32[8,128,128]{2,1,0:T(8,128)}, u32[]{:S(2)}) copy-start(f32[8,128,128]{2,1,0:T(8,128)} %get-tuple-element.148) | copy-start | bytes 1572868
  194.7 1.4 copy-start.5
  194.7 2.1 copy-start.10
  207.0 18.5 %all-to-all-start.4 = ((bf16[4,128,1024]{2,1,0:T(8,128)(2,1)}), bf16[4,128,1024]{2,1,0:T(8,128)(2,1)S(1)}, u32[]{:S(2)}, u32[]{:S(2)}) async-start(bf16[4,128,1024]{2,1,0:T(8,128)(2,1)} %bitcast.35), calls=%async_computation.4 | async-start | bytes 2097152 | tf_op jit(solution)/shard_map/all_to_all | solution.py:163
  225.5 17.7 %all-to-all-start.5 = ((bf16[4,128,1024]{2,1,0:T(8,128)(2,1)}), bf16[4,128,1024]{2,1,0:T(8,128)(2,1)S(1)}, u32[]{:S(2)}, u32[]{:S(2)}) async-start(bf16[4,128,1024]{2,1,0:T(8,128)(2,1)} %bitcast.38), calls=%async_computation.5 | async-start | bytes 2097152 | tf_op jit(solution)/shard_map/all_to_all | solution.py:164
  243.2 16.8 %all-to-all-start.6 = ((bf16[4,128,1024]{2,1,0:T(8,128)(2,1)}), bf16[4,128,1024]{2,1,0:T(8,128)(2,1)S(1)}, u32[]{:S(2)}, u32[]{:S(2)}) async-start(bf16[4,128,1024]{2,1,0:T(8,128)(2,1)} %bitcast.41), calls=%async_computation.6 | async-start | bytes 2097152 | tf_op jit(solution)/shard_map/all_to_all | solution.py:165
Sparse Core Ops, SparseCore 0:
  119.5 29.4 all-gather.6
  150.6 28.5 all-gather.4
where the time goes:
time: 274 us; the launch traced here: 269 us
  waiting for transfers between devices  107 us (39%)
  local copies, waits for them, and re-layouts  51.9 us (19%)
  other arithmetic  35.9 us (13%)
  starting transfers between devices  31.7 us (12%)
  matrix products  28.3 us (10%)
  between operations  14.4 us (5%)
    all_gather x2, waiting for transfers between devices, entering(): gathered = lax.all_gather(value.astype(jnp.bfloat16), axis)  34.6 us
    unnamed x39, local copies, waits for them, and re-layouts  14.9 us
    all_to_all x1, waiting for transfers between devices, local(): lax.all_to_all(first, 'grp', split_axis=0, concat_axis=1, tiled=True)  13.6 us
    all_to_all x1, waiting for transfers between devices, local(): lax.all_to_all(second, 'grp', split_axis=0, concat_axis=1, tiled=True)  12.8 us
    all_to_all x1, waiting for transfers between devices, local(): lax.all_to_all(grad_out, 'grp', split_axis=1, concat_axis=0, tiled=True)  12.3 us
    all_to_all x1, waiting for transfers between devices, local(): lax.all_to_all(key_raw, 'grp', split_axis=1, concat_axis=0, tiled=True)  10.8 us
    all_to_all x1, waiting for transfers between devices, local(): lax.all_to_all(value_raw, 'grp', split_axis=1, concat_axis=0, tiled=True)  10.8 us
    convert_element_type x1, other arithmetic, local_grads(): features = mixed.astype(jnp.bfloat16)  8.88 us
  transfers between devices with their start and end apart: 11, of which 9 were waited for; matrix products, arithmetic and copies ran while one was open for 20% of the time, Pallas kernels for 0%

commit v1 on v0

v1 whole, which is shorter than its diff:
```python
import functools
import math

import jax
import jax.numpy as jnp
from jax import lax
from jax.experimental import pallas as pl
from jax.experimental.pallas import tpu as pltpu
from jax.sharding import Mesh, PartitionSpec as P

HEAD = 128
KERNEL = 4
REACH = KERNEL - 1
CORES = 2
PAD = 8
EDGE = 16
CHUNKS = 4
STEP_HEADS = 4

F32 = jnp.float32
BF16 = jnp.bfloat16


def dot(a, b, ca, cb):
    return lax.dot_general(a, b, (((ca,), (cb,)), ((), ())), preferred_element_type=F32)


def states_kernel(
    q_ref, k_ref, v_ref, g_ref, prev_ref, next_ref, tq_ref, tk_ref, tv_ref,
    qf_ref, kf_ref, vf_ref, ge_ref, s_ref, x_ref,
):
    rows, width = q_ref.shape
    ext = rows + EDGE
    prev = prev_ref[...].astype(F32)
    after = next_ref[...].astype(F32)
    parts = ((q_ref, tq_ref, qf_ref), (k_ref, tk_ref, kf_ref), (v_ref, tv_ref, vf_ref))
    for i, (raw, tap_ref, out) in enumerate(parts):
        taps = tap_ref[...].astype(F32)
        x_ref[i, PAD - REACH : PAD] = prev[REACH * i : REACH * (i + 1)]
        x_ref[i, PAD : PAD + rows] = raw[...].astype(F32)
        x_ref[i, PAD + rows :] = jnp.zeros((EDGE, width), F32)
        x_ref[i, PAD + rows : PAD + rows + REACH] = after[REACH * i : REACH * (i + 1)]
        mixed = taps[0:1] * x_ref[i, PAD : PAD + ext]
        for j in range(1, KERNEL):
            mixed = mixed + taps[j : j + 1] * x_ref[i, PAD - j : PAD - j + ext]
        out[...] = mixed.astype(BF16)
    edge = jnp.concatenate([after[REACH * 3 : REACH * 4], jnp.zeros((EDGE - REACH, width), F32)], 0)
    ge_ref[...] = edge.astype(BF16)
    for h in range(width // HEAD):
        col = slice(h * HEAD, (h + 1) * HEAD)
        s_ref[h, 0] = dot(vf_ref[:rows, col], kf_ref[:rows, col], 0, 0).astype(BF16)
        s_ref[h, 1] = dot(g_ref[:, col], qf_ref[:rows, col], 0, 0).astype(BF16)


def grads_kernel(
    scale, alias, qf_ref, kf_ref, vf_ref, g_ref, ge_ref, s_ref, tq_ref, tk_ref, tv_ref, *rest
):
    dq_ref, dk_ref, dv_ref, d_ref = rest[3:] if alias else rest
    rows, width = g_ref.shape
    ext = rows + EDGE

    def order(shape):
        return lax.broadcasted_iota(jnp.int32, shape, 0), lax.broadcasted_iota(jnp.int32, shape, 1)

    row, col = order((ext, rows))
    lower = row >= col
    row, col = order((rows, rows))
    upper = col >= row
    row, col = order((EDGE, EDGE))
    edge_lower = row >= col
    edge_strict = col < row
    for h in range(width // HEAD):
        c = slice(h * HEAD, (h + 1) * HEAD)
        q, qe = qf_ref[:rows, c], qf_ref[rows:, c]
        k, ke = kf_ref[:rows, c], kf_ref[rows:, c]
        v, ve = vf_ref[:rows, c], vf_ref[rows:, c]
        g, ge = g_ref[:, c], ge_ref[:, c]
        vk, gq = s_ref[h, 0], s_ref[h, 1]
        gx = jnp.concatenate([g, ge], 0)
        scores = jnp.where(lower, dot(gx, v, 1, 1), 0.0).astype(BF16)
        d_ref[0, :, c] = dot(
            jnp.concatenate([scores, gx], 1), jnp.concatenate([k, vk], 0), 1, 0
        )
        scores_e = jnp.where(edge_lower, dot(ge, ve, 1, 1), 0.0).astype(BF16)
        d_ref[0, rows:, c] += dot(scores_e, ke, 1, 0)
        scores_t = jnp.where(upper, dot(v, g, 1, 1), 0.0).astype(BF16)
        d_ref[1, :rows, c] = dot(
            jnp.concatenate([scores_t, v], 1), jnp.concatenate([q, gq], 0), 1, 0
        )
        strict = jnp.where(edge_strict, dot(ve, ge, 1, 1), 0.0).astype(BF16)
        d_ref[1, rows:, c] = dot(ve, gq, 1, 0) - dot(strict, qe, 1, 0)
        similar_t = jnp.where(upper, dot(k, q, 1, 1), 0.0).astype(BF16)
        d_ref[2, :rows, c] = dot(similar_t, g, 1, 0) + dot(k, gq, 1, 1)
        strict = jnp.where(edge_strict, dot(ke, qe, 1, 1), 0.0).astype(BF16)
        d_ref[2, rows:, c] = dot(ke, gq, 1, 1) - dot(strict, ge, 1, 0)
    for i, (tap_ref, out) in enumerate(((tq_ref, dq_ref), (tk_ref, dk_ref), (tv_ref, dv_ref))):
        taps = tap_ref[...].astype(F32) * scale
        total = taps[0:1] * d_ref[i, 0:rows]
        for j in range(1, KERNEL):
            total = total + taps[j : j + 1] * d_ref[i, j : j + rows]
        out[...] = total.astype(BF16)


def states_call(chunk, heads, raws, prev, after, taps):
    rows = raws[0].shape[0]
    step = min(STEP_HEADS, heads)
    steps, width = heads // step, step * HEAD
    first = chunk * steps

    def wide(n):
        return pl.BlockSpec((n, width), lambda i: (0, first + i))

    def out(n):
        return pl.BlockSpec((n, width), lambda i: (0, i))

    ext = rows + EDGE
    return pl.pallas_call(
        states_kernel,
        grid=(steps,),
        in_specs=[wide(rows)] * 4 + [wide(EDGE)] * 2 + [wide(KERNEL)] * 3,
        out_specs=[out(ext)] * 3
        + [out(EDGE), pl.BlockSpec((step, 2, HEAD, HEAD), lambda i: (i, 0, 0, 0))],
        out_shape=[jax.ShapeDtypeStruct((ext, heads * HEAD), BF16)] * 3
        + [
            jax.ShapeDtypeStruct((EDGE, heads * HEAD), BF16),
            jax.ShapeDtypeStruct((heads, 2, HEAD, HEAD), BF16),
        ],
        scratch_shapes=[pltpu.VMEM((3, PAD + ext, width), F32)],
        compiler_params=pltpu.CompilerParams(vmem_limit_bytes=32 * 1024 * 1024),
        cost_estimate=pl.CostEstimate(
            flops=4 * heads * rows * HEAD * HEAD + 24 * heads * rows * HEAD,
            bytes_accessed=2 * heads * HEAD * (7 * rows + 2 * HEAD + 96),
            transcendentals=0,
        ),
        name="states",
    )(*raws, prev, after, *taps)


def grads_call(chunk, heads, total_width, scale, feats, g, state, taps, outs):
    rows = g.shape[0]
    step = min(STEP_HEADS, heads)
    steps, width = heads // step, step * HEAD
    first = chunk * steps
    ext = rows + EDGE

    def wide(n):
        return pl.BlockSpec((n, width), lambda i: (0, first + i))

    def own(n):
        return pl.BlockSpec((n, width), lambda i: (0, i))

    alias = outs is not None
    specs = [own(ext)] * 3 + [wide(rows), own(EDGE)]
    specs += [pl.BlockSpec((step, 2, HEAD, HEAD), lambda i: (i, 0, 0, 0))] + [wide(KERNEL)] * 3
    args = [*feats[:3], g, feats[3], state, *taps]
    aliases = {}
    if alias:
        aliases = {len(args) + i: i for i in range(3)}
        specs += [pl.BlockSpec(memory_space=pl.ANY)] * 3
        args += list(outs)
    return pl.pallas_call(
        functools.partial(grads_kernel, scale, alias),
        grid=(steps,),
        in_specs=specs,
        out_specs=[wide(rows)] * 3,
        out_shape=[jax.ShapeDtypeStruct((rows, total_width), BF16)] * 3,
        input_output_aliases=aliases,
        scratch_shapes=[pltpu.VMEM((3, ext, width), F32)],
        compiler_params=pltpu.CompilerParams(vmem_limit_bytes=32 * 1024 * 1024),
        cost_estimate=pl.CostEstimate(
            flops=20 * heads * rows * HEAD * HEAD,
            bytes_accessed=2 * heads * HEAD * (7 * rows + 2 * HEAD + 96),
            transcendentals=0,
        ),
        name="grads",
    )(*args)


def plane_sums(states):
    wide = states.astype(F32)
    return jnp.sum(wide[:, :, 0], 0), jnp.sum(wide[:, :, 1], 0)


def plane_scan(own_kv, own_gq):
    planes = lax.axis_size("z")
    place = lax.axis_index("z")
    kv, gq = own_kv, own_gq
    half = 1
    while half < planes:
        high = (place // half) % 2 == 1
        payload = jnp.where(high, gq, kv).astype(BF16)
        got = []
        for k in range(half):
            pairs = []
            for base in range(0, planes, 2 * half):
                pairs += [
                    (base + half - 1, base + half + k),
                    (base + half, base + half - 1 - k),
                ]
            got.append(lax.ppermute(payload, "z", pairs).astype(F32))
        arrived = sum(got[1:], got[0])
        kv = kv + jnp.where(high, arrived, 0.0)
        gq = gq + jnp.where(high, 0.0, arrived)
        half *= 2
    return kv - own_kv, gq - own_gq


def member_states(states, before, after):
    wide = states.astype(F32)
    members = wide.shape[0]
    kv, gq = [], []
    run = before
    for m in range(members):
        kv.append(run)
        run = run + wide[m, :, 0]
    run = after
    for m in reversed(range(members)):
        gq.append(run)
        run = run + wide[m, :, 1]
    gq.reverse()
    return jnp.stack([jnp.stack(kv), jnp.stack(gq)], 2).astype(BF16)


def local(query_raw, key_raw, value_raw, grad_out, query_kernel, key_kernel, value_kernel):
    rows, total_width = query_raw.shape
    z, grp = lax.axis_size("z"), lax.axis_size("grp")
    devices = z * CORES * grp
    members = CORES * grp
    scale = float(HEAD * rows * devices) ** (-0.5)
    heads_all = total_width // HEAD
    chunks = math.gcd(CHUNKS, heads_all // members)
    heads = heads_all // chunks
    everyone = ("z", "core", "grp")
    plane = ("core", "grp")
    raws = (query_raw, key_raw, value_raw, grad_out)
    taps = (query_kernel, key_kernel, value_kernel)

    up = [(i, i + 1) for i in range(devices - 1)]
    down = [(i + 1, i) for i in range(devices - 1)]
    tail = jnp.concatenate([r[rows - REACH :] for r in raws[:3]], 0)
    tail = jnp.pad(tail, ((0, EDGE - 3 * REACH), (0, 0)))
    lead = jnp.concatenate([r[:REACH] for r in raws], 0)
    lead = jnp.pad(lead, ((0, EDGE - 4 * REACH), (0, 0)))
    prev = lax.ppermute(tail, everyone, up)
    after = lax.ppermute(lead, everyone, down)

    feats, states = [], []
    for c in range(chunks):
        *f, s = states_call(c, heads, raws, prev, after, taps)
        feats.append(f)
        states.append(lax.all_to_all(s, plane, 0, 0, tiled=True))
    backs = []
    for c in range(chunks):
        s = states[c].reshape(members, heads // members, 2, HEAD, HEAD)
        own_kv, own_gq = plane_sums(s)
        before, later = plane_scan(own_kv, own_gq)
        back = member_states(s, before, later).reshape(heads, 2, HEAD, HEAD)
        backs.append(lax.all_to_all(back, plane, 0, 0, tiled=True))
    outs = None
    for c in range(chunks):
        outs = grads_call(c, heads, total_width, scale, feats[c], grad_out, backs[c], taps, outs)
    return tuple(outs)


def solution(mesh):
    chain, grp = mesh.shape["chain"], mesh.shape["grp"]
    split = Mesh(mesh.devices.reshape(chain // CORES, CORES, grp), ("z", "core", "grp"))
    tokens = P(("z", "core", "grp"), None)
    return jax.shard_map(
        local,
        mesh=split,
        in_specs=(tokens,) * 4 + (P(),) * 3,
        out_specs=(tokens,) * 3,
        check_vma=False,
    )
```

time: 274 us -> 190 us (0.69)
  the two profiles are of different devices: /device:TPU:0 before, /device:TPU:19 now
where the time goes in v1:
time: 190 us; the launch traced here: 187 us
  starting transfers between devices  67.1 us (35%)
  other arithmetic  30.9 us (16%)
  waiting for transfers between devices  30 us (16%)
  Pallas kernels  29.5 us (16%)
  local copies, waits for them, and re-layouts  28.5 us (15%)
    unnamed x128, local copies, waits for them, and re-layouts  25.7 us
    ppermute x12, starting transfers between devices, plane_scan(): got.append(lax.ppermute(payload, 'z', pairs).astype(F32))  22.4 us
    pallas_call x4, Pallas kernels, grads_call(): pl.pallas_call(functools.partial(grads_kernel, scale, alias), grid=(steps...  21.6 us
    all_to_all x4, starting transfers between devices, local(): states.append(lax.all_to_all(s, plane, 0, 0, tiled=True))  19.4 us
    all_to_all x4, starting transfers between devices, local(): backs.append(lax.all_to_all(back, plane, 0, 0, tiled=True))  19.2 us
    all_to_all x4, waiting for transfers between devices, local(): states.append(lax.all_to_all(s, plane, 0, 0, tiled=True))  15.5 us
    unnamed x48, other arithmetic  15.2 us
    all_to_all x4, waiting for transfers between devices, local(): backs.append(lax.all_to_all(back, plane, 0, 0, tiled=True))  9.41 us
  transfers between devices with their start and end apart: 22, of which 7 were waited for; matrix products, arithmetic and copies ran while one was open for 16% of the time, Pallas kernels for 12%

profile of v1, /device:TPU:19, one launch (start us, length us, event | category | flops | bytes accessed | tf_op | source)
XLA Modules:
  0.0 187.4 jit_solution(9833366612749008626)
XLA Ops:
  3.5 2.2 %collective-permute-start.1 = (bf16[16,4096]{1,0:T(8,128)(2,1)S(1)}, bf16[16,4096]{1,0:T(8,128)(2,1)S(1)}, u32[]{:S(2)}, u32[]{:S(2)}) collective-permute-start(bf16[16,4096]{1,0:T(8,128)(2,1)S(1)} %fusion.11), channel_id=1, source_target_pairs={{1,0},{2,1},{3,2},{4,3},{5,4},{6,5},{7,6},{8,7},{9,8},{10,9},{11,1... | collective-permute-start | bytes 393224 | tf_op jit(solution)/shard_map/ppermute | solution.py:245
  5.8 4.0 %collective-permute-start = (bf16[16,4096]{1,0:T(8,128)(2,1)S(1)}, bf16[16,4096]{1,0:T(8,128)(2,1)S(1)}, u32[]{:S(2)}, u32[]{:S(2)}) collective-permute-start(bf16[16,4096]{1,0:T(8,128)(2,1)S(1)} %fusion.8), channel_id=1, source_target_pairs={{0,1},{1,2},{2,3},{3,4},{4,5},{5,6},{6,7},{7,8},{8,9},{9,10},{10,1... | collective-permute-start | bytes 393224 | tf_op jit(solution)/shard_map/ppermute | solution.py:244
  10.7 4.3 %collective-permute-done.prev_ref = bf16[16,4096]{1,0:T(8,128)(2,1)S(1)} collective-permute-done((bf16[16,4096]{1,0:T(8,128)(2,1)S(1)}, bf16[16,4096]{1,0:T(8,128)(2,1)S(1)}, u32[]{:S(2)}, u32[]{:S(2)}) %collective-permute-start) | collective-permute-done | bytes 131104 | tf_op jit(solution)/shard_map/ppermute | solution.py:244
  15.0 1.2 copy-done
  16.2 1.2 copy-done.2
  17.4 1.2 copy-done.4
  18.6 1.2 copy-done.6
  19.9 1.6 states.7
  25.0 5.6 %all-to-all-start.6 = ((bf16[8,2,128,128]{3,2,1,0:T(8,128)(2,1)}), bf16[8,2,128,128]{3,2,1,0:T(8,128)(2,1)}, u32[]{:S(2)}, u32[]{:S(2)}) async-start(bf16[8,2,128,128]{3,2,1,0:T(8,128)(2,1)} %copy-done.11), calls=%async_computation.6 | async-start | bytes 1048576 | tf_op jit(solution)/shard_map/all_to_all | solution.py:251
  30.6 1.2 copy-done.7
  31.8 1.6 states.6
  37.1 2.3 %states.5 = (bf16[144,1024]{1,0:T(8,128)(2,1)S(1)}, bf16[144,1024]{1,0:T(8,128)(2,1)S(1)}, bf16[144,1024]{1,0:T(8,128)(2,1)S(1)}, bf16[16,1024]{1,0:T(8,128)(2,1)S(1)}, bf16[8,2,128,128]{3,2,1,0:T(8,128)(2,1)}) custom-call(bf16[128,4096]{1,0:T(8,128)(2,1)S(1)} %copy-done.3, bf16[128,4096]{1,0:T(8,128)(2,1)S(1)} %copy-done.5, ...), custom_call_target="tpu_custom_call" | custom-call | flops 70254592 | bytes 2555904 | tf_op jit(solution)/shard_map/states/pallas_call | solution.py:117
  42.2 2.3 %states.4 = (bf16[144,1024]{1,0:T(8,128)(2,1)S(1)}, bf16[144,1024]{1,0:T(8,128)(2,1)S(1)}, bf16[144,1024]{1,0:T(8,128)(2,1)S(1)}, bf16[16,1024]{1,0:T(8,128)(2,1)S(1)}, bf16[8,2,128,128]{3,2,1,0:T(8,128)(2,1)}) custom-call(bf16[128,4096]{1,0:T(8,128)(2,1)S(1)} %copy-done.3, bf16[128,4096]{1,0:T(8,128)(2,1)S(1)} %copy-done.5, ...), custom_call_target="tpu_custom_call" | custom-call | flops 70254592 | bytes 2555904 | tf_op jit(solution)/shard_map/states/pallas_call | solution.py:117
  47.3 4.2 %all-to-all-start.4 = ((bf16[8,2,128,128]{3,2,1,0:T(8,128)(2,1)}), bf16[8,2,128,128]{3,2,1,0:T(8,128)(2,1)S(1)}, u32[]{:S(2)}, u32[]{:S(2)}) async-start(bf16[8,2,128,128]{3,2,1,0:T(8,128)(2,1)} %copy-done.12), calls=%async_computation.4 | async-start | bytes 1048576 | tf_op jit(solution)/shard_map/all_to_all | solution.py:251
  53.3 1.3 collective-permute-start.11
  54.6 5.1 %all-to-all-done.4 = bf16[8,2,128,128]{3,2,1,0:T(8,128)(2,1)S(1)} async-done(((bf16[8,2,128,128]{3,2,1,0:T(8,128)(2,1)}), bf16[8,2,128,128]{3,2,1,0:T(8,128)(2,1)S(1)}, u32[]{:S(2)}, u32[]{:S(2)}) %all-to-all-start.4) | async-done | bytes 524320 | tf_op jit(solution)/shard_map/all_to_all | solution.py:251
  59.7 4.5 %all-to-all-start.2 = ((bf16[8,2,128,128]{3,2,1,0:T(8,128)(2,1)}), bf16[8,2,128,128]{3,2,1,0:T(8,128)(2,1)S(1)}, u32[]{:S(2)}, u32[]{:S(2)}) async-start(bf16[8,2,128,128]{3,2,1,0:T(8,128)(2,1)} %get-tuple-element.41), calls=%async_computation.2 | async-start | bytes 1048576 | tf_op jit(solution)/shard_map/all_to_all | solution.py:251
  65.9 1.3 collective-permute-start.8
  67.2 5.1 %all-to-all-done.2 = bf16[8,2,128,128]{3,2,1,0:T(8,128)(2,1)S(1)} async-done(((bf16[8,2,128,128]{3,2,1,0:T(8,128)(2,1)}), bf16[8,2,128,128]{3,2,1,0:T(8,128)(2,1)S(1)}, u32[]{:S(2)}, u32[]{:S(2)}) %all-to-all-start.2) | async-done | bytes 524320 | tf_op jit(solution)/shard_map/all_to_all | solution.py:251
  72.4 5.1 %all-to-all-start = ((bf16[8,2,128,128]{3,2,1,0:T(8,128)(2,1)}), bf16[8,2,128,128]{3,2,1,0:T(8,128)(2,1)}, u32[]{:S(2)}, u32[]{:S(2)}) async-start(bf16[8,2,128,128]{3,2,1,0:T(8,128)(2,1)} %get-tuple-element.36), calls=%async_computation | async-start | bytes 1048576 | tf_op jit(solution)/shard_map/all_to_all | solution.py:251
  79.2 1.3 collective-permute-start.5
  80.5 5.3 %all-to-all-done = bf16[8,2,128,128]{3,2,1,0:T(8,128)(2,1)} async-done(((bf16[8,2,128,128]{3,2,1,0:T(8,128)(2,1)}), bf16[8,2,128,128]{3,2,1,0:T(8,128)(2,1)}, u32[]{:S(2)}, u32[]{:S(2)}) %all-to-all-start) | async-done | bytes 524320 | tf_op jit(solution)/shard_map/all_to_all | solution.py:251
  85.8 1.1 bitcast_convert_fusion.3
  87.0 1.4 collective-permute-start.2
  89.2 2.1 %collective-permute-start.12 = (bf16[1,128,128]{2,1,0:T(8,128)(2,1)S(1)}, bf16[1,128,128]{2,1,0:T(8,128)(2,1)S(1)}, u32[]{:S(2)}, u32[]{:S(2)}) collective-permute-start(bf16[1,128,128]{2,1,0:T(8,128)(2,1)S(1)} %select_convert_fusion), channel_id=1, source_target_pairs={{8,16},{16,8},{9,17},{17,9},{10,18},{18,10},{11,19},{19,11},{12,20... | collective-permute-start | bytes 98312 | tf_op jit(solution)/shard_map/ppermute | solution.py:200
  91.3 1.3 collective-permute-start.13
  92.6 1.4 select_convert_fusion.1
  94.0 1.9 %collective-permute-start.10 = (bf16[1,128,128]{2,1,0:T(8,128)(2,1)}, bf16[1,128,128]{2,1,0:T(8,128)(2,1)}, u32[]{:S(2)}, u32[]{:S(2)}) collective-permute-start(bf16[1,128,128]{2,1,0:T(8,128)(2,1)} %select_convert_fusion.1), channel_id=1, source_target_pairs={{8,24},{16,0},{9,25},{17,1},{10,26},{18,2},{11,27},{19,3},{12,28},... | collective-permute-start | bytes 98312 | tf_op jit(solution)/shard_map/ppermute | solution.py:200
  95.9 3.4 %collective-permute-start.9 = (bf16[1,128,128]{2,1,0:T(8,128)(2,1)}, bf16[1,128,128]{2,1,0:T(8,128)(2,1)}, u32[]{:S(2)}, u32[]{:S(2)}) collective-permute-start(bf16[1,128,128]{2,1,0:T(8,128)(2,1)} %select_convert_fusion.1), channel_id=1, source_target_pairs={{8,16},{16,8},{9,17},{17,9},{10,18},{18,10},{11,19},{19,11},{12,20... | collective-permute-start | bytes 98312 | tf_op jit(solution)/shard_map/ppermute | solution.py:200
  99.2 1.4 select_convert_fusion.2
  100.6 1.9 %collective-permute-start.6 = (bf16[1,128,128]{2,1,0:T(8,128)(2,1)}, bf16[1,128,128]{2,1,0:T(8,128)(2,1)}, u32[]{:S(2)}, u32[]{:S(2)}) collective-permute-start(bf16[1,128,128]{2,1,0:T(8,128)(2,1)} %select_convert_fusion.2), channel_id=1, source_target_pairs={{8,16},{16,8},{9,17},{17,9},{10,18},{18,10},{11,19},{19,11},{12,20... | collective-permute-start | bytes 98312 | tf_op jit(solution)/shard_map/ppermute | solution.py:200
  103.2 1.9 %collective-permute-start.7 = (bf16[1,128,128]{2,1,0:T(8,128)(2,1)}, bf16[1,128,128]{2,1,0:T(8,128)(2,1)}, u32[]{:S(2)}, u32[]{:S(2)}) collective-permute-start(bf16[1,128,128]{2,1,0:T(8,128)(2,1)} %select_convert_fusion.2), channel_id=1, source_target_pairs={{8,24},{16,0},{9,25},{17,1},{10,26},{18,2},{11,27},{19,3},{12,28},... | collective-permute-start | bytes 98312 | tf_op jit(solution)/shard_map/ppermute | solution.py:200
  105.1 3.4 %collective-permute-start.3 = (bf16[1,128,128]{2,1,0:T(8,128)(2,1)}, bf16[1,128,128]{2,1,0:T(8,128)(2,1)}, u32[]{:S(2)}, u32[]{:S(2)}) collective-permute-start(bf16[1,128,128]{2,1,0:T(8,128)(2,1)} %select_convert_fusion.3), channel_id=1, source_target_pairs={{8,16},{16,8},{9,17},{17,9},{10,18},{18,10},{11,19},{19,11},{12,20... | collective-permute-start | bytes 98312 | tf_op jit(solution)/shard_map/ppermute | solution.py:200
  111.2 6.0 %all-to-all-start.7 = ((bf16[8,2,128,128]{3,2,1,0:T(8,128)(2,1)}), bf16[8,2,128,128]{3,2,1,0:T(8,128)(2,1)S(1)}, u32[]{:S(2)}, u32[]{:S(2)}) async-start(bf16[8,2,128,128]{3,2,1,0:T(8,128)(2,1)} %pad_maximum_fusion.3), calls=%async_computation.7 | async-start | bytes 1048576 | tf_op jit(solution)/shard_map/all_to_all | solution.py:258
  117.2 1.4 collective-permute-start.4
  129.3 1.4 constant_dynamic-update-slice_fusion.15
  133.4 4.2 %all-to-all-start.5 = ((bf16[8,2,128,128]{3,2,1,0:T(8,128)(2,1)}), bf16[8,2,128,128]{3,2,1,0:T(8,128)(2,1)S(1)}, u32[]{:S(2)}, u32[]{:S(2)}) async-start(bf16[8,2,128,128]{3,2,1,0:T(8,128)(2,1)} %pad_maximum_fusion.2), calls=%async_computation.5 | async-start | bytes 1048576 | tf_op jit(solution)/shard_map/all_to_all | solution.py:258
  137.6 1.9 pad_maximum_fusion.1
  140.7 5.1 %all-to-all-done.5.s_ref = bf16[8,2,128,128]{3,2,1,0:T(8,128)(2,1)S(1)} async-done(((bf16[8,2,128,128]{3,2,1,0:T(8,128)(2,1)}), bf16[8,2,128,128]{3,2,1,0:T(8,128)(2,1)S(1)}, u32[]{:S(2)}, u32[]{:S(2)}) %all-to-all-start.5) | async-done | bytes 524320 | tf_op jit(solution)/shard_map/all_to_all | solution.py:258
  145.8 4.5 %all-to-all-start.3 = ((bf16[8,2,128,128]{3,2,1,0:T(8,128)(2,1)}), bf16[8,2,128,128]{3,2,1,0:T(8,128)(2,1)S(1)}, u32[]{:S(2)}, u32[]{:S(2)}) async-start(bf16[8,2,128,128]{3,2,1,0:T(8,128)(2,1)} %pad_maximum_fusion.1), calls=%async_computation.3 | async-start | bytes 1048576 | tf_op jit(solution)/shard_map/all_to_all | solution.py:258
  150.3 1.5 constant_dynamic-update-slice_fusion.9
  152.4 1.8 pad_maximum_fusion
  154.2 4.3 %all-to-all-done.3.s_ref = bf16[8,2,128,128]{3,2,1,0:T(8,128)(2,1)S(1)} async-done(((bf16[8,2,128,128]{3,2,1,0:T(8,128)(2,1)}), bf16[8,2,128,128]{3,2,1,0:T(8,128)(2,1)S(1)}, u32[]{:S(2)}, u32[]{:S(2)}) %all-to-all-start.3) | async-done | bytes 524320 | tf_op jit(solution)/shard_map/all_to_all | solution.py:258
  158.5 4.5 %all-to-all-start.1 = ((bf16[8,2,128,128]{3,2,1,0:T(8,128)(2,1)}), bf16[8,2,128,128]{3,2,1,0:T(8,128)(2,1)S(1)}, u32[]{:S(2)}, u32[]{:S(2)}) async-start(bf16[8,2,128,128]{3,2,1,0:T(8,128)(2,1)} %pad_maximum_fusion), calls=%async_computation.1 | async-start | bytes 1048576 | tf_op jit(solution)/shard_map/all_to_all | solution.py:258
  165.7 5.4 %grads.4 = (bf16[128,4096]{1,0:T(8,128)(2,1)}, bf16[128,4096]{1,0:T(8,128)(2,1)}, bf16[128,4096]{1,0:T(8,128)(2,1)}) custom-call(bf16[144,1024]{1,0:T(8,128)(2,1)S(1)} %copy-done.14, bf16[144,1024]{1,0:T(8,128)(2,1)S(1)} %copy-done.16, bf16[144,1024]{1,0:T(8,128)(2,1)S(1)} %copy-done.18, bf16[128,4096]{1,0:T(8,128)(2,1)S(1)} %copy-done.1, ...), custom_call_target="tpu_custom_call" | custom-call | flops 335544320 | bytes 2555904 | tf_op jit(solution)/shard_map/grads/pallas_call | solution.py:161
  171.1 5.4 %grads.5 = (bf16[128,4096]{1,0:T(8,128)(2,1)}, bf16[128,4096]{1,0:T(8,128)(2,1)}, bf16[128,4096]{1,0:T(8,128)(2,1)}) custom-call(bf16[144,1024]{1,0:T(8,128)(2,1)S(1)} %copy-done.32, bf16[144,1024]{1,0:T(8,128)(2,1)S(1)} %copy-done.34, bf16[144,1024]{1,0:T(8,128)(2,1)S(1)} %copy-done.36, ...), custom_call_target="tpu_custom_call", output_to_operand_aliasing={{0}: (9, {}), {1}: (10, {}), {2}: (11, {})} | custom-call | flops 335544320 | bytes 2555904 | tf_op jit(solution)/shard_map/grads/pallas_call | solution.py:161
  176.6 5.4 %grads.6 = (bf16[128,4096]{1,0:T(8,128)(2,1)}, bf16[128,4096]{1,0:T(8,128)(2,1)}, bf16[128,4096]{1,0:T(8,128)(2,1)}) custom-call(bf16[144,1024]{1,0:T(8,128)(2,1)S(1)} %copy-done.26, bf16[144,1024]{1,0:T(8,128)(2,1)S(1)} %copy-done.28, bf16[144,1024]{1,0:T(8,128)(2,1)S(1)} %copy-done.30, ...), custom_call_target="tpu_custom_call", output_to_operand_aliasing={{0}: (9, {}), {1}: (10, {}), {2}: (11, {})} | custom-call | flops 335544320 | bytes 2555904 | tf_op jit(solution)/shard_map/grads/pallas_call | solution.py:161
  182.0 5.4 %grads.7 = (bf16[128,4096]{1,0:T(8,128)(2,1)}, bf16[128,4096]{1,0:T(8,128)(2,1)}, bf16[128,4096]{1,0:T(8,128)(2,1)}) custom-call(bf16[144,1024]{1,0:T(8,128)(2,1)S(1)} %copy-done.20, bf16[144,1024]{1,0:T(8,128)(2,1)S(1)} %copy-done.22, bf16[144,1024]{1,0:T(8,128)(2,1)S(1)} %copy-done.24, ...), custom_call_target="tpu_custom_call", output_to_operand_aliasing={{0}: (9, {}), {1}: (10, {}), {2}: (11, {})} | custom-call | flops 335544320 | bytes 2555904 | tf_op jit(solution)/shard_map/grads/pallas_call | solution.py:161
  (213 shorter events, 43.7 us)
Async XLA Ops:
  3.5 7.2 %collective-permute-start.1 = (bf16[16,4096]{1,0:T(8,128)(2,1)S(1)}, bf16[16,4096]{1,0:T(8,128)(2,1)S(1)}, u32[]{:S(2)}, u32[]{:S(2)}) collective-permute-start(bf16[16,4096]{1,0:T(8,128)(2,1)S(1)} %fusion.11), channel_id=1, source_target_pairs={{1,0},{2,1},{3,2},{4,3},{5,4},{6,5},{7,6},{8,7},{9,8},{10,9},{11,1... | collective-permute-start | bytes 393224 | tf_op jit(solution)/shard_map/ppermute | solution.py:245
  5.7 9.3 %copy-start.8 = (bf16[4,4096]{1,0:T(4,128)(2,1)S(1)}, bf16[4,4096]{1,0:T(4,128)(2,1)}, u32[]{:S(2)}) copy-start(bf16[4,4096]{1,0:T(4,128)(2,1)} %tq_ref.15) | copy-start | bytes 98308
  5.7 9.3 %copy-start.9 = (bf16[4,4096]{1,0:T(4,128)(2,1)S(1)}, bf16[4,4096]{1,0:T(4,128)(2,1)}, u32[]{:S(2)}) copy-start(bf16[4,4096]{1,0:T(4,128)(2,1)} %tk_ref.15) | copy-start | bytes 98308
  5.7 9.3 %copy-start.10 = (bf16[4,4096]{1,0:T(4,128)(2,1)S(1)}, bf16[4,4096]{1,0:T(4,128)(2,1)}, u32[]{:S(2)}) copy-start(bf16[4,4096]{1,0:T(4,128)(2,1)} %tv_ref.15) | copy-start | bytes 98308
  5.8 9.1 %collective-permute-start = (bf16[16,4096]{1,0:T(8,128)(2,1)S(1)}, bf16[16,4096]{1,0:T(8,128)(2,1)S(1)}, u32[]{:S(2)}, u32[]{:S(2)}) collective-permute-start(bf16[16,4096]{1,0:T(8,128)(2,1)S(1)} %fusion.8), channel_id=1, source_target_pairs={{0,1},{1,2},{2,3},{3,4},{4,5},{5,6},{6,7},{7,8},{8,9},{9,10},{10,1... | collective-permute-start | bytes 393224 | tf_op jit(solution)/shard_map/ppermute | solution.py:244
  19.9 10.7 %copy-start.3 = (bf16[128,4096]{1,0:T(8,128)(2,1)S(1)}, bf16[128,4096]{1,0:T(8,128)(2,1)}, u32[]{:S(2)}) copy-start(bf16[128,4096]{1,0:T(8,128)(2,1)} %q_ref.7) | copy-start | bytes 3145732
  19.9 10.7 %copy-start.5 = (bf16[128,4096]{1,0:T(8,128)(2,1)S(1)}, bf16[128,4096]{1,0:T(8,128)(2,1)}, u32[]{:S(2)}) copy-start(bf16[128,4096]{1,0:T(8,128)(2,1)} %k_ref.7) | copy-start | bytes 3145732
  25.0 5.6 %copy-start.1 = (bf16[128,4096]{1,0:T(8,128)(2,1)S(1)}, bf16[128,4096]{1,0:T(8,128)(2,1)}, u32[]{:S(2)}) copy-start(bf16[128,4096]{1,0:T(8,128)(2,1)} %g_ref.15) | copy-start | bytes 3145732
  25.0 22.3 %all-to-all-start.6 = ((bf16[8,2,128,128]{3,2,1,0:T(8,128)(2,1)}), bf16[8,2,128,128]{3,2,1,0:T(8,128)(2,1)}, u32[]{:S(2)}, u32[]{:S(2)}) async-start(bf16[8,2,128,128]{3,2,1,0:T(8,128)(2,1)} %copy-done.11), calls=%async_computation.6 | async-start | bytes 1048576 | tf_op jit(solution)/shard_map/all_to_all | solution.py:251
  47.3 12.4 %all-to-all-start.4 = ((bf16[8,2,128,128]{3,2,1,0:T(8,128)(2,1)}), bf16[8,2,128,128]{3,2,1,0:T(8,128)(2,1)S(1)}, u32[]{:S(2)}, u32[]{:S(2)}) async-start(bf16[8,2,128,128]{3,2,1,0:T(8,128)(2,1)} %copy-done.12), calls=%async_computation.4 | async-start | bytes 1048576 | tf_op jit(solution)/shard_map/all_to_all | solution.py:251
  53.3 35.1 %collective-permute-start.11 = (bf16[1,128,128]{2,1,0:T(8,128)(2,1)}, bf16[1,128,128]{2,1,0:T(8,128)(2,1)}, u32[]{:S(2)}, u32[]{:S(2)}) collective-permute-start(bf16[1,128,128]{2,1,0:T(8,128)(2,1)} %fusion.84), channel_id=1, source_target_pairs={{0,8},{8,0},{16,24},{24,16},{1,9},{9,1},{17,25},{25,17},{2,10},{10... | collective-permute-start | bytes 98312 | tf_op jit(solution)/shard_map/ppermute | solution.py:200
  59.7 12.7 %all-to-all-start.2 = ((bf16[8,2,128,128]{3,2,1,0:T(8,128)(2,1)}), bf16[8,2,128,128]{3,2,1,0:T(8,128)(2,1)S(1)}, u32[]{:S(2)}, u32[]{:S(2)}) async-start(bf16[8,2,128,128]{3,2,1,0:T(8,128)(2,1)} %get-tuple-element.41), calls=%async_computation.2 | async-start | bytes 1048576 | tf_op jit(solution)/shard_map/all_to_all | solution.py:251
  65.9 26.6 %collective-permute-start.8 = (bf16[1,128,128]{2,1,0:T(8,128)(2,1)}, bf16[1,128,128]{2,1,0:T(8,128)(2,1)}, u32[]{:S(2)}, u32[]{:S(2)}) collective-permute-start(bf16[1,128,128]{2,1,0:T(8,128)(2,1)} %fusion.85), channel_id=1, source_target_pairs={{0,8},{8,0},{16,24},{24,16},{1,9},{9,1},{17,25},{25,17},{2,10},{10... | collective-permute-start | bytes 98312 | tf_op jit(solution)/shard_map/ppermute | solution.py:200
  72.4 13.4 %all-to-all-start = ((bf16[8,2,128,128]{3,2,1,0:T(8,128)(2,1)}), bf16[8,2,128,128]{3,2,1,0:T(8,128)(2,1)}, u32[]{:S(2)}, u32[]{:S(2)}) async-start(bf16[8,2,128,128]{3,2,1,0:T(8,128)(2,1)} %get-tuple-element.36), calls=%async_computation | async-start | bytes 1048576 | tf_op jit(solution)/shard_map/all_to_all | solution.py:251
  79.2 16.6 %collective-permute-start.5 = (bf16[1,128,128]{2,1,0:T(8,128)(2,1)}, bf16[1,128,128]{2,1,0:T(8,128)(2,1)}, u32[]{:S(2)}, u32[]{:S(2)}) collective-permute-start(bf16[1,128,128]{2,1,0:T(8,128)(2,1)} %fusion.86), channel_id=1, source_target_pairs={{0,8},{8,0},{16,24},{24,16},{1,9},{9,1},{17,25},{25,17},{2,10},{10... | collective-permute-start | bytes 98312 | tf_op jit(solution)/shard_map/ppermute | solution.py:200
  86.9 52.6 %copy-start.45 = (f32[8,1,2,128,128]{4,3,2,1,0:T(8,128)}, f32[8,1,2,128,128]{4,3,2,1,0:T(8,128)S(1)}, u32[]{:S(2)}) copy-start(f32[8,1,2,128,128]{4,3,2,1,0:T(8,128)S(1)} %bitcast_convert_fusion.3) | copy-start | bytes 3145732
  87.0 15.5 %copy-start.50 = (f32[128,128]{1,0:T(8,128)}, f32[128,128]{1,0:T(8,128)S(1)}, u32[]{:S(2)}) copy-start(f32[128,128]{1,0:T(8,128)S(1)} %get-tuple-element.67) | copy-start | bytes 196612
  87.0 5.5 %copy-start.56 = (f32[128,128]{1,0:T(8,128)S(1)}, f32[128,128]{1,0:T(8,128)}, u32[]{:S(2)}) copy-start(f32[128,128]{1,0:T(8,128)} %copy-done.55) | copy-start | bytes 196612
  87.0 13.6 %collective-permute-start.2 = (bf16[1,128,128]{2,1,0:T(8,128)(2,1)S(1)}, bf16[1,128,128]{2,1,0:T(8,128)(2,1)S(1)}, u32[]{:S(2)}, u32[]{:S(2)}) collective-permute-start(bf16[1,128,128]{2,1,0:T(8,128)(2,1)S(1)} %fusion.87), channel_id=1, source_target_pairs={{0,8},{8,0},{16,24},{24,16},{1,9},{9,1},{17,25},{25,17},{2,10},{10... | collective-permute-start | bytes 98312 | tf_op jit(solution)/shard_map/ppermute | solution.py:200
  89.2 10.0 %copy-start.53 = (f32[128,128]{1,0:T(8,128)S(1)}, f32[128,128]{1,0:T(8,128)}, u32[]{:S(2)}) copy-start(f32[128,128]{1,0:T(8,128)} %copy-done.52) | copy-start | bytes 196612
  89.2 14.0 %collective-permute-start.12 = (bf16[1,128,128]{2,1,0:T(8,128)(2,1)S(1)}, bf16[1,128,128]{2,1,0:T(8,128)(2,1)S(1)}, u32[]{:S(2)}, u32[]{:S(2)}) collective-permute-start(bf16[1,128,128]{2,1,0:T(8,128)(2,1)S(1)} %select_convert_fusion), channel_id=1, source_target_pairs={{8,16},{16,8},{9,17},{17,9},{10,18},{18,10},{11,19},{19,11},{12,20... | collective-permute-start | bytes 98312 | tf_op jit(solution)/shard_map/ppermute | solution.py:200
  91.3 13.8 %collective-permute-start.13 = (bf16[1,128,128]{2,1,0:T(8,128)(2,1)S(1)}, bf16[1,128,128]{2,1,0:T(8,128)(2,1)S(1)}, u32[]{:S(2)}, u32[]{:S(2)}) collective-permute-start(bf16[1,128,128]{2,1,0:T(8,128)(2,1)S(1)} %select_convert_fusion), channel_id=1, source_target_pairs={{8,24},{16,0},{9,25},{17,1},{10,26},{18,2},{11,27},{19,3},{12,28},... | collective-permute-start | bytes 98312 | tf_op jit(solution)/shard_map/ppermute | solution.py:200
  94.0 23.2 %collective-permute-start.10 = (bf16[1,128,128]{2,1,0:T(8,128)(2,1)}, bf16[1,128,128]{2,1,0:T(8,128)(2,1)}, u32[]{:S(2)}, u32[]{:S(2)}) collective-permute-start(bf16[1,128,128]{2,1,0:T(8,128)(2,1)} %select_convert_fusion.1), channel_id=1, source_target_pairs={{8,24},{16,0},{9,25},{17,1},{10,26},{18,2},{11,27},{19,3},{12,28},... | collective-permute-start | bytes 98312 | tf_op jit(solution)/shard_map/ppermute | solution.py:200
  95.9 22.8 %collective-permute-start.9 = (bf16[1,128,128]{2,1,0:T(8,128)(2,1)}, bf16[1,128,128]{2,1,0:T(8,128)(2,1)}, u32[]{:S(2)}, u32[]{:S(2)}) collective-permute-start(bf16[1,128,128]{2,1,0:T(8,128)(2,1)} %select_convert_fusion.1), channel_id=1, source_target_pairs={{8,16},{16,8},{9,17},{17,9},{10,18},{18,10},{11,19},{19,11},{12,20... | collective-permute-start | bytes 98312 | tf_op jit(solution)/shard_map/ppermute | solution.py:200
  100.6 23.4 %collective-permute-start.6 = (bf16[1,128,128]{2,1,0:T(8,128)(2,1)}, bf16[1,128,128]{2,1,0:T(8,128)(2,1)}, u32[]{:S(2)}, u32[]{:S(2)}) collective-permute-start(bf16[1,128,128]{2,1,0:T(8,128)(2,1)} %select_convert_fusion.2), channel_id=1, source_target_pairs={{8,16},{16,8},{9,17},{17,9},{10,18},{18,10},{11,19},{19,11},{12,20... | collective-permute-start | bytes 98312 | tf_op jit(solution)/shard_map/ppermute | solution.py:200
  103.2 20.9 %collective-permute-start.7 = (bf16[1,128,128]{2,1,0:T(8,128)(2,1)}, bf16[1,128,128]{2,1,0:T(8,128)(2,1)}, u32[]{:S(2)}, u32[]{:S(2)}) collective-permute-start(bf16[1,128,128]{2,1,0:T(8,128)(2,1)} %select_convert_fusion.2), channel_id=1, source_target_pairs={{8,24},{16,0},{9,25},{17,1},{10,26},{18,2},{11,27},{19,3},{12,28},... | collective-permute-start | bytes 98312 | tf_op jit(solution)/shard_map/ppermute | solution.py:200
  105.1 22.5 %collective-permute-start.3 = (bf16[1,128,128]{2,1,0:T(8,128)(2,1)}, bf16[1,128,128]{2,1,0:T(8,128)(2,1)}, u32[]{:S(2)}, u32[]{:S(2)}) collective-permute-start(bf16[1,128,128]{2,1,0:T(8,128)(2,1)} %select_convert_fusion.3), channel_id=1, source_target_pairs={{8,16},{16,8},{9,17},{17,9},{10,18},{18,10},{11,19},{19,11},{12,20... | collective-permute-start | bytes 98312 | tf_op jit(solution)/shard_map/ppermute | solution.py:200
  111.2 7.5 %copy-start.57 = (f32[128,128]{1,0:T(8,128)S(1)}, f32[128,128]{1,0:T(8,128)}, u32[]{:S(2)}) copy-start(f32[128,128]{1,0:T(8,128)} %copy-done.55) | copy-start | bytes 196612
  111.2 22.3 %all-to-all-start.7 = ((bf16[8,2,128,128]{3,2,1,0:T(8,128)(2,1)}), bf16[8,2,128,128]{3,2,1,0:T(8,128)(2,1)S(1)}, u32[]{:S(2)}, u32[]{:S(2)}) async-start(bf16[8,2,128,128]{3,2,1,0:T(8,128)(2,1)} %pad_maximum_fusion.3), calls=%async_computation.7 | async-start | bytes 1048576 | tf_op jit(solution)/shard_map/all_to_all | solution.py:258
  117.2 5.8 %copy-start.49 = (f32[8,1,2,128,128]{4,3,2,1,0:T(8,128)S(1)}, f32[8,1,2,128,128]{4,3,2,1,0:T(8,128)}, u32[]{:S(2)}) copy-start(f32[8,1,2,128,128]{4,3,2,1,0:T(8,128)} %copy-done.48) | copy-start | bytes 3145732
  117.2 10.4 %collective-permute-start.4 = (bf16[1,128,128]{2,1,0:T(8,128)(2,1)}, bf16[1,128,128]{2,1,0:T(8,128)(2,1)S(1)}, u32[]{:S(2)}, u32[]{:S(2)}) collective-permute-start(bf16[1,128,128]{2,1,0:T(8,128)(2,1)} %select_convert_fusion.3), channel_id=1, source_target_pairs={{8,24},{16,0},{9,25},{17,1},{10,26},{18,2},{11,27},{19,3},{12,28},... | collective-permute-start | bytes 98312 | tf_op jit(solution)/shard_map/ppermute | solution.py:200
  133.4 12.4 %all-to-all-start.5 = ((bf16[8,2,128,128]{3,2,1,0:T(8,128)(2,1)}), bf16[8,2,128,128]{3,2,1,0:T(8,128)(2,1)S(1)}, u32[]{:S(2)}, u32[]{:S(2)}) async-start(bf16[8,2,128,128]{3,2,1,0:T(8,128)(2,1)} %pad_maximum_fusion.2), calls=%async_computation.5 | async-start | bytes 1048576 | tf_op jit(solution)/shard_map/all_to_all | solution.py:258
  145.8 12.7 %all-to-all-start.3 = ((bf16[8,2,128,128]{3,2,1,0:T(8,128)(2,1)}), bf16[8,2,128,128]{3,2,1,0:T(8,128)(2,1)S(1)}, u32[]{:S(2)}, u32[]{:S(2)}) async-start(bf16[8,2,128,128]{3,2,1,0:T(8,128)(2,1)} %pad_maximum_fusion.1), calls=%async_computation.3 | async-start | bytes 1048576 | tf_op jit(solution)/shard_map/all_to_all | solution.py:258
  150.3 2.1 %copy-start.63 = (bf16[8,1,128,128]{3,2,1,0:T(8,128)(2,1)S(1)}, bf16[8,1,128,128]{3,2,1,0:T(8,128)(2,1)}, u32[]{:S(2)}) copy-start(bf16[8,1,128,128]{3,2,1,0:T(8,128)(2,1)} %copy-done.62) | copy-start | bytes 786436
  154.2 8.8 %copy-start.14 = (bf16[144,1024]{1,0:T(8,128)(2,1)S(1)}, bf16[144,1024]{1,0:T(8,128)(2,1)}, u32[]{:S(2)}) copy-start(bf16[144,1024]{1,0:T(8,128)(2,1)} %copy-done.13) | copy-start | bytes 884740
  158.5 23.5 %all-to-all-start.1 = ((bf16[8,2,128,128]{3,2,1,0:T(8,128)(2,1)}), bf16[8,2,128,128]{3,2,1,0:T(8,128)(2,1)S(1)}, u32[]{:S(2)}, u32[]{:S(2)}) async-start(bf16[8,2,128,128]{3,2,1,0:T(8,128)(2,1)} %pad_maximum_fusion), calls=%async_computation.1 | async-start | bytes 1048576 | tf_op jit(solution)/shard_map/all_to_all | solution.py:258
  165.7 5.4 %copy-start.32 = (bf16[144,1024]{1,0:T(8,128)(2,1)S(1)}, bf16[144,1024]{1,0:T(8,128)(2,1)}, u32[]{:S(2)}) copy-start(bf16[144,1024]{1,0:T(8,128)(2,1)} %copy-done.31) | copy-start | bytes 884740
  165.7 5.4 %copy-start.34 = (bf16[144,1024]{1,0:T(8,128)(2,1)S(1)}, bf16[144,1024]{1,0:T(8,128)(2,1)}, u32[]{:S(2)}) copy-start(bf16[144,1024]{1,0:T(8,128)(2,1)} %copy-done.33) | copy-start | bytes 884740
  165.7 5.4 %copy-start.36 = (bf16[144,1024]{1,0:T(8,128)(2,1)S(1)}, bf16[144,1024]{1,0:T(8,128)(2,1)}, u32[]{:S(2)}) copy-start(bf16[144,1024]{1,0:T(8,128)(2,1)} %copy-done.35) | copy-start | bytes 884740
  165.7 5.4 %copy-start.44 = (bf16[16,1024]{1,0:T(8,128)(2,1)S(1)}, bf16[16,1024]{1,0:T(8,128)(2,1)}, u32[]{:S(2)}) copy-start(bf16[16,1024]{1,0:T(8,128)(2,1)} %copy-done.43) | copy-start | bytes 98308
  171.1 5.4 %copy-start.26 = (bf16[144,1024]{1,0:T(8,128)(2,1)S(1)}, bf16[144,1024]{1,0:T(8,128)(2,1)}, u32[]{:S(2)}) copy-start(bf16[144,1024]{1,0:T(8,128)(2,1)} %copy-done.25) | copy-start | bytes 884740
  171.1 5.4 %copy-start.28 = (bf16[144,1024]{1,0:T(8,128)(2,1)S(1)}, bf16[144,1024]{1,0:T(8,128)(2,1)}, u32[]{:S(2)}) copy-start(bf16[144,1024]{1,0:T(8,128)(2,1)} %copy-done.27) | copy-start | bytes 884740
  171.1 5.4 %copy-start.30 = (bf16[144,1024]{1,0:T(8,128)(2,1)S(1)}, bf16[144,1024]{1,0:T(8,128)(2,1)}, u32[]{:S(2)}) copy-start(bf16[144,1024]{1,0:T(8,128)(2,1)} %copy-done.29) | copy-start | bytes 884740
  171.1 5.4 %copy-start.42 = (bf16[16,1024]{1,0:T(8,128)(2,1)S(1)}, bf16[16,1024]{1,0:T(8,128)(2,1)}, u32[]{:S(2)}) copy-start(bf16[16,1024]{1,0:T(8,128)(2,1)} %copy-done.41) | copy-start | bytes 98308
  176.6 5.4 %copy-start.20 = (bf16[144,1024]{1,0:T(8,128)(2,1)S(1)}, bf16[144,1024]{1,0:T(8,128)(2,1)}, u32[]{:S(2)}) copy-start(bf16[144,1024]{1,0:T(8,128)(2,1)} %copy-done.19) | copy-start | bytes 884740
  176.6 5.4 %copy-start.22 = (bf16[144,1024]{1,0:T(8,128)(2,1)S(1)}, bf16[144,1024]{1,0:T(8,128)(2,1)}, u32[]{:S(2)}) copy-start(bf16[144,1024]{1,0:T(8,128)(2,1)} %copy-done.21) | copy-start | bytes 884740
  176.6 5.4 %copy-start.24 = (bf16[144,1024]{1,0:T(8,128)(2,1)S(1)}, bf16[144,1024]{1,0:T(8,128)(2,1)}, u32[]{:S(2)}) copy-start(bf16[144,1024]{1,0:T(8,128)(2,1)} %copy-done.23) | copy-start | bytes 884740
  176.6 5.4 %copy-start.40 = (bf16[16,1024]{1,0:T(8,128)(2,1)S(1)}, bf16[16,1024]{1,0:T(8,128)(2,1)}, u32[]{:S(2)}) copy-start(bf16[16,1024]{1,0:T(8,128)(2,1)} %copy-done.39) | copy-start | bytes 98308
  (38 other events, 33.6 us)

commit v2 on v1

v2 whole, which is shorter than its diff:
```python
import functools
import math

import jax
import jax.numpy as jnp
from jax import lax
from jax.experimental import pallas as pl
from jax.experimental.pallas import tpu as pltpu
from jax.sharding import Mesh, PartitionSpec as P

HEAD = 128
KERNEL = 4
REACH = KERNEL - 1
CORES = 2
PAD = 8
EDGE = 16
MIB = 1024 * 1024

F32 = jnp.float32
BF16 = jnp.bfloat16
MEMBER, PLANE = 0, 1


def dot(a, b, ca, cb):
    return lax.dot_general(a, b, (((ca,), (cb,)), ((), ())), preferred_element_type=F32)


def shape(dims, dtype=BF16):
    return jax.ShapeDtypeStruct(dims, dtype)


def params():
    return pltpu.CompilerParams(vmem_limit_bytes=60 * MIB)


def cost(flops, moved):
    return pl.CostEstimate(flops=int(flops), bytes_accessed=int(moved), transcendentals=0)


def pack_kernel(ql, kl, vl, qf, kf, vf, gf, tail_ref, lead_ref):
    def rows_of(refs, start, total):
        parts = [r[...].astype(F32)[start : start + REACH] for r in refs]
        fill = jnp.zeros((total - REACH * len(refs), parts[0].shape[1]), F32)
        return jnp.concatenate(parts + [fill], 0).astype(BF16)

    tail_ref[...] = rows_of((ql, kl, vl), EDGE - REACH, EDGE)
    lead_ref[...] = rows_of((qf, kf, vf, gf), 0, EDGE)


def pack(raws):
    rows, width = raws[0].shape
    last = pl.BlockSpec((EDGE, width), lambda i: (rows // EDGE - 1, 0))
    first = pl.BlockSpec((EDGE, width), lambda i: (0, 0))
    return pl.pallas_call(
        pack_kernel,
        grid=(1,),
        in_specs=[last] * 3 + [first] * 4,
        out_specs=[first] * 2,
        out_shape=[shape((EDGE, width))] * 2,
        compiler_params=params(),
        cost_estimate=cost(0, 9 * 2 * EDGE * width),
        name="pack",
    )(*raws[:3], *raws)


def states_kernel(peers, idx, cols, q_ref, k_ref, v_ref, g_ref, prev_ref, tq, tk, tv, *rest):
    outs, s_refs, x_ref = rest[:3], rest[3:-1], rest[-1]
    rows, width = q_ref.shape
    prev = prev_ref[...].astype(F32)
    states = []
    for h in range(width // HEAD):
        c = slice(h * HEAD, (h + 1) * HEAD)
        feats = []
        for i, (raw, tap_ref) in enumerate(((q_ref, tq), (k_ref, tk), (v_ref, tv))):
            taps = tap_ref[:, c].astype(F32)
            x_ref[h, i, PAD - REACH : PAD] = prev[REACH * i : REACH * (i + 1), c]
            x_ref[h, i, PAD:] = raw[:, c].astype(F32)
            mixed = taps[0:1] * x_ref[h, i, PAD:]
            for j in range(1, KERNEL):
                mixed = mixed + taps[j : j + 1] * x_ref[h, i, PAD - j : PAD - j + rows]
            feats.append(mixed.astype(BF16))
            outs[i][:, c] = feats[-1]
        qf, kf, vf = feats
        states.append((dot(vf, kf, 0, 0).astype(BF16), dot(g_ref[:, c], qf, 0, 0).astype(BF16)))
    for d in range(peers):

        @pl.when(pl.program_id(0) == d)
        def _():
            for h, (vk, gq) in enumerate(states):
                s_refs[d][h, 0] = vk
                s_refs[d][h, 1] = gq


def states_call(peers, heads, idx, cols, raws, prev, taps):
    rows = raws[0].shape[0]
    width = heads * HEAD

    def wide(n):
        return pl.BlockSpec((n, width), lambda i, x, p: (0, p[i]))

    def out(n):
        return pl.BlockSpec((n, width), lambda i, x, p: (0, i))

    whole = pl.BlockSpec((heads, 2, HEAD, HEAD), lambda i, x, p: (0, 0, 0, 0))
    return pl.pallas_call(
        functools.partial(states_kernel, peers),
        grid_spec=pltpu.PrefetchScalarGridSpec(
            num_scalar_prefetch=2,
            grid=(peers,),
            in_specs=[wide(rows)] * 4 + [wide(EDGE)] + [wide(KERNEL)] * 3,
            out_specs=[out(rows)] * 3 + [whole] * peers,
            scratch_shapes=[pltpu.VMEM((heads, 3, PAD + rows, HEAD), F32)],
        ),
        out_shape=[shape((rows, peers * width))] * 3 + [shape((heads, 2, HEAD, HEAD))] * peers,
        compiler_params=params(),
        cost_estimate=cost(
            4 * heads * peers * rows * HEAD * HEAD, 2 * heads * peers * HEAD * (7 * rows + 2 * HEAD)
        ),
        name="states",
    )(idx, cols, *raws, prev, *taps)


def intra_kernel(
    cols, qf, kf, vf, g_ref, ql, kl, vl, next_ref, tq, tk, tv, d_ref, ke_ref, ve_ref, ge_ref, x_ref
):
    rows, width = g_ref.shape
    after = next_ref[...].astype(F32)
    edges = []
    for i, (raw, tap_ref) in enumerate(((ql, tq), (kl, tk), (vl, tv))):
        taps = tap_ref[...].astype(F32)
        x_ref[i, :EDGE] = raw[...].astype(F32)
        x_ref[i, EDGE:] = jnp.zeros((EDGE, width), F32)
        x_ref[i, EDGE : EDGE + REACH] = after[REACH * i : REACH * (i + 1)]
        mixed = taps[0:1] * x_ref[i, EDGE:]
        for j in range(1, KERNEL):
            mixed = mixed + taps[j : j + 1] * x_ref[i, EDGE - j : 2 * EDGE - j]
        edges.append(mixed.astype(BF16))
    fill = jnp.zeros((EDGE - REACH, width), F32)
    edges.append(jnp.concatenate([after[3 * REACH : 4 * REACH], fill], 0).astype(BF16))
    qe_all, ke_all, ve_all, ge_all = edges
    ke_ref[...] = ke_all
    ve_ref[...] = ve_all
    ge_ref[...] = ge_all
    heads = width // HEAD

    def order(dims):
        return lax.broadcasted_iota(jnp.int32, dims, 0), lax.broadcasted_iota(jnp.int32, dims, 1)

    def stack(field):
        return jnp.concatenate([field[:, h * HEAD : (h + 1) * HEAD] for h in range(heads)], 0)

    qs, ks, vs, gs = [stack(field) for field in edges]
    row, col = order((heads * EDGE, heads * EDGE))
    same = row // EDGE == col // EDGE
    scores = dot(gs, vs, 1, 1)
    scores_t = dot(vs, gs, 1, 1)
    similar_t = dot(ks, qs, 1, 1)
    eq = dot(jnp.where(same & (row >= col), scores, 0.0).astype(BF16), ks, 1, 0)
    ek = dot(jnp.where(same & (col < row), scores_t, 0.0).astype(BF16), qs, 1, 0)
    ev = dot(jnp.where(same & (col < row), similar_t, 0.0).astype(BF16), gs, 1, 0)
    row, col = order((rows, rows))
    lower = row >= col
    upper = col >= row
    for h in range(heads):
        c = slice(h * HEAD, (h + 1) * HEAD)
        r = slice(h * EDGE, (h + 1) * EDGE)
        q, k, v, g = qf[:, c], kf[:, c], vf[:, c], g_ref[:, c]
        ge = ge_all[:, c]
        scores = jnp.where(lower, dot(g, v, 1, 1), 0.0).astype(BF16)
        d_ref[h, 0, :rows] = dot(scores, k, 1, 0)
        d_ref[h, 0, rows:] = dot(dot(ge, v, 1, 1).astype(BF16), k, 1, 0) + eq[r]
        scores_t = jnp.where(upper, dot(v, g, 1, 1), 0.0).astype(BF16)
        d_ref[h, 1, :rows] = dot(scores_t, q, 1, 0)
        d_ref[h, 1, rows:] = -ek[r]
        similar_t = jnp.where(upper, dot(k, q, 1, 1), 0.0).astype(BF16)
        d_ref[h, 2, :rows] = dot(similar_t, g, 1, 0)
        d_ref[h, 2, rows:] = -ev[r]


def intra_call(peers, heads, cols, feats, raws, after, taps):
    rows = raws[0].shape[0]
    width = heads * HEAD
    ext = rows + EDGE
    total = peers * width

    def wide(n, r=0):
        return pl.BlockSpec((n, width), lambda i, p: (r, p[i]))

    def own(n):
        return pl.BlockSpec((n, width), lambda i, p: (0, i))

    return pl.pallas_call(
        intra_kernel,
        grid_spec=pltpu.PrefetchScalarGridSpec(
            num_scalar_prefetch=1,
            grid=(peers,),
            in_specs=[own(rows)] * 3
            + [wide(rows)]
            + [wide(EDGE, rows // EDGE - 1)] * 3
            + [wide(EDGE)]
            + [wide(KERNEL)] * 3,
            out_specs=[pl.BlockSpec((heads, 3, ext, HEAD), lambda i, p: (i, 0, 0, 0))]
            + [own(EDGE)] * 3,
            scratch_shapes=[pltpu.VMEM((3, 2 * EDGE, width), F32)],
        ),
        out_shape=[shape((peers * heads, 3, ext, HEAD), F32)] + [shape((EDGE, total))] * 3,
        compiler_params=params(),
        cost_estimate=cost(
            12 * peers * heads * rows * HEAD * HEAD, peers * heads * HEAD * 4 * (3 * ext + 2 * rows)
        ),
        name="intra",
    )(cols, *feats, raws[3], *raws[:3], after, *taps)


def sums_kernel(members, idx, *refs):
    s_refs, outs = refs[:members], refs[members:]
    for h in range(outs[0].shape[0]):
        total = s_refs[0][h].astype(F32)
        for r in s_refs[1:]:
            total = total + r[h].astype(F32)
        for bit, out in enumerate(outs):
            low = (idx[PLANE] >> bit) & 1 == 0
            out[h] = jnp.where(low, total[0], total[1]).astype(BF16)


def members_kernel(members, planes, idx, *refs):
    s_refs, z_refs = refs[:members], refs[members : members + planes - 1]
    outs, run_ref = refs[members + planes - 1 : -1], refs[-1]
    for h in range(z_refs[0].shape[0]):
        kv = jnp.zeros((HEAD, HEAD), F32)
        gq = jnp.zeros((HEAD, HEAD), F32)
        for d in range(1, planes):
            got = z_refs[d - 1][h].astype(F32)
            earlier = (idx[PLANE] ^ d) < idx[PLANE]
            kv = kv + jnp.where(earlier, got, 0.0)
            gq = gq + jnp.where(earlier, 0.0, got)
        for d in range(members):
            run_ref[idx[MEMBER] ^ d] = s_refs[d][h].astype(F32)
        for m in range(members):
            own = run_ref[m, 0]
            run_ref[m, 0] = kv
            kv = kv + own
        for m in reversed(range(members)):
            own = run_ref[m, 1]
            run_ref[m, 1] = gq
            gq = gq + own
        for d in range(members):
            outs[d][h] = run_ref[idx[MEMBER] ^ d].astype(BF16)


def small_call(kernel, name, idx, args, outs, scratch=()):
    moved = sum(math.prod(x.shape) * x.dtype.itemsize for x in [*args, *outs])
    whole = pl.BlockSpec(memory_space=pltpu.VMEM)
    return pl.pallas_call(
        kernel,
        in_specs=[pl.BlockSpec(memory_space=pltpu.SMEM)] + [whole] * len(args),
        out_specs=[whole] * len(outs),
        out_shape=outs,
        scratch_shapes=scratch,
        compiler_params=pltpu.CompilerParams(vmem_limit_bytes=24 * MIB),
        cost_estimate=cost(0, moved),
        name=name,
    )(idx, *args)


def grads_kernel(
    scale, peers, alias, cols, kf, vf, g_ref, d_in, ke_ref, ve_ref, ge_ref, tq, tk, tv, *rest
):
    p_refs = rest[:peers]
    dq_ref, dk_ref, dv_ref, p_ref, d_ref = rest[peers + (3 if alias else 0) :]
    rows, width = g_ref.shape
    for d in range(peers):

        @pl.when(pl.program_id(0) == d)
        def _():
            p_ref[...] = p_refs[d][...]

    for h in range(width // HEAD):
        c = slice(h * HEAD, (h + 1) * HEAD)
        vk, gq = p_ref[h, 0], p_ref[h, 1]
        gx = jnp.concatenate([g_ref[:, c], ge_ref[:, c]], 0)
        vx = jnp.concatenate([vf[:, c], ve_ref[:, c]], 0)
        kx = jnp.concatenate([kf[:, c], ke_ref[:, c]], 0)
        d_ref[h, 0] = d_in[h, 0] + dot(gx, vk, 1, 0)
        d_ref[h, 1] = d_in[h, 1] + dot(vx, gq, 1, 0)
        d_ref[h, 2] = d_in[h, 2] + dot(kx, gq, 1, 1)
        for i, (tap_ref, out) in enumerate(((tq, dq_ref), (tk, dk_ref), (tv, dv_ref))):
            taps = tap_ref[:, c].astype(F32) * scale
            total = taps[0:1] * d_ref[h, i, 0:rows]
            for j in range(1, KERNEL):
                total = total + taps[j : j + 1] * d_ref[h, i, j : j + rows]
            out[:, c] = total.astype(BF16)


def grads_call(peers, heads, scale, cols, feats, g, intra, states, taps, outs):
    rows, total_width = g.shape
    width = heads * HEAD
    ext = rows + EDGE

    def wide(n):
        return pl.BlockSpec((n, width), lambda i, p: (0, p[i]))

    def own(n):
        return pl.BlockSpec((n, width), lambda i, p: (0, i))

    alias = outs is not None
    specs = [own(rows)] * 2 + [wide(rows)]
    specs += [pl.BlockSpec((heads, 3, ext, HEAD), lambda i, p: (i, 0, 0, 0))] + [own(EDGE)] * 3
    specs += [wide(KERNEL)] * 3
    specs += [pl.BlockSpec((heads, 2, HEAD, HEAD), lambda i, p: (0, 0, 0, 0))] * peers
    args = [feats[1], feats[2], g, *intra, *taps, *states]
    aliases = {}
    if alias:
        aliases = {1 + len(args) + i: i for i in range(3)}
        specs += [pl.BlockSpec(memory_space=pl.ANY)] * 3
        args += list(outs)
    return pl.pallas_call(
        functools.partial(grads_kernel, scale, peers, alias),
        grid_spec=pltpu.PrefetchScalarGridSpec(
            num_scalar_prefetch=1,
            grid=(peers,),
            in_specs=specs,
            out_specs=[wide(rows)] * 3,
            scratch_shapes=[
                pltpu.VMEM((heads, 2, HEAD, HEAD), BF16),
                pltpu.VMEM((heads, 3, ext, HEAD), F32),
            ],
        ),
        out_shape=[shape((rows, total_width))] * 3,
        input_output_aliases=aliases,
        compiler_params=params(),
        cost_estimate=cost(
            6 * heads * peers * ext * HEAD * HEAD, heads * peers * HEAD * (12 * ext + 12 * rows + 512)
        ),
        name="grads",
    )(cols, *args)


def local(query_raw, key_raw, value_raw, grad_out, query_kernel, key_kernel, value_kernel):
    rows, total_width = query_raw.shape
    planes, grp = lax.axis_size("z"), lax.axis_size("grp")
    members = CORES * grp
    devices = planes * members
    scale = float(HEAD * rows * devices) ** (-0.5)
    heads = total_width // HEAD // members
    everyone = ("z", "core", "grp")
    plane = ("core", "grp")
    raws = (query_raw, key_raw, value_raw, grad_out)
    taps = (query_kernel, key_kernel, value_kernel)
    me = lax.axis_index("core") * grp + lax.axis_index("grp")
    idx = jnp.stack([me, lax.axis_index("z")]).astype(jnp.int32)
    groups = [list(range(1, members, 2)), [*range(2, members, 2), 0]]
    cols = [(me ^ jnp.array(ds, jnp.int32)).astype(jnp.int32) for ds in groups]

    def swap(x, axes, count, d):
        return lax.ppermute(x, axes, [(i, i ^ d) for i in range(count)])

    def held(first, second):
        return lax.optimization_barrier((first, second))

    tail, lead = pack(raws)
    prev = lax.ppermute(tail, everyone, [(i, i + 1) for i in range(devices - 1)])
    after = lax.ppermute(lead, everyone, [(i + 1, i) for i in range(devices - 1)])

    feats, states = [], {}
    for n, ds in enumerate(groups):
        out = states_call(len(ds), heads, idx, cols[n], raws, prev, taps)
        feats.append(out[:3])
        for d, s in zip(ds, out[3:]):
            states[d] = swap(s, plane, members, d) if d else s
    intra = [None] * len(groups)
    intra[0] = intra_call(len(groups[0]), heads, cols[0], feats[0], raws, after, taps)
    states, intra[0] = held(states, intra[0])
    states = [states[d] for d in range(members)]
    bits = (planes - 1).bit_length()
    levels = small_call(
        functools.partial(sums_kernel, members),
        "sums",
        idx,
        states,
        [shape((heads, HEAD, HEAD))] * bits,
    )
    feats[1], levels = held(feats[1], levels)
    across = [swap(levels[d.bit_length() - 1], "z", planes, d) for d in range(1, planes)]
    intra[1] = intra_call(len(groups[1]), heads, cols[1], feats[1], raws, after, taps)
    across, intra[1] = held(across, intra[1])
    sent = small_call(
        functools.partial(members_kernel, members, planes),
        "members",
        idx,
        [*states, *across],
        [shape((heads, 2, HEAD, HEAD))] * members,
        [pltpu.VMEM((members, 2, HEAD, HEAD), F32)],
    )
    backs = {0: sent[0]}
    for d in [*groups[0], *groups[1]]:
        if d:
            backs[d] = swap(sent[d], plane, members, d)
    outs = None
    for n in (1, 0):
        ds = groups[n]
        outs = grads_call(
            len(ds), heads, scale, cols[n], feats[n], grad_out, intra[n], [backs[d] for d in ds], taps, outs
        )
    return tuple(outs)


def solution(mesh):
    chain, grp = mesh.shape["chain"], mesh.shape["grp"]
    split = Mesh(mesh.devices.reshape(chain // CORES, CORES, grp), ("z", "core", "grp"))
    tokens = P(("z", "core", "grp"), None)
    return jax.shard_map(
        local,
        mesh=split,
        in_specs=(tokens,) * 4 + (P(),) * 3,
        out_specs=(tokens,) * 3,
        check_vma=False,
    )
```

time: 190 us -> 113 us (0.59)
  the two profiles are of different devices: /device:TPU:19 before, /device:TPU:0 now
where the time goes in v2:
time: 113 us; the launch traced here: 112 us
  Pallas kernels  57.5 us (51%)
  starting transfers between devices  29.2 us (26%)
  waiting for transfers between devices  19.7 us (17%)
  local copies, waits for them, and re-layouts  2.8 us (2%)
  other arithmetic  1.62 us (1%)
    pallas_call x2, Pallas kernels, intra_call(): pl.pallas_call(intra_kernel, grid_spec=pltpu.PrefetchScalarGridSpec(num_s...  28.5 us
    ppermute x17, starting transfers between devices, swap(): return lax.ppermute(x, axes, [(i, i ^ d) for i in range(count)])  23 us
    ppermute x17, waiting for transfers between devices, swap(): return lax.ppermute(x, axes, [(i, i ^ d) for i in range(count)])  17.7 us
    pallas_call x2, Pallas kernels, grads_call(): pl.pallas_call(functools.partial(grads_kernel, scale, peers, alias), grid...  13.1 us
    pallas_call x2, Pallas kernels, states_call(): pl.pallas_call(functools.partial(states_kernel, peers), grid_spec=pltpu.P...  11.8 us
    ppermute x1, starting transfers between devices, local(): lax.ppermute(tail, everyone, [(i, i + 1) for i in range(devices - 1)])  4.97 us
    unnamed x30, local copies, waits for them, and re-layouts  2.8 us
  transfers between devices with their start and end apart: 19, of which 6 were waited for; matrix products, arithmetic and copies ran while one was open for 1% of the time, Pallas kernels for 37%

profile of v2, /device:TPU:0, one launch (start us, length us, event | category | flops | bytes accessed | tf_op | source)
XLA Modules:
  0.0 111.7 jit_solution(5425041187750841911)
XLA Ops:
  0.6 0.0 copy-start.14
  0.6 2.0 %pack.1 = (bf16[16,4096]{1,0:T(8,128)(2,1)}, bf16[16,4096]{1,0:T(8,128)(2,1)}) custom-call(bf16[128,4096]{1,0:T(8,128)(2,1)} %ql.5, bf16[128,4096]{1,0:T(8,128)(2,1)} %kl.5, bf16[128,4096]{1,0:T(8,128)(2,1)} %vl.5, bf16[128,4096]{1,0:T(8,128)(2,1)} %ql.5, bf16[128,4096]{1,0:T(8,128)(2,1)} %kl.5, bf16[128,4096]{1,0:T(8,128)(2,1)} %vl.5, bf16[128,4096]{1,0:T(8,128)(2,1)} %g_ref.11), custom_call_target="tpu_custom_call" | custom-call | bytes 1179648 | tf_op jit(solution)/shard_map/pack/pallas_call | solution.py:54
  2.7 5.0 %collective-permute-start = (bf16[16,4096]{1,0:T(8,128)(2,1)}, bf16[16,4096]{1,0:T(8,128)(2,1)S(1)}, u32[]{:S(2)}, u32[]{:S(2)}) collective-permute-start(bf16[16,4096]{1,0:T(8,128)(2,1)} %get-tuple-element.64), channel_id=1, source_target_pairs={{0,1},{1,2},{2,3},{3,4},{4,5},{5,6},{6,7},{7,8},{8,9},{9,10},{10,1... | collective-permute-start | bytes 393224 | tf_op jit(solution)/shard_map/ppermute | solution.py:362
  7.6 0.5 broadcast_xor_fusion.cols
  8.2 0.6 pad_add_fusion.idx
  8.7 1.9 %collective-permute-done.prev_ref = bf16[16,4096]{1,0:T(8,128)(2,1)S(1)} collective-permute-done((bf16[16,4096]{1,0:T(8,128)(2,1)}, bf16[16,4096]{1,0:T(8,128)(2,1)S(1)}, u32[]{:S(2)}, u32[]{:S(2)}) %collective-permute-start) | collective-permute-done | bytes 131104 | tf_op jit(solution)/shard_map/ppermute | solution.py:362
  10.7 0.7 copy-done.4
  11.3 5.9 %states.3 = (bf16[128,2048]{1,0:T(8,128)(2,1)}, bf16[128,2048]{1,0:T(8,128)(2,1)}, bf16[128,2048]{1,0:T(8,128)(2,1)}, bf16[4,2,128,128]{3,2,1,0:T(8,128)(2,1)}, ...) custom-call(s32[2]{0:T(128)} %pad_add_fusion.idx, ...), custom_call_target="tpu_custom_call" | custom-call | flops 134217728 | bytes 4718592 | tf_op jit(solution)/shard_map/states/pallas_call | solution.py:105
  17.2 3.4 %collective-permute-start.2 = (bf16[4,2,128,128]{3,2,1,0:T(8,128)(2,1)}, bf16[4,2,128,128]{3,2,1,0:T(8,128)(2,1)S(1)}, u32[]{:S(2)}, u32[]{:S(2)}) collective-permute-start(bf16[4,2,128,128]{3,2,1,0:T(8,128)(2,1)} %get-tuple-element.69), channel_id=1, source_target_pairs={{0,2},{1,3},{2,0},{3,1},{4,6},{5,7},{6,4},{7,5},{8,10},{9,11},{10,... | collective-permute-start | bytes 786440 | tf_op jit(solution)/shard_map/ppermute | solution.py:356
  20.6 1.3 %collective-permute-start.8 = (bf16[16,4096]{1,0:T(8,128)(2,1)S(1)}, bf16[16,4096]{1,0:T(8,128)(2,1)S(1)}, u32[]{:S(2)}, u32[]{:S(2)}) collective-permute-start(bf16[16,4096]{1,0:T(8,128)(2,1)S(1)} %copy-done.12), channel_id=1, source_target_pairs={{1,0},{2,1},{3,2},{4,3},{5,4},{6,5},{7,6},{8,7},{9,8},{10,9},{11,1... | collective-permute-start | bytes 393224 | tf_op jit(solution)/shard_map/ppermute | solution.py:363
  21.9 0.5 broadcast_xor_fusion.1.cols
  22.4 2.5 %collective-permute-start.6 = (bf16[4,2,128,128]{3,2,1,0:T(8,128)(2,1)}, bf16[4,2,128,128]{3,2,1,0:T(8,128)(2,1)S(1)}, u32[]{:S(2)}, u32[]{:S(2)}) collective-permute-start(bf16[4,2,128,128]{3,2,1,0:T(8,128)(2,1)} %get-tuple-element.73), channel_id=1, source_target_pairs={{0,6},{1,7},{2,4},{3,5},{4,2},{5,3},{6,0},{7,1},{8,14},{9,15},{10,... | collective-permute-start | bytes 786440 | tf_op jit(solution)/shard_map/ppermute | solution.py:356
  24.9 5.9 %states.2 = (bf16[128,2048]{1,0:T(8,128)(2,1)}, bf16[128,2048]{1,0:T(8,128)(2,1)}, bf16[128,2048]{1,0:T(8,128)(2,1)}, bf16[4,2,128,128]{3,2,1,0:T(8,128)(2,1)}, ...) custom-call(s32[2]{0:T(128)} %pad_add_fusion.idx, ...), custom_call_target="tpu_custom_call" | custom-call | flops 134217728 | bytes 4718592 | tf_op jit(solution)/shard_map/states/pallas_call | solution.py:105
  30.9 0.2 collective-permute-start.1
  31.1 1.7 %collective-permute-start.3 = (bf16[4,2,128,128]{3,2,1,0:T(8,128)(2,1)}, bf16[4,2,128,128]{3,2,1,0:T(8,128)(2,1)S(1)}, u32[]{:S(2)}, u32[]{:S(2)}) collective-permute-start(bf16[4,2,128,128]{3,2,1,0:T(8,128)(2,1)} %get-tuple-element.70), channel_id=1, source_target_pairs={{0,3},{1,2},{2,1},{3,0},{4,7},{5,6},{6,5},{7,4},{8,11},{9,10},{10,... | collective-permute-start | bytes 786440 | tf_op jit(solution)/shard_map/ppermute | solution.py:356
  32.8 0.0 collective-permute-done.2.refs_2_
  32.8 0.9 collective-permute-start.5
  33.7 0.0 collective-permute-done.4.refs_4_
  33.7 1.9 %collective-permute-start.7 = (bf16[4,2,128,128]{3,2,1,0:T(8,128)(2,1)}, bf16[4,2,128,128]{3,2,1,0:T(8,128)(2,1)S(1)}, u32[]{:S(2)}, u32[]{:S(2)}) collective-permute-start(bf16[4,2,128,128]{3,2,1,0:T(8,128)(2,1)} %get-tuple-element.74), channel_id=1, source_target_pairs={{0,7},{1,6},{2,5},{3,4},{4,3},{5,2},{6,1},{7,0},{8,15},{9,14},{10,... | collective-permute-start | bytes 786440 | tf_op jit(solution)/shard_map/ppermute | solution.py:356
  35.6 14.2 %intra.2 = (f32[16,3,144,128]{3,2,1,0:T(8,128)}, bf16[16,2048]{1,0:T(8,128)(2,1)}, bf16[16,2048]{1,0:T(8,128)(2,1)}, bf16[16,2048]{1,0:T(8,128)(2,1)}) custom-call(s32[4]{0:T(128)} %broadcast_xor_fusion.1.cols, bf16[128,2048]{1,0:T(8,128)(2,1)} %get-tuple-element.75.qf, bf16[128,2048]{1,0:T(8,128)(2,1)} %get-tuple-element.65.kf, ...), custom_call_target="tpu_custom_call" | custom-call | flops 402653184 | bytes 5636096 | tf_op jit(solution)/shard_map/intra/pallas_call | solution.py:192
  49.9 0.0 collective-permute-done.6.refs_6_
  49.9 0.0 collective-permute-done.1.refs_1_
  49.9 0.3 collective-permute-done.5.refs_5_
  50.2 5.1 %collective-permute-done.7.refs_7_ = bf16[4,2,128,128]{3,2,1,0:T(8,128)(2,1)S(1)} collective-permute-done((bf16[4,2,128,128]{3,2,1,0:T(8,128)(2,1)}, bf16[4,2,128,128]{3,2,1,0:T(8,128)(2,1)S(1)}, u32[]{:S(2)}, u32[]{:S(2)}) %collective-permute-start.7) | collective-permute-done | bytes 262176 | tf_op jit(solution)/shard_map/ppermute | solution.py:356
  55.4 0.8 sums.1
  56.2 2.3 %collective-permute-start.9 = (bf16[4,128,128]{2,1,0:T(8,128)(2,1)S(1)}, bf16[4,128,128]{2,1,0:T(8,128)(2,1)S(1)}, u32[]{:S(2)}, u32[]{:S(2)}) collective-permute-start(bf16[4,128,128]{2,1,0:T(8,128)(2,1)S(1)} %get-tuple-element.98), channel_id=1, source_target_pairs={{0,8},{8,0},{16,24},{24,16},{1,9},{9,1},{17,25},{25,17},{2,10},{10... | collective-permute-start | bytes 393224 | tf_op jit(solution)/shard_map/ppermute | solution.py:356
  58.5 2.4 %collective-permute-start.11 = (bf16[4,128,128]{2,1,0:T(8,128)(2,1)S(1)}, bf16[4,128,128]{2,1,0:T(8,128)(2,1)S(1)}, u32[]{:S(2)}, u32[]{:S(2)}) collective-permute-start(bf16[4,128,128]{2,1,0:T(8,128)(2,1)S(1)} %get-tuple-element.99), channel_id=1, source_target_pairs={{0,24},{8,16},{16,8},{24,0},{1,25},{9,17},{17,9},{25,1},{2,26},{10... | collective-permute-start | bytes 393224 | tf_op jit(solution)/shard_map/ppermute | solution.py:356
  60.8 0.1 collective-permute-start.10
  61.0 14.2 %intra.3 = (f32[16,3,144,128]{3,2,1,0:T(8,128)}, bf16[16,2048]{1,0:T(8,128)(2,1)}, bf16[16,2048]{1,0:T(8,128)(2,1)}, bf16[16,2048]{1,0:T(8,128)(2,1)}) custom-call(s32[4]{0:T(128)} %broadcast_xor_fusion.cols, bf16[128,2048]{1,0:T(8,128)(2,1)} %get-tuple-element.100.qf, bf16[128,2048]{1,0:T(8,128)(2,1)} %get-tuple-element.101.kf, ...), custom_call_target="tpu_custom_call" | custom-call | flops 402653184 | bytes 5636096 | tf_op jit(solution)/shard_map/intra/pallas_call | solution.py:192
  75.2 0.0 collective-permute-done.9.refs_8_
  75.2 0.0 collective-permute-done.11.refs_10_
  75.2 1.4 %members.1 = (bf16[4,2,128,128]{3,2,1,0:T(8,128)(2,1)S(1)}, bf16[4,2,128,128]{3,2,1,0:T(8,128)(2,1)S(1)}, bf16[4,2,128,128]{3,2,1,0:T(8,128)(2,1)S(1)}, bf16[4,2...) custom-call(s32[2]{0:T(128)S(1)} %copy-done.2, ...), custom_call_target="tpu_custom_call" | custom-call | bytes 4587520 | tf_op jit(solution)/shard_map/members/pallas_call | solution.py:254
  76.6 0.7 copy-done.1
  77.3 1.4 %collective-permute-start.16 = (bf16[4,2,128,128]{3,2,1,0:T(8,128)(2,1)S(1)}, bf16[4,2,128,128]{3,2,1,0:T(8,128)(2,1)S(1)}, u32[]{:S(2)}, u32[]{:S(2)}) collective-permute-start(bf16[4,2,128,128]{3,2,1,0:T(8,128)(2,1)S(1)} %get-tuple-element.118), channel_id=1, source_target_pairs={{0,2},{1,3},{2,0},{3,1},{4,6},{5,7},{6,4},{7,5},{8,10},{9,11},{10,... | collective-permute-start | bytes 786440 | tf_op jit(solution)/shard_map/ppermute | solution.py:356
  78.7 0.0 collective-permute-start.17
  78.7 0.7 collective-permute-start.18
  79.4 1.4 %collective-permute-start.12 = (bf16[4,2,128,128]{3,2,1,0:T(8,128)(2,1)S(1)}, bf16[4,2,128,128]{3,2,1,0:T(8,128)(2,1)S(1)}, u32[]{:S(2)}, u32[]{:S(2)}) collective-permute-start(bf16[4,2,128,128]{3,2,1,0:T(8,128)(2,1)S(1)} %get-tuple-element.110), channel_id=1, source_target_pairs={{0,1},{1,0},{2,3},{3,2},{4,5},{5,4},{6,7},{7,6},{8,9},{9,8},{10,11... | collective-permute-start | bytes 786440 | tf_op jit(solution)/shard_map/ppermute | solution.py:356
  80.8 1.5 %collective-permute-start.13 = (bf16[4,2,128,128]{3,2,1,0:T(8,128)(2,1)S(1)}, bf16[4,2,128,128]{3,2,1,0:T(8,128)(2,1)S(1)}, u32[]{:S(2)}, u32[]{:S(2)}) collective-permute-start(bf16[4,2,128,128]{3,2,1,0:T(8,128)(2,1)S(1)} %get-tuple-element.111), channel_id=1, source_target_pairs={{0,3},{1,2},{2,1},{3,0},{4,7},{5,6},{6,5},{7,4},{8,11},{9,10},{10,... | collective-permute-start | bytes 786440 | tf_op jit(solution)/shard_map/ppermute | solution.py:356
  82.3 4.2 %collective-permute-done.16.rest_0_ = bf16[4,2,128,128]{3,2,1,0:T(8,128)(2,1)S(1)} collective-permute-done((bf16[4,2,128,128]{3,2,1,0:T(8,128)(2,1)S(1)}, bf16[4,2,128,128]{3,2,1,0:T(8,128)(2,1)S(1)}, u32[]{:S(2)}, u32[]{:S(2)}) %collective-permute-start.16) | collective-permute-done | bytes 262176 | tf_op jit(solution)/shard_map/ppermute | solution.py:356
  86.5 0.0 collective-permute-start.14
  86.5 0.0 collective-permute-done.17.rest_1_
  86.5 2.6 %collective-permute-start.15 = (bf16[4,2,128,128]{3,2,1,0:T(8,128)(2,1)S(1)}, bf16[4,2,128,128]{3,2,1,0:T(8,128)(2,1)S(1)}, u32[]{:S(2)}, u32[]{:S(2)}) collective-permute-start(bf16[4,2,128,128]{3,2,1,0:T(8,128)(2,1)S(1)} %get-tuple-element.113), channel_id=1, source_target_pairs={{0,7},{1,6},{2,5},{3,4},{4,3},{5,2},{6,1},{7,0},{8,15},{9,14},{10,... | collective-permute-start | bytes 786440 | tf_op jit(solution)/shard_map/ppermute | solution.py:356
  89.1 6.5 %collective-permute-done.18.rest_2_ = bf16[4,2,128,128]{3,2,1,0:T(8,128)(2,1)S(1)} collective-permute-done((bf16[4,2,128,128]{3,2,1,0:T(8,128)(2,1)S(1)}, bf16[4,2,128,128]{3,2,1,0:T(8,128)(2,1)S(1)}, u32[]{:S(2)}, u32[]{:S(2)}) %collective-permute-start.18) | collective-permute-done | bytes 262176 | tf_op jit(solution)/shard_map/ppermute | solution.py:356
  95.6 0.7 copy-done.11
  96.3 6.5 %grads.2 = (bf16[128,4096]{1,0:T(8,128)(2,1)}, bf16[128,4096]{1,0:T(8,128)(2,1)}, bf16[128,4096]{1,0:T(8,128)(2,1)}) custom-call(s32[4]{0:T(128)} %broadcast_xor_fusion.cols, bf16[128,2048]{1,0:T(8,128)(2,1)} %get-tuple-element.101.kf, bf16[128,2048]{1,0:T(8,128)(2,1)} %get-tuple-element.102.vf, bf16[128,4096]{1,0:T(8,128)(2,1)} %g_ref.11, ...), custom_call_target="tpu_custom_call" | custom-call | flops 226492416 | bytes 7733248 | tf_op jit(solution)/shard_map/grads/pallas_call | solution.py:317
  102.9 1.5 %collective-permute-done.15.rest_3_ = bf16[4,2,128,128]{3,2,1,0:T(8,128)(2,1)S(1)} collective-permute-done((bf16[4,2,128,128]{3,2,1,0:T(8,128)(2,1)S(1)}, bf16[4,2,128,128]{3,2,1,0:T(8,128)(2,1)S(1)}, u32[]{:S(2)}, u32[]{:S(2)}) %collective-permute-start.15) | collective-permute-done | bytes 262176 | tf_op jit(solution)/shard_map/ppermute | solution.py:356
  104.4 0.7 copy-done.8
  105.1 6.5 %grads.3 = (bf16[128,4096]{1,0:T(8,128)(2,1)}, bf16[128,4096]{1,0:T(8,128)(2,1)}, bf16[128,4096]{1,0:T(8,128)(2,1)}) custom-call(s32[4]{0:T(128)} %broadcast_xor_fusion.1.cols, bf16[128,2048]{1,0:T(8,128)(2,1)} %get-tuple-element.65.kf, bf16[128,2048]{1,0:T(8,128)(2,1)} %get-tuple-element.66.vf, ...), custom_call_target="tpu_custom_call", output_to_operand_aliasing={{0}: (15, {}), {1}: (16, {}), {2}: (17, {})} | custom-call | flops 226492416 | bytes 7733248 | tf_op jit(solution)/shard_map/grads/pallas_call | solution.py:317
  (32 shorter events, 0.1 us)
Async XLA Ops:
  0.6 7.0 %copy-start.14 = (s32[4]{0:T(128)S(1)}, s32[4]{0:T(128)}, u32[]{:S(2)}) copy-start(s32[4]{0:T(128)} %constant.19.clone) | copy-start | bytes 52
  2.6 18.0 %copy-start.12 = (bf16[16,4096]{1,0:T(8,128)(2,1)S(1)}, bf16[16,4096]{1,0:T(8,128)(2,1)}, u32[]{:S(2)}) copy-start(bf16[16,4096]{1,0:T(8,128)(2,1)} %get-tuple-element.76) | copy-start | bytes 393220
  2.6 19.2 %copy-start.13 = (s32[4]{0:T(128)S(1)}, s32[4]{0:T(128)}, u32[]{:S(2)}) copy-start(s32[4]{0:T(128)} %constant.18.clone) | copy-start | bytes 52
  2.7 8.0 %collective-permute-start = (bf16[16,4096]{1,0:T(8,128)(2,1)}, bf16[16,4096]{1,0:T(8,128)(2,1)S(1)}, u32[]{:S(2)}, u32[]{:S(2)}) collective-permute-start(bf16[16,4096]{1,0:T(8,128)(2,1)} %get-tuple-element.64), channel_id=1, source_target_pairs={{0,1},{1,2},{2,3},{3,4},{4,5},{5,6},{6,7},{7,8},{8,9},{9,10},{10,1... | collective-permute-start | bytes 393224 | tf_op jit(solution)/shard_map/ppermute | solution.py:362
  10.7 0.7 copy-start.4
  17.2 15.6 %collective-permute-start.2 = (bf16[4,2,128,128]{3,2,1,0:T(8,128)(2,1)}, bf16[4,2,128,128]{3,2,1,0:T(8,128)(2,1)S(1)}, u32[]{:S(2)}, u32[]{:S(2)}) collective-permute-start(bf16[4,2,128,128]{3,2,1,0:T(8,128)(2,1)} %get-tuple-element.69), channel_id=1, source_target_pairs={{0,2},{1,3},{2,0},{3,1},{4,6},{5,7},{6,4},{7,5},{8,10},{9,11},{10,... | collective-permute-start | bytes 786440 | tf_op jit(solution)/shard_map/ppermute | solution.py:356
  20.6 13.1 %collective-permute-start.4 = (bf16[4,2,128,128]{3,2,1,0:T(8,128)(2,1)}, bf16[4,2,128,128]{3,2,1,0:T(8,128)(2,1)S(1)}, u32[]{:S(2)}, u32[]{:S(2)}) collective-permute-start(bf16[4,2,128,128]{3,2,1,0:T(8,128)(2,1)} %get-tuple-element.71), channel_id=1, source_target_pairs={{0,4},{1,5},{2,6},{3,7},{4,0},{5,1},{6,2},{7,3},{8,12},{9,13},{10,... | collective-permute-start | bytes 786440 | tf_op jit(solution)/shard_map/ppermute | solution.py:356
  20.6 10.5 %collective-permute-start.8 = (bf16[16,4096]{1,0:T(8,128)(2,1)S(1)}, bf16[16,4096]{1,0:T(8,128)(2,1)S(1)}, u32[]{:S(2)}, u32[]{:S(2)}) collective-permute-start(bf16[16,4096]{1,0:T(8,128)(2,1)S(1)} %copy-done.12), channel_id=1, source_target_pairs={{1,0},{2,1},{3,2},{4,3},{5,4},{6,5},{7,6},{8,7},{9,8},{10,9},{11,1... | collective-permute-start | bytes 393224 | tf_op jit(solution)/shard_map/ppermute | solution.py:363
  22.4 27.4 %collective-permute-start.6 = (bf16[4,2,128,128]{3,2,1,0:T(8,128)(2,1)}, bf16[4,2,128,128]{3,2,1,0:T(8,128)(2,1)S(1)}, u32[]{:S(2)}, u32[]{:S(2)}) collective-permute-start(bf16[4,2,128,128]{3,2,1,0:T(8,128)(2,1)} %get-tuple-element.73), channel_id=1, source_target_pairs={{0,6},{1,7},{2,4},{3,5},{4,2},{5,3},{6,0},{7,1},{8,14},{9,15},{10,... | collective-permute-start | bytes 786440 | tf_op jit(solution)/shard_map/ppermute | solution.py:356
  30.8 24.5 %copy-start = (bf16[4,2,128,128]{3,2,1,0:T(8,128)(2,1)S(1)}, bf16[4,2,128,128]{3,2,1,0:T(8,128)(2,1)}, u32[]{:S(2)}) copy-start(bf16[4,2,128,128]{3,2,1,0:T(8,128)(2,1)} %get-tuple-element.85.refs_0_) | copy-start | bytes 786436
  30.9 24.5 %copy-start.2 = (s32[2]{0:T(128)S(1)}, s32[2]{0:T(128)}, u32[]{:S(2)}) copy-start(s32[2]{0:T(128)} %pad_add_fusion.idx) | copy-start | bytes 28
  30.9 19.0 %collective-permute-start.1 = (bf16[4,2,128,128]{3,2,1,0:T(8,128)(2,1)}, bf16[4,2,128,128]{3,2,1,0:T(8,128)(2,1)S(1)}, u32[]{:S(2)}, u32[]{:S(2)}) collective-permute-start(bf16[4,2,128,128]{3,2,1,0:T(8,128)(2,1)} %get-tuple-element.68), channel_id=1, source_target_pairs={{0,1},{1,0},{2,3},{3,2},{4,5},{5,4},{6,7},{7,6},{8,9},{9,8},{10,11... | collective-permute-start | bytes 786440 | tf_op jit(solution)/shard_map/ppermute | solution.py:356
  31.1 4.6 %copy-start.3 = (bf16[16,4096]{1,0:T(8,128)(2,1)}, bf16[16,4096]{1,0:T(8,128)(2,1)S(1)}, u32[]{:S(2)}) copy-start(bf16[16,4096]{1,0:T(8,128)(2,1)S(1)} %collective-permute-done.8.next_ref) | copy-start | bytes 393220
  31.1 18.8 %collective-permute-start.3 = (bf16[4,2,128,128]{3,2,1,0:T(8,128)(2,1)}, bf16[4,2,128,128]{3,2,1,0:T(8,128)(2,1)S(1)}, u32[]{:S(2)}, u32[]{:S(2)}) collective-permute-start(bf16[4,2,128,128]{3,2,1,0:T(8,128)(2,1)} %get-tuple-element.70), channel_id=1, source_target_pairs={{0,3},{1,2},{2,1},{3,0},{4,7},{5,6},{6,5},{7,4},{8,11},{9,10},{10,... | collective-permute-start | bytes 786440 | tf_op jit(solution)/shard_map/ppermute | solution.py:356
  32.8 17.4 %collective-permute-start.5 = (bf16[4,2,128,128]{3,2,1,0:T(8,128)(2,1)}, bf16[4,2,128,128]{3,2,1,0:T(8,128)(2,1)S(1)}, u32[]{:S(2)}, u32[]{:S(2)}) collective-permute-start(bf16[4,2,128,128]{3,2,1,0:T(8,128)(2,1)} %get-tuple-element.72), channel_id=1, source_target_pairs={{0,5},{1,4},{2,7},{3,6},{4,1},{5,0},{6,3},{7,2},{8,13},{9,12},{10,... | collective-permute-start | bytes 786440 | tf_op jit(solution)/shard_map/ppermute | solution.py:356
  33.7 21.6 %collective-permute-start.7 = (bf16[4,2,128,128]{3,2,1,0:T(8,128)(2,1)}, bf16[4,2,128,128]{3,2,1,0:T(8,128)(2,1)S(1)}, u32[]{:S(2)}, u32[]{:S(2)}) collective-permute-start(bf16[4,2,128,128]{3,2,1,0:T(8,128)(2,1)} %get-tuple-element.74), channel_id=1, source_target_pairs={{0,7},{1,6},{2,5},{3,4},{4,3},{5,2},{6,1},{7,0},{8,15},{9,14},{10,... | collective-permute-start | bytes 786440 | tf_op jit(solution)/shard_map/ppermute | solution.py:356
  56.2 19.0 %collective-permute-start.9 = (bf16[4,128,128]{2,1,0:T(8,128)(2,1)S(1)}, bf16[4,128,128]{2,1,0:T(8,128)(2,1)S(1)}, u32[]{:S(2)}, u32[]{:S(2)}) collective-permute-start(bf16[4,128,128]{2,1,0:T(8,128)(2,1)S(1)} %get-tuple-element.98), channel_id=1, source_target_pairs={{0,8},{8,0},{16,24},{24,16},{1,9},{9,1},{17,25},{25,17},{2,10},{10... | collective-permute-start | bytes 393224 | tf_op jit(solution)/shard_map/ppermute | solution.py:356
  58.5 16.7 %collective-permute-start.11 = (bf16[4,128,128]{2,1,0:T(8,128)(2,1)S(1)}, bf16[4,128,128]{2,1,0:T(8,128)(2,1)S(1)}, u32[]{:S(2)}, u32[]{:S(2)}) collective-permute-start(bf16[4,128,128]{2,1,0:T(8,128)(2,1)S(1)} %get-tuple-element.99), channel_id=1, source_target_pairs={{0,24},{8,16},{16,8},{24,0},{1,25},{9,17},{17,9},{25,1},{2,26},{10... | collective-permute-start | bytes 393224 | tf_op jit(solution)/shard_map/ppermute | solution.py:356
  60.8 14.4 %collective-permute-start.10 = (bf16[4,128,128]{2,1,0:T(8,128)(2,1)S(1)}, bf16[4,128,128]{2,1,0:T(8,128)(2,1)S(1)}, u32[]{:S(2)}, u32[]{:S(2)}) collective-permute-start(bf16[4,128,128]{2,1,0:T(8,128)(2,1)S(1)} %get-tuple-element.99), channel_id=1, source_target_pairs={{0,16},{8,24},{16,0},{24,8},{1,17},{9,25},{17,1},{25,9},{2,18},{10... | collective-permute-start | bytes 393224 | tf_op jit(solution)/shard_map/ppermute | solution.py:356
  76.6 0.7 copy-start.1
  77.3 9.2 %collective-permute-start.16 = (bf16[4,2,128,128]{3,2,1,0:T(8,128)(2,1)S(1)}, bf16[4,2,128,128]{3,2,1,0:T(8,128)(2,1)S(1)}, u32[]{:S(2)}, u32[]{:S(2)}) collective-permute-start(bf16[4,2,128,128]{3,2,1,0:T(8,128)(2,1)S(1)} %get-tuple-element.118), channel_id=1, source_target_pairs={{0,2},{1,3},{2,0},{3,1},{4,6},{5,7},{6,4},{7,5},{8,10},{9,11},{10,... | collective-permute-start | bytes 786440 | tf_op jit(solution)/shard_map/ppermute | solution.py:356
  78.7 7.8 %collective-permute-start.17 = (bf16[4,2,128,128]{3,2,1,0:T(8,128)(2,1)S(1)}, bf16[4,2,128,128]{3,2,1,0:T(8,128)(2,1)S(1)}, u32[]{:S(2)}, u32[]{:S(2)}) collective-permute-start(bf16[4,2,128,128]{3,2,1,0:T(8,128)(2,1)S(1)} %get-tuple-element.119), channel_id=1, source_target_pairs={{0,4},{1,5},{2,6},{3,7},{4,0},{5,1},{6,2},{7,3},{8,12},{9,13},{10,... | collective-permute-start | bytes 786440 | tf_op jit(solution)/shard_map/ppermute | solution.py:356
  78.7 16.9 %collective-permute-start.18 = (bf16[4,2,128,128]{3,2,1,0:T(8,128)(2,1)S(1)}, bf16[4,2,128,128]{3,2,1,0:T(8,128)(2,1)S(1)}, u32[]{:S(2)}, u32[]{:S(2)}) collective-permute-start(bf16[4,2,128,128]{3,2,1,0:T(8,128)(2,1)S(1)} %get-tuple-element.120), channel_id=1, source_target_pairs={{0,6},{1,7},{2,4},{3,5},{4,2},{5,3},{6,0},{7,1},{8,14},{9,15},{10,... | collective-permute-start | bytes 786440 | tf_op jit(solution)/shard_map/ppermute | solution.py:356
  79.4 23.4 %collective-permute-start.12 = (bf16[4,2,128,128]{3,2,1,0:T(8,128)(2,1)S(1)}, bf16[4,2,128,128]{3,2,1,0:T(8,128)(2,1)S(1)}, u32[]{:S(2)}, u32[]{:S(2)}) collective-permute-start(bf16[4,2,128,128]{3,2,1,0:T(8,128)(2,1)S(1)} %get-tuple-element.110), channel_id=1, source_target_pairs={{0,1},{1,0},{2,3},{3,2},{4,5},{5,4},{6,7},{7,6},{8,9},{9,8},{10,11... | collective-permute-start | bytes 786440 | tf_op jit(solution)/shard_map/ppermute | solution.py:356
  80.8 22.0 %collective-permute-start.13 = (bf16[4,2,128,128]{3,2,1,0:T(8,128)(2,1)S(1)}, bf16[4,2,128,128]{3,2,1,0:T(8,128)(2,1)S(1)}, u32[]{:S(2)}, u32[]{:S(2)}) collective-permute-start(bf16[4,2,128,128]{3,2,1,0:T(8,128)(2,1)S(1)} %get-tuple-element.111), channel_id=1, source_target_pairs={{0,3},{1,2},{2,1},{3,0},{4,7},{5,6},{6,5},{7,4},{8,11},{9,10},{10,... | collective-permute-start | bytes 786440 | tf_op jit(solution)/shard_map/ppermute | solution.py:356
  86.5 9.1 %copy-start.9 = (bf16[4,2,128,128]{3,2,1,0:T(8,128)(2,1)}, bf16[4,2,128,128]{3,2,1,0:T(8,128)(2,1)S(1)}, u32[]{:S(2)}) copy-start(bf16[4,2,128,128]{3,2,1,0:T(8,128)(2,1)S(1)} %collective-permute-done.16.rest_0_) | copy-start | bytes 786436
  86.5 16.4 %collective-permute-start.14 = (bf16[4,2,128,128]{3,2,1,0:T(8,128)(2,1)S(1)}, bf16[4,2,128,128]{3,2,1,0:T(8,128)(2,1)S(1)}, u32[]{:S(2)}, u32[]{:S(2)}) collective-permute-start(bf16[4,2,128,128]{3,2,1,0:T(8,128)(2,1)S(1)} %get-tuple-element.112), channel_id=1, source_target_pairs={{0,5},{1,4},{2,7},{3,6},{4,1},{5,0},{6,3},{7,2},{8,13},{9,12},{10,... | collective-permute-start | bytes 786440 | tf_op jit(solution)/shard_map/ppermute | solution.py:356
  86.5 9.1 %copy-start.10 = (bf16[4,2,128,128]{3,2,1,0:T(8,128)(2,1)}, bf16[4,2,128,128]{3,2,1,0:T(8,128)(2,1)S(1)}, u32[]{:S(2)}) copy-start(bf16[4,2,128,128]{3,2,1,0:T(8,128)(2,1)S(1)} %collective-permute-done.17.rest_1_) | copy-start | bytes 786436
  86.5 17.9 %collective-permute-start.15 = (bf16[4,2,128,128]{3,2,1,0:T(8,128)(2,1)S(1)}, bf16[4,2,128,128]{3,2,1,0:T(8,128)(2,1)S(1)}, u32[]{:S(2)}, u32[]{:S(2)}) collective-permute-start(bf16[4,2,128,128]{3,2,1,0:T(8,128)(2,1)S(1)} %get-tuple-element.113), channel_id=1, source_target_pairs={{0,7},{1,6},{2,5},{3,4},{4,3},{5,2},{6,1},{7,0},{8,15},{9,14},{10,... | collective-permute-start | bytes 786440 | tf_op jit(solution)/shard_map/ppermute | solution.py:356
  95.6 0.7 copy-start.11
  102.8 1.6 %copy-start.5 = (bf16[4,2,128,128]{3,2,1,0:T(8,128)(2,1)}, bf16[4,2,128,128]{3,2,1,0:T(8,128)(2,1)S(1)}, u32[]{:S(2)}) copy-start(bf16[4,2,128,128]{3,2,1,0:T(8,128)(2,1)S(1)} %collective-permute-done.12.rest_0_) | copy-start | bytes 786436
  102.9 1.6 %copy-start.6 = (bf16[4,2,128,128]{3,2,1,0:T(8,128)(2,1)}, bf16[4,2,128,128]{3,2,1,0:T(8,128)(2,1)S(1)}, u32[]{:S(2)}) copy-start(bf16[4,2,128,128]{3,2,1,0:T(8,128)(2,1)S(1)} %collective-permute-done.13.rest_1_) | copy-start | bytes 786436
  102.9 1.6 %copy-start.7 = (bf16[4,2,128,128]{3,2,1,0:T(8,128)(2,1)}, bf16[4,2,128,128]{3,2,1,0:T(8,128)(2,1)S(1)}, u32[]{:S(2)}) copy-start(bf16[4,2,128,128]{3,2,1,0:T(8,128)(2,1)S(1)} %collective-permute-done.14.rest_2_) | copy-start | bytes 786436
  104.4 0.7 copy-start.8

commit v3 on v0

v3 whole, which is shorter than its diff:
```python
import functools
import math

import jax
import jax.numpy as jnp
from jax import lax
from jax.experimental import pallas as pl
from jax.experimental.pallas import tpu as pltpu
from jax.sharding import Mesh, PartitionSpec as P

HEAD = 128
KERNEL = 4
REACH = KERNEL - 1
CORES = 2
PAD = 8
TILE = 16
EDGE = 16
MIB = 1024 * 1024

F32 = jnp.float32
BF16 = jnp.bfloat16


def dot(a, b, ca, cb):
    return lax.dot_general(a, b, (((ca,), (cb,)), ((), ())), preferred_element_type=F32)


def shape(dims, dtype=BF16):
    return jax.ShapeDtypeStruct(dims, dtype)


def far(x):
    return pltpu.with_memory_space_constraint(x, pltpu.HBM)


def params(mib=20):
    return pltpu.CompilerParams(vmem_limit_bytes=mib * MIB)


def cost(flops, moved):
    return pl.CostEstimate(flops=int(flops), bytes_accessed=int(moved), transcendentals=0)


def pack_kernel(q_ref, k_ref, v_ref, g_ref, tail_ref, lead_ref, x_ref, sems):
    rows = q_ref.shape[0]
    copies = []
    for i, ref in enumerate((q_ref, k_ref, v_ref)):
        copies.append((ref.at[pl.ds(rows - EDGE, EDGE)], x_ref.at[i]))
    for i, ref in enumerate((q_ref, k_ref, v_ref, g_ref)):
        copies.append((ref.at[pl.ds(0, EDGE)], x_ref.at[3 + i]))
    copies = [pltpu.make_async_copy(a, b, sems.at[i]) for i, (a, b) in enumerate(copies)]
    for copy in copies:
        copy.start()

    def rows_of(first, count, start):
        parts = [x_ref[first + i].astype(F32)[start : start + REACH] for i in range(count)]
        fill = jnp.zeros((EDGE - REACH * count, parts[0].shape[1]), F32)
        return jnp.concatenate(parts + [fill], 0).astype(BF16)

    for copy in copies[:3]:
        copy.wait()
    tail_ref[...] = rows_of(0, 3, EDGE - REACH)
    for copy in copies[3:]:
        copy.wait()
    lead_ref[...] = rows_of(3, 4, 0)


def pack(raws):
    width = raws[0].shape[1]
    return pl.pallas_call(
        pack_kernel,
        in_specs=[pl.BlockSpec(memory_space=pltpu.HBM)] * 4,
        out_specs=[pl.BlockSpec(memory_space=pltpu.VMEM)] * 2,
        out_shape=[shape((EDGE, width))] * 2,
        scratch_shapes=[pltpu.VMEM((7, EDGE, width), BF16), pltpu.SemaphoreType.DMA((7,))],
        compiler_params=params(),
        cost_estimate=cost(0, 9 * 2 * EDGE * width),
        name="pack",
    )(*[far(x) for x in raws])


def lanes(start, width=HEAD):
    return pl.ds(pl.multiple_of(start, HEAD), width)


class Copies:
    def __init__(self, sems):
        self.sems, self.count = sems, 0

    def start(self, source, target):
        copy = pltpu.make_async_copy(source, target, self.sems.at[self.count])
        self.count += 1
        copy.start()
        return copy


def wait(copies):
    for copy in copies:
        copy.wait()


HBM = pl.BlockSpec(memory_space=pltpu.HBM)
VMEM = pl.BlockSpec(memory_space=pltpu.VMEM)
SMEM = pl.BlockSpec(memory_space=pltpu.SMEM)


def marked_call(kernel, name, cols, near, remote, outs, scratch=(), flops=0, behind=(), aliases=()):
    args = [*near, *remote]
    hidden = len(behind)
    total = len(args) + len(outs)

    def body(cols, *refs):
        refs[hidden + total][0] = 0
        kernel(cols, *refs[hidden : hidden + total], *refs[hidden + total + 1 :])

    def out_spec(x):
        return HBM if getattr(x, "memory_space", None) == pltpu.HBM else VMEM

    moved = sum(math.prod(x.shape) * jnp.dtype(x.dtype).itemsize for x in [*args, *outs])
    *results, mark = pl.pallas_call(
        body,
        in_specs=[SMEM] * (1 + hidden) + [VMEM] * len(near) + [HBM] * len(remote),
        out_specs=[out_spec(x) for x in outs] + [SMEM],
        out_shape=[*outs, shape((1,), jnp.int32)],
        scratch_shapes=scratch,
        input_output_aliases={1 + hidden + i: o for i, o in aliases},
        compiler_params=params(),
        cost_estimate=cost(flops, moved),
        name=name,
    )(cols, *behind, *near, *[far(x) for x in remote])
    return results, mark


def conv(x, taps, raw, before, rows):
    x[PAD - REACH : PAD] = before
    x[PAD : PAD + raw.shape[0]] = raw.astype(F32)
    mixed = taps[0:1] * x[PAD : PAD + rows]
    for j in range(1, KERNEL):
        mixed = mixed + taps[j : j + 1] * x[PAD - j : PAD - j + rows]
    return mixed.astype(BF16)


def states_kernel(peers, heads, cols, prev_ref, tq, tk, tv, *rest):
    raws, s_refs = rest[:4], rest[4:-3]
    raw_ref, x_ref, sems = rest[-3:]
    rows, width = raw_ref.shape[2:]
    copies = Copies(sems)
    loads = []
    for p in range(peers):
        c = lanes(cols[p] * width, width)
        loads.append([copies.start(raw.at[:, c], raw_ref.at[p, i]) for i, raw in enumerate(raws)])
    for p in range(peers):
        wait(loads[p])
        for h in range(heads):
            c = lanes((cols[p] * heads + h) * HEAD)
            own = slice(h * HEAD, (h + 1) * HEAD)
            prev = prev_ref[:, c].astype(F32)
            qf, kf, vf = [
                conv(
                    x_ref.at[(p * heads + h) % 4, i],
                    tap_ref[:, c].astype(F32),
                    raw_ref[p, i, :, own],
                    prev[REACH * i : REACH * (i + 1)],
                    rows,
                )
                for i, tap_ref in enumerate((tq, tk, tv))
            ]
            s_refs[p][h, 0] = dot(vf, kf, 0, 0).astype(BF16)
            s_refs[p][h, 1] = dot(raw_ref[p, 3, :, own], qf, 0, 0).astype(BF16)


def states_call(peers, heads, cols, raws, prev, taps, behind):
    rows = raws[0].shape[0]
    return marked_call(
        functools.partial(states_kernel, peers, heads),
        "states",
        cols,
        [prev, *taps],
        raws,
        [shape((heads, 2, HEAD, HEAD))] * peers,
        [
            pltpu.VMEM((peers, 4, rows, heads * HEAD), BF16),
            pltpu.VMEM((4, 3, PAD + rows, HEAD), F32),
            pltpu.SemaphoreType.DMA((peers * 4,)),
        ],
        4 * peers * heads * rows * HEAD * HEAD,
        behind,
    )


def intra_kernel(
    peers, heads, cols, prev_ref, next_ref, tq, tk, tv, q_hbm, k_hbm, v_hbm, g_hbm, _,
    d_hbm, e_hbm, f_hbm, raw_ref, d_ref, e_ref, f_ref, x_ref, sems,
):
    rows, width = raw_ref.shape[2:]
    ext = rows + EDGE
    copies = Copies(sems)
    loads = []
    for p in range(peers):
        c = lanes(cols[p] * width, width)
        raws = (q_hbm, k_hbm, v_hbm, g_hbm)
        loads.append([copies.start(raw.at[:, c], raw_ref.at[p, i]) for i, raw in enumerate(raws)])

    def order(dims):
        return lax.broadcasted_iota(jnp.int32, dims, 0), lax.broadcasted_iota(jnp.int32, dims, 1)

    row, col = order((heads * EDGE, heads * EDGE))
    same = row // EDGE == col // EDGE
    edge_lower = same & (row >= col)
    edge_strict = same & (col < row)
    row, col = order((ext, rows))
    lower = row >= col
    row, col = order((rows, rows))
    upper = col >= row
    fill = jnp.zeros((EDGE - REACH, HEAD), F32)
    saves = []
    for p in range(peers):
        wait(loads[p])
        whole = []
        for h in range(heads):
            c = lanes((cols[p] * heads + h) * HEAD)
            own = slice(h * HEAD, (h + 1) * HEAD)
            prev = prev_ref[:, c].astype(F32)
            after = next_ref[:, c].astype(F32)
            feats = []
            for i, tap_ref in enumerate((tq, tk, tv)):
                x = x_ref.at[h, i]
                ahead = slice(REACH * i, REACH * (i + 1))
                x[PAD + rows : PAD + rows + REACH] = after[ahead]
                x[PAD + rows + REACH :] = fill
                taps = tap_ref[:, c].astype(F32)
                feats.append(conv(x, taps, raw_ref[p, i, :, own], prev[ahead], ext))
            edge = jnp.concatenate([after[3 * REACH : 4 * REACH], fill], 0).astype(BF16)
            feats.append(jnp.concatenate([raw_ref[p, 3, :, own], edge], 0))
            for i in range(3):
                e_ref[p, i, :, own] = feats[1 + i][rows:]
            for i in range(2):
                f_ref[p, i, :, own] = feats[1 + i][:rows]
            whole.append(feats)
        qs, ks, vs, gs = [jnp.concatenate([f[i][rows:] for f in whole], 0) for i in range(4)]
        scores = dot(gs, vs, 1, 1)
        scores_t = dot(vs, gs, 1, 1)
        similar_t = dot(ks, qs, 1, 1)
        eq = dot(jnp.where(edge_lower, scores, 0.0).astype(BF16), ks, 1, 0)
        ek = dot(jnp.where(edge_strict, scores_t, 0.0).astype(BF16), qs, 1, 0)
        ev = dot(jnp.where(edge_strict, similar_t, 0.0).astype(BF16), gs, 1, 0)
        for h in range(heads):
            r = slice(h * EDGE, (h + 1) * EDGE)
            q, k, v, gx = whole[h]
            q, k, v, g = q[:rows], k[:rows], v[:rows], gx[:rows]
            scores = dot(gx, v, 1, 1)
            part = dot(jnp.where(lower, scores, 0.0).astype(BF16), k, 1, 0)
            d_ref[p, h, 0, :rows] = part[:rows].astype(BF16)
            d_ref[p, h, 0, rows:] = (part[rows:] + eq[r]).astype(BF16)
            scores_t = jnp.where(upper, scores[:rows].T, 0.0).astype(BF16)
            d_ref[p, h, 1, :rows] = dot(scores_t, q, 1, 0).astype(BF16)
            d_ref[p, h, 1, rows:] = (-ek[r]).astype(BF16)
            similar_t = jnp.where(upper, dot(k, q, 1, 1), 0.0).astype(BF16)
            d_ref[p, h, 2, :rows] = dot(similar_t, g, 1, 0).astype(BF16)
            d_ref[p, h, 2, rows:] = (-ev[r]).astype(BF16)
        saves.append(copies.start(d_ref.at[p], d_hbm.at[p]))
        saves.append(copies.start(e_ref.at[p], e_hbm.at[p]))
        saves.append(copies.start(f_ref.at[p], f_hbm.at[p]))
    wait(saves)


def intra_call(peers, heads, cols, raws, prev, after, taps, arrived, behind):
    rows = raws[0].shape[0]
    ext = rows + EDGE
    width = heads * HEAD
    outs = [(peers, heads, 3, ext, HEAD), (peers, 3, EDGE, width), (peers, 2, rows, width)]
    return marked_call(
        functools.partial(intra_kernel, peers, heads),
        "intra",
        cols,
        [prev, after, *taps],
        [*raws, arrived],
        [pltpu.HBM(dims, BF16) for dims in outs],
        [pltpu.VMEM((peers, 4, rows, width), BF16)]
        + [pltpu.VMEM(dims, BF16) for dims in outs]
        + [
            pltpu.VMEM((heads, 3, PAD + ext, HEAD), F32),
            pltpu.SemaphoreType.DMA((peers * 7,)),
        ],
        12 * peers * heads * rows * HEAD * HEAD,
        behind,
    )


def sums_kernel(count, idx, *refs):
    s_refs, outs = refs[:count], refs[count:]
    heads = outs[0].shape[0]
    for h in range(heads):
        total = 0.0
        for r in s_refs:
            total = total + r[h].astype(F32)
        for bit, out in enumerate(outs):
            low = (idx[0] >> bit) & 1 == 0
            out[h] = jnp.where(low, total[0], total[1]).astype(BF16)


def members_kernel(count, planes, places, idx, *refs):
    s_refs, z_refs = refs[:count], refs[count : count + planes - 1]
    outs = refs[count + planes - 1 :]

    def share(condition):
        return jnp.where(condition, 1.0, 0.0)

    lower = [share((idx[0] ^ d) < idx[0]) for d in range(1, planes)]
    weights = [
        [
            (share(idx[1 + e] < idx[1 + place]), share(idx[1 + e] > idx[1 + place]))
            for e in range(count)
        ]
        for place in places
    ]
    for h in range(z_refs[0].shape[0]):
        for top in range(0, HEAD, TILE):
            r = slice(top, top + TILE)
            base = [0.0, 0.0]
            for z_ref, low in zip(z_refs, lower):
                got = z_ref[h, r].astype(F32)
                base = [base[0] + got * low, base[1] + got * (1.0 - low)]
            states = [[s_ref[h, i, r].astype(F32) for i in range(2)] for s_ref in s_refs]
            for out, shares in zip(outs, weights):
                for i in range(2):
                    total = base[i]
                    for state, weight in zip(states, shares):
                        total = total + state[i] * weight[i]
                    out[h, i, r] = total.astype(BF16)


def grads_kernel(scale, peers, heads, alias, cols, *refs):
    tq, tk, tv, d_ref, e_ref, f_ref, g_ref = refs[:7]
    p_refs = refs[7 : 7 + peers]
    outs, (out_ref, x_ref, sems) = refs[-6:-3], refs[-3:]
    rows, width = out_ref.shape[2:]
    copies = Copies(sems)
    saves = []
    for p in range(peers):
        for h in range(heads):
            c = lanes((cols[p] * heads + h) * HEAD)
            own = slice(h * HEAD, (h + 1) * HEAD)
            vk, gq = p_refs[p][h, 0], p_refs[p][h, 1]
            kx, vx, gx = [
                jnp.concatenate([field, e_ref[p, i, :, own]], 0)
                for i, field in enumerate((f_ref[p, 0, :, own], f_ref[p, 1, :, own], g_ref[:, c]))
            ]
            d = x_ref.at[h]
            d[0] = d_ref[p, h, 0].astype(F32) + dot(gx, vk, 1, 0)
            d[1] = d_ref[p, h, 1].astype(F32) + dot(vx, gq, 1, 0)
            d[2] = d_ref[p, h, 2].astype(F32) + dot(kx, gq, 1, 1)
            for i, tap_ref in enumerate((tq, tk, tv)):
                taps = tap_ref[:, c].astype(F32) * scale
                total = taps[0:1] * d[i, 0:rows]
                for j in range(1, KERNEL):
                    total = total + taps[j : j + 1] * d[i, j : j + rows]
                out_ref[p, i, :, own] = total.astype(BF16)
        c = lanes(cols[p] * width, width)
        saves += [copies.start(out_ref.at[p, i], outs[i].at[:, c]) for i in range(3)]
    wait(saves)


def grads_call(peers, heads, scale, cols, g, intra, states, taps, outs):
    rows, total_width = g.shape
    ext = rows + EDGE
    near = [*taps, *intra, g, *states]
    remote = []
    aliases = []
    if outs is not None:
        aliases = [(len(near) + i, i) for i in range(3)]
        remote = outs
    results, _ = marked_call(
        functools.partial(grads_kernel, scale, peers, heads, outs is not None),
        "grads",
        cols,
        near,
        remote,
        [pltpu.HBM((rows, total_width), BF16)] * 3,
        [
            pltpu.VMEM((peers, 3, rows, heads * HEAD), BF16),
            pltpu.VMEM((heads, 3, ext, HEAD), F32),
            pltpu.SemaphoreType.DMA((peers * 3,)),
        ],
        6 * heads * peers * ext * HEAD * HEAD,
        aliases=aliases,
    )
    return results


def local(query_raw, key_raw, value_raw, grad_out, query_kernel, key_kernel, value_kernel):
    rows, total_width = query_raw.shape
    planes = lax.axis_size("z")
    members = CORES * lax.axis_size("y") * lax.axis_size("x")
    devices = planes * members
    scale = float(HEAD * rows * devices) ** (-0.5)
    heads = total_width // HEAD // members
    everyone = ("z", "core", "y", "x")
    plane = ("core", "y", "x")
    raws = (query_raw, key_raw, value_raw, grad_out)
    taps = (query_kernel, key_kernel, value_kernel)
    x, z = lax.axis_index("x"), lax.axis_index("z")
    me = (lax.axis_index("core") * lax.axis_size("y") + lax.axis_index("y")) * lax.axis_size("x") + x
    width_y = lax.axis_size("y")
    steps = {d: (d % 2 > 0) + (d // 2 % width_y > 0) for d in range(members)}
    direct, diagonal, near = [[d for d in steps if steps[d] == n] for n in (1, 2, 0)]
    direct.sort(key=lambda d: (d // (2 * width_y), d))
    near.reverse()
    order = [*direct, *diagonal, *near]

    def numbers(ds):
        return (me ^ jnp.array(ds, jnp.int32)).astype(jnp.int32)

    idx = jnp.concatenate([z[None].astype(jnp.int32), numbers(order)])

    def swap(field, axes, count, d):
        return lax.ppermute(field, axes, [(i, i ^ d) for i in range(count)]) if d else field

    tail, lead = pack(raws)
    prev = lax.ppermute(tail, everyone, [(i, i + 1) for i in range(devices - 1)])
    after = lax.ppermute(lead, everyone, [(i + 1, i) for i in range(devices - 1)])

    states, mark = {}, []

    def make_states(ds, mark):
        out, mark = states_call(len(ds), heads, numbers(ds), raws, prev, taps, mark)
        states.update({d: swap(s, plane, members, d) for s, d in zip(out, ds)})
        return [mark]

    intra = {}

    def make_intra(ds, arrived, mark):
        args = (numbers(ds), raws, prev, after, taps, arrived, mark)
        intra[ds[0]], mark = intra_call(len(ds), heads, *args)
        return [mark]

    others = [*near, *diagonal]
    mark = make_states(direct, mark)
    mark = make_states(diagonal, mark)
    mark = make_states(near, mark)
    mark = make_intra(direct, states[direct[0]], mark)
    states = [states[d] for d in order]
    bits = (planes - 1).bit_length()
    levels, mark = marked_call(
        functools.partial(sums_kernel, members),
        "sums",
        idx,
        states,
        [],
        [shape((heads, HEAD, HEAD))] * bits,
        behind=mark,
    )
    across = [swap(levels[d.bit_length() - 1], "z", planes, d) for d in range(1, planes)]
    mark = make_intra(others, states[0], [mark])
    backs = {}
    for ds in (direct, [*diagonal, *near]):
        sent, mark = marked_call(
            functools.partial(members_kernel, members, planes, [order.index(d) for d in ds]),
            "members",
            idx,
            [*states, *across],
            [],
            [shape((heads, 2, HEAD, HEAD))] * len(ds),
            behind=mark,
        )
        mark = [mark]
        backs |= {d: swap(s, plane, members, d) for s, d in zip(sent, ds)}
    outs = None
    for ds in (direct, others):
        got = [backs[d] for d in ds]
        outs = grads_call(len(ds), heads, scale, numbers(ds), grad_out, intra[ds[0]], got, taps, outs)
    return tuple(outs)


def solution(mesh):
    chain, grp = mesh.shape["chain"], mesh.shape["grp"]
    sizes = (chain // CORES, CORES, grp // 2, 2)
    split = Mesh(mesh.devices.reshape(sizes), ("z", "core", "y", "x"))
    tokens = P(("z", "core", "y", "x"), None)
    return jax.shard_map(
        local,
        mesh=split,
        in_specs=(tokens,) * 4 + (P(),) * 3,
        out_specs=(tokens,) * 3,
        check_vma=False,
    )
```

time: 274 us -> 96.8 us (0.35); the launches traced: 269 us -> 96.4 us
  waiting for transfers between devices: 107 us -> 27 us
  local copies, waits for them, and re-layouts: 51.9 us -> 1.04 us
  Pallas kernels: 0 us -> 40.8 us
  other arithmetic: 35.9 us -> 0.09 us
  matrix products: 28.3 us -> 0 us
  between operations: 14.4 us -> 1.18 us
  starting transfers between devices: 31.7 us -> 26.3 us
    all_to_all x7 -> x0, waiting for transfers between devices: 71.9 us -> none  [the longest x1 13.6 us: local(): lax.all_to_all(first, 'grp', split_axis=0, concat_axis=1, tiled=True)]
    pallas_call x0 -> x11, Pallas kernels: none -> 40.8 us  [the longest x10 39.4 us: marked_call(): pl.pallas_call(body, in_specs=[SMEM] * (1 + hidden) + [VMEM] * len(near)...]
    all_gather x2 -> x0, waiting for transfers between devices: 34.6 us -> none  [entering(): gathered = lax.all_gather(value.astype(jnp.bfloat16), axis)]
    dot_general x17 -> x0, matrix products: 28.3 us -> none  [the longest x1 6.01 us: block_grads(): jnp.einsum('hrc,rhe->che', masked_sim, cot_block, preferred_element_type=...]
    all_to_all x7 -> x0, starting transfers between devices: 27.1 us -> none  [the longest x1 5.16 us: local(): lax.all_to_all(grad_out, 'grp', split_axis=1, concat_axis=0, tiled=True)]
    ppermute x2 -> x19, waiting for transfers between devices: 0.01 us -> 27 us  [the longest x17 24.4 us: swap(): lax.ppermute(field, axes, [(i, i ^ d) for i in range(count)])]
    convert_element_type x5 -> x0, other arithmetic: 23.7 us -> none  [the longest x1 8.88 us: local_grads(): features = mixed.astype(jnp.bfloat16)]
    ppermute x2 -> x19, starting transfers between devices: 4.32 us -> 26.3 us  [the longest x17 20.1 us: swap(): lax.ppermute(field, axes, [(i, i ^ d) for i in range(count)])]
  transfers between devices with their start and end apart: 11 -> 19, of which waited for: 9 -> 7; matrix products, arithmetic and copies ran while one was open for 20% -> 0% of each run, Pallas kernels for 0% -> 29%
where the time goes in v3:
time: 96.8 us; the launch traced here: 96.4 us
  Pallas kernels  40.8 us (42%)
  waiting for transfers between devices  27 us (28%)
  starting transfers between devices  26.3 us (27%)
  between operations  1.18 us (1%)
  local copies, waits for them, and re-layouts  1.04 us (1%)
    pallas_call x10, Pallas kernels, marked_call(): pl.pallas_call(body, in_specs=[SMEM] * (1 + hidden) + [VMEM] * len(near)...  39.4 us
    ppermute x17, waiting for transfers between devices, swap(): lax.ppermute(field, axes, [(i, i ^ d) for i in range(count)])  24.4 us
    ppermute x17, starting transfers between devices, swap(): lax.ppermute(field, axes, [(i, i ^ d) for i in range(count)])  20.1 us
    ppermute x1, starting transfers between devices, local(): lax.ppermute(tail, everyone, [(i, i + 1) for i in range(devices - 1)])  4.85 us
    ppermute x1, waiting for transfers between devices, local(): lax.ppermute(tail, everyone, [(i, i + 1) for i in range(devices - 1)])  2.67 us
  transfers between devices with their start and end apart: 19, of which 7 were waited for; matrix products, arithmetic and copies ran while one was open for 0% of the time, Pallas kernels for 29%

profile of v3, /device:TPU:0, one launch (start us, length us, event | category | flops | bytes accessed | tf_op | source)
XLA Modules:
  0.0 96.4 jit_solution(10264952673643933868)
XLA Ops:
  0.6 0.0 copy-start.17
  0.7 1.4 %pack.1 = (bf16[16,4096]{1,0:T(8,128)(2,1)S(1)}, bf16[16,4096]{1,0:T(8,128)(2,1)S(1)}) custom-call(bf16[128,4096]{1,0:T(8,128)(2,1)} %refs_6_.11, bf16[128,4096]{1,0:T(8,128)(2,1)} %refs_7_.9, bf16[128,4096]{1,0:T(8,128)(2,1)} %refs_8_.7, bf16[128,4096]{1,0:T(8,128)(2,1)} %refs_6_.13), custom_call_target="tpu_custom_call" | custom-call | bytes 1179648 | tf_op jit(solution)/shard_map/pack/pallas_call | solution.py:70
  2.1 4.8 %collective-permute-start = (bf16[16,4096]{1,0:T(8,128)(2,1)S(1)}, bf16[16,4096]{1,0:T(8,128)(2,1)S(1)}, u32[]{:S(2)}, u32[]{:S(2)}) collective-permute-start(bf16[16,4096]{1,0:T(8,128)(2,1)S(1)} %get-tuple-element.42), channel_id=1, source_target_pairs={{0,1},{1,2},{2,3},{3,4},{4,5},{5,6},{6,7},{7,8},{8,9},{9,10},{10,1... | collective-permute-start | bytes 393224 | tf_op jit(solution)/shard_map/ppermute | solution.py:420
  6.9 0.0 copy-start.13
  7.0 0.0 copy-start.14
  7.0 2.7 %collective-permute-done.refs_0_.refs_1_ = bf16[16,4096]{1,0:T(8,128)(2,1)S(1)} collective-permute-done((bf16[16,4096]{1,0:T(8,128)(2,1)S(1)}, bf16[16,4096]{1,0:T(8,128)(2,1)S(1)}, u32[]{:S(2)}, u32[]{:S(2)}) %collective-permute-start) | collective-permute-done | bytes 131104 | tf_op jit(solution)/shard_map/ppermute | solution.py:420
  9.7 3.6 %states.3 = (bf16[4,2,128,128]{3,2,1,0:T(8,128)(2,1)S(1)}, bf16[4,2,128,128]{3,2,1,0:T(8,128)(2,1)S(1)}, bf16[4,2,128,128]{3,2,1,0:T(8,128)(2,1)S(1)}, bf16[4,2,128,128]{3,2,1,0:T(8,128)(2,1)S(1)}, s32[1]{0:T(128)}) custom-call(s32[4]{0:T(128)S(1)} %broadcast_xor_fusion.3.cols, bf16[16,4096]{1,0:T(8,128)(2,1)S(1)} %collective-permute-done.refs_0_.refs_1_, ...), custom_call_target="tpu_custom_call" | custom-call | flops 134217728 | bytes 5472256 | tf_op jit(solution)/shard_map/states/pallas_call | solution.py:120
  13.3 2.6 %collective-permute-start.2 = (bf16[4,2,128,128]{3,2,1,0:T(8,128)(2,1)S(1)}, bf16[4,2,128,128]{3,2,1,0:T(8,128)(2,1)S(1)}, u32[]{:S(2)}, u32[]{:S(2)}) collective-permute-start(bf16[4,2,128,128]{3,2,1,0:T(8,128)(2,1)S(1)} %get-tuple-element.47), channel_id=1, source_target_pairs={{0,1},{1,0},{2,3},{3,2},{4,5},{5,4},{6,7},{7,6},{8,9},{9,8},{10,11... | collective-permute-start | bytes 786440 | tf_op jit(solution)/shard_map/ppermute | solution.py:417
  15.9 1.5 %collective-permute-start.3 = (bf16[4,2,128,128]{3,2,1,0:T(8,128)(2,1)S(1)}, bf16[4,2,128,128]{3,2,1,0:T(8,128)(2,1)S(1)}, u32[]{:S(2)}, u32[]{:S(2)}) collective-permute-start(bf16[4,2,128,128]{3,2,1,0:T(8,128)(2,1)S(1)} %get-tuple-element.49), channel_id=1, source_target_pairs={{0,2},{1,3},{2,0},{3,1},{4,6},{5,7},{6,4},{7,5},{8,10},{9,11},{10,... | collective-permute-start | bytes 786440 | tf_op jit(solution)/shard_map/ppermute | solution.py:417
  17.4 1.3 %collective-permute-start.1 = (bf16[16,4096]{1,0:T(8,128)(2,1)S(1)}, bf16[16,4096]{1,0:T(8,128)(2,1)S(1)}, u32[]{:S(2)}, u32[]{:S(2)}) collective-permute-start(bf16[16,4096]{1,0:T(8,128)(2,1)S(1)} %get-tuple-element.46), channel_id=1, source_target_pairs={{1,0},{2,1},{3,2},{4,3},{5,4},{6,5},{7,6},{8,7},{9,8},{10,9},{11,1... | collective-permute-start | bytes 393224 | tf_op jit(solution)/shard_map/ppermute | solution.py:421
  18.7 0.4 collective-permute-start.4
  19.1 2.5 %collective-permute-start.5 = (bf16[4,2,128,128]{3,2,1,0:T(8,128)(2,1)S(1)}, bf16[4,2,128,128]{3,2,1,0:T(8,128)(2,1)S(1)}, u32[]{:S(2)}, u32[]{:S(2)}) collective-permute-start(bf16[4,2,128,128]{3,2,1,0:T(8,128)(2,1)S(1)} %get-tuple-element.51), channel_id=1, source_target_pairs={{0,6},{1,7},{2,4},{3,5},{4,2},{5,3},{6,0},{7,1},{8,14},{9,15},{10,... | collective-permute-start | bytes 786440 | tf_op jit(solution)/shard_map/ppermute | solution.py:417
  21.6 3.5 %states.4 = (bf16[4,2,128,128]{3,2,1,0:T(8,128)(2,1)}, bf16[4,2,128,128]{3,2,1,0:T(8,128)(2,1)S(1)}, s32[1]{0:T(128)}) custom-call(s32[2]{0:T(128)S(1)} %get-tuple-element.81.cols, s32[1]{0:T(128)} %get-tuple-element.43.refs_0_, bf16[16,4096]{1,0:T(8,128)(2,1)S(1)} %collective-permute-done.refs_0_.refs_1_, bf16[4,4096]{1,0:T(4,128)(2,1)S(1)} %copy-done.6, ...), custom_call_target="tpu_custom_call" | custom-call | flops 67108864 | bytes 4947968 | tf_op jit(solution)/shard_map/states/pallas_call | solution.py:120
  25.2 0.0 copy-start.16
  25.2 3.3 %states.5 = (bf16[4,2,128,128]{3,2,1,0:T(8,128)(2,1)S(1)}, bf16[4,2,128,128]{3,2,1,0:T(8,128)(2,1)S(1)}, s32[1]{0:T(128)}) custom-call(s32[2]{0:T(128)S(1)} %get-tuple-element.82.cols, s32[1]{0:T(128)} %get-tuple-element.44.refs_0_, bf16[16,4096]{1,0:T(8,128)(2,1)S(1)} %collective-permute-done.refs_0_.refs_1_, bf16[4,4096]{1,0:T(4,128)(2,1)S(1)} %copy-done.6, ...), custom_call_target="tpu_custom_call" | custom-call | flops 67108864 | bytes 4947968 | tf_op jit(solution)/shard_map/states/pallas_call | solution.py:120
  28.6 0.4 collective-permute-start.6
  29.0 2.7 %collective-permute-start.7 = (bf16[4,2,128,128]{3,2,1,0:T(8,128)(2,1)S(1)}, bf16[4,2,128,128]{3,2,1,0:T(8,128)(2,1)S(1)}, u32[]{:S(2)}, u32[]{:S(2)}) collective-permute-start(bf16[4,2,128,128]{3,2,1,0:T(8,128)(2,1)S(1)} %get-tuple-element.53), channel_id=1, source_target_pairs={{0,7},{1,6},{2,5},{3,4},{4,3},{5,2},{6,1},{7,0},{8,15},{9,14},{10,... | collective-permute-start | bytes 786440 | tf_op jit(solution)/shard_map/ppermute | solution.py:417
  31.7 0.0 collective-permute-done.3.refs_2_
  31.7 0.0 collective-permute-start.8
  31.7 0.1 pad_add_fusion.cols
  31.8 7.3 %intra.2 = (bf16[4,4,3,144,128]{4,3,2,1,0:T(8,128)(2,1)}, bf16[4,3,16,512]{3,2,1,0:T(8,128)(2,1)}, bf16[4,2,128,512]{3,2,1,0:T(8,128)(2,1)}, s32[1]{0:T(128)}) custom-call(s32[4]{0:T(128)S(1)} %broadcast_xor_fusion.3.cols, s32[1]{0:T(128)} %get-tuple-element.45.refs_0_, bf16[16,4096]{1,0:T(8,128)(2,1)S(1)} %collective-permute-done.refs_0_.refs_1_, ...), custom_call_target="tpu_custom_call" | custom-call | flops 402653184 | bytes 7831552 | tf_op jit(solution)/shard_map/intra/pallas_call | solution.py:120
  39.1 0.0 copy-start.15
  39.1 0.0 collective-permute-done.4.refs_3_
  39.1 5.1 %collective-permute-done.7.refs_6_ = bf16[4,2,128,128]{3,2,1,0:T(8,128)(2,1)S(1)} collective-permute-done((bf16[4,2,128,128]{3,2,1,0:T(8,128)(2,1)S(1)}, bf16[4,2,128,128]{3,2,1,0:T(8,128)(2,1)S(1)}, u32[]{:S(2)}, u32[]{:S(2)}) %collective-permute-start.7) | collective-permute-done | bytes 262176 | tf_op jit(solution)/shard_map/ppermute | solution.py:417
  44.3 0.9 copy-done.2
  45.2 1.6 %sums.1 = (bf16[4,128,128]{2,1,0:T(8,128)(2,1)S(1)}, bf16[4,128,128]{2,1,0:T(8,128)(2,1)S(1)}, s32[1]{0:T(128)}) custom-call(s32[9]{0:T(128)S(1)} %pad_add_fusion.cols, s32[1]{0:T(128)} %get-tuple-element.48.refs_0_, bf16[4,2,128,128]{3,2,1,0:T(8,128)(2,1)S(1)} %copy-done.2, bf16[4,2,128,128]{3,2,1,0:T(8,128)(2,1)S(1)} %collective-permute-done.3.refs_2_, ...), custom_call_target="tpu_custom_call" | custom-call | bytes 2359296 | tf_op jit(solution)/shard_map/sums/pallas_call | solution.py:120
  46.9 3.7 %collective-permute-start.11 = (bf16[4,128,128]{2,1,0:T(8,128)(2,1)S(1)}, bf16[4,128,128]{2,1,0:T(8,128)(2,1)S(1)}, u32[]{:S(2)}, u32[]{:S(2)}) collective-permute-start(bf16[4,128,128]{2,1,0:T(8,128)(2,1)S(1)} %get-tuple-element.62), channel_id=1, source_target_pairs={{0,24},{8,16},{16,8},{24,0},{1,25},{9,17},{17,9},{25,1},{2,26},{10... | collective-permute-start | bytes 393224 | tf_op jit(solution)/shard_map/ppermute | solution.py:417
  50.5 0.0 collective-permute-start.10
  50.5 0.8 collective-permute-start.9
  51.3 7.3 %intra.3 = (bf16[4,4,3,144,128]{4,3,2,1,0:T(8,128)(2,1)}, bf16[4,3,16,512]{3,2,1,0:T(8,128)(2,1)}, bf16[4,2,128,512]{3,2,1,0:T(8,128)(2,1)}, s32[1]{0:T(128)}) custom-call(s32[4]{0:T(128)S(1)} %broadcast_xor_fusion.4.cols, s32[1]{0:T(128)} %get-tuple-element.56.refs_0_, bf16[16,4096]{1,0:T(8,128)(2,1)S(1)} %collective-permute-done.refs_0_.refs_1_, ...), custom_call_target="tpu_custom_call" | custom-call | flops 402653184 | bytes 7831552 | tf_op jit(solution)/shard_map/intra/pallas_call | solution.py:120
  58.7 0.6 collective-permute-done.9.refs_9_
  59.3 0.0 collective-permute-done.11.refs_11_
  59.3 2.6 %collective-permute-done.10.refs_10_ = bf16[4,128,128]{2,1,0:T(8,128)(2,1)S(1)} collective-permute-done((bf16[4,128,128]{2,1,0:T(8,128)(2,1)S(1)}, bf16[4,128,128]{2,1,0:T(8,128)(2,1)S(1)}, u32[]{:S(2)}, u32[]{:S(2)}) %collective-permute-start.10) | collective-permute-done | bytes 131104 | tf_op jit(solution)/shard_map/ppermute | solution.py:417
  61.9 2.7 %members.2 = (bf16[4,2,128,128]{3,2,1,0:T(8,128)(2,1)S(1)}, bf16[4,2,128,128]{3,2,1,0:T(8,128)(2,1)S(1)}, bf16[4,2,128,128]{3,2,1,0:T(8,128)(2,1)S(1)}, bf16[4,2,128,128]{3,2,1,0:T(8,128)(2,1)S(1)}, s32[1]{0:T(128)}) custom-call(s32[9]{0:T(128)S(1)} %pad_add_fusion.cols, s32[1]{0:T(128)} %get-tuple-element.60.refs_0_, ...), custom_call_target="tpu_custom_call" | custom-call | bytes 3538944 | tf_op jit(solution)/shard_map/members/pallas_call | solution.py:120
  64.5 0.0 copy-start
  64.5 0.0 copy-start.10
  64.6 0.1 collective-permute-start.15
  64.6 2.2 %collective-permute-start.16 = (bf16[4,2,128,128]{3,2,1,0:T(8,128)(2,1)S(1)}, bf16[4,2,128,128]{3,2,1,0:T(8,128)(2,1)S(1)}, u32[]{:S(2)}, u32[]{:S(2)}) collective-permute-start(bf16[4,2,128,128]{3,2,1,0:T(8,128)(2,1)S(1)} %get-tuple-element.72), channel_id=1, source_target_pairs={{0,2},{1,3},{2,0},{3,1},{4,6},{5,7},{6,4},{7,5},{8,10},{9,11},{10,... | collective-permute-start | bytes 786440 | tf_op jit(solution)/shard_map/ppermute | solution.py:417
  66.8 0.0 collective-permute-start.17
  66.8 1.6 %collective-permute-start.18 = (bf16[4,2,128,128]{3,2,1,0:T(8,128)(2,1)S(1)}, bf16[4,2,128,128]{3,2,1,0:T(8,128)(2,1)S(1)}, u32[]{:S(2)}, u32[]{:S(2)}) collective-permute-start(bf16[4,2,128,128]{3,2,1,0:T(8,128)(2,1)S(1)} %get-tuple-element.74), channel_id=1, source_target_pairs={{0,6},{1,7},{2,4},{3,5},{4,2},{5,3},{6,0},{7,1},{8,14},{9,15},{10,... | collective-permute-start | bytes 786440 | tf_op jit(solution)/shard_map/ppermute | solution.py:417
  68.4 2.6 %members.3 = (bf16[4,2,128,128]{3,2,1,0:T(8,128)(2,1)S(1)}, bf16[4,2,128,128]{3,2,1,0:T(8,128)(2,1)S(1)}, bf16[4,2,128,128]{3,2,1,0:T(8,128)(2,1)S(1)}, bf16[4,2,128,128]{3,2,1,0:T(8,128)(2,1)S(1)}, s32[1]{0:T(128)}) custom-call(s32[9]{0:T(128)S(1)} %pad_add_fusion.cols, s32[1]{0:T(128)} %get-tuple-element.63.refs_0_, ...), custom_call_target="tpu_custom_call" | custom-call | bytes 3538944 | tf_op jit(solution)/shard_map/members/pallas_call | solution.py:120
  71.0 0.1 collective-permute-start.12
  71.1 2.8 %collective-permute-done.15.refs_7_ = bf16[4,2,128,128]{3,2,1,0:T(8,128)(2,1)S(1)} collective-permute-done((bf16[4,2,128,128]{3,2,1,0:T(8,128)(2,1)S(1)}, bf16[4,2,128,128]{3,2,1,0:T(8,128)(2,1)S(1)}, u32[]{:S(2)}, u32[]{:S(2)}) %collective-permute-start.15) | collective-permute-done | bytes 262176 | tf_op jit(solution)/shard_map/ppermute | solution.py:417
  73.9 1.6 %collective-permute-start.13 = (bf16[4,2,128,128]{3,2,1,0:T(8,128)(2,1)S(1)}, bf16[4,2,128,128]{3,2,1,0:T(8,128)(2,1)S(1)}, u32[]{:S(2)}, u32[]{:S(2)}) collective-permute-start(bf16[4,2,128,128]{3,2,1,0:T(8,128)(2,1)S(1)} %get-tuple-element.66), channel_id=1, source_target_pairs={{0,3},{1,2},{2,1},{3,0},{4,7},{5,6},{6,5},{7,4},{8,11},{9,10},{10,... | collective-permute-start | bytes 786440 | tf_op jit(solution)/shard_map/ppermute | solution.py:417
  75.5 1.5 %collective-permute-done.17.refs_9_ = bf16[4,2,128,128]{3,2,1,0:T(8,128)(2,1)S(1)} collective-permute-done((bf16[4,2,128,128]{3,2,1,0:T(8,128)(2,1)S(1)}, bf16[4,2,128,128]{3,2,1,0:T(8,128)(2,1)S(1)}, u32[]{:S(2)}, u32[]{:S(2)}) %collective-permute-start.17) | collective-permute-done | bytes 262176 | tf_op jit(solution)/shard_map/ppermute | solution.py:417
  77.0 11.7 %collective-permute-done.18.refs_10_ = bf16[4,2,128,128]{3,2,1,0:T(8,128)(2,1)S(1)} collective-permute-done((bf16[4,2,128,128]{3,2,1,0:T(8,128)(2,1)S(1)}, bf16[4,2,128,128]{3,2,1,0:T(8,128)(2,1)S(1)}, u32[]{:S(2)}, u32[]{:S(2)}) %collective-permute-start.18) | collective-permute-done | bytes 262176 | tf_op jit(solution)/shard_map/ppermute | solution.py:417
  88.8 3.8 %grads.2 = (bf16[128,4096]{1,0:T(8,128)(2,1)}, bf16[128,4096]{1,0:T(8,128)(2,1)}, bf16[128,4096]{1,0:T(8,128)(2,1)}, s32[1]{0:T(128)}) custom-call(s32[4]{0:T(128)S(1)} %broadcast_xor_fusion.3.cols, bf16[4,4096]{1,0:T(4,128)(2,1)S(1)} %copy-done.6, bf16[4,4096]{1,0:T(4,128)(2,1)S(1)} %copy-done.7, bf16[4,4096]{1,0:T(4,128)(2,1)S(1)} %copy-done.8, ...), custom_call_target="tpu_custom_call" | custom-call | flops 226492416 | bytes 8355840 | tf_op jit(solution)/shard_map/grads/pallas_call | solution.py:120
  92.6 3.6 %grads.3 = (bf16[128,4096]{1,0:T(8,128)(2,1)}, bf16[128,4096]{1,0:T(8,128)(2,1)}, bf16[128,4096]{1,0:T(8,128)(2,1)}, s32[1]{0:T(128)}) custom-call(s32[4]{0:T(128)S(1)} %broadcast_xor_fusion.4.cols, bf16[4,4096]{1,0:T(4,128)(2,1)S(1)} %copy-done.6, bf16[4,4096]{1,0:T(4,128)(2,1)S(1)} %copy-done.7, ...), custom_call_target="tpu_custom_call", output_to_operand_aliasing={{0}: (12, {}), {1}: (13, {}), {2}: (14, {})} | custom-call | flops 226492416 | bytes 11501568 | tf_op jit(solution)/shard_map/grads/pallas_call | solution.py:120
  (42 shorter events, 0.1 us)
Async XLA Ops:
  0.6 6.3 %copy-start.17 = (s32[4]{0:T(128)S(1)}, s32[4]{0:T(128)}, u32[]{:S(2)}) copy-start(s32[4]{0:T(128)} %constant.27.clone) | copy-start | bytes 52
  0.6 9.0 %copy-start.8 = (bf16[4,4096]{1,0:T(4,128)(2,1)S(1)}, bf16[4,4096]{1,0:T(4,128)(2,1)}, u32[]{:S(2)}) copy-start(bf16[4,4096]{1,0:T(4,128)(2,1)} %refs_2_.9) | copy-start | bytes 98308
  0.7 9.0 %copy-start.7 = (bf16[4,4096]{1,0:T(4,128)(2,1)S(1)}, bf16[4,4096]{1,0:T(4,128)(2,1)}, u32[]{:S(2)}) copy-start(bf16[4,4096]{1,0:T(4,128)(2,1)} %refs_1_.5) | copy-start | bytes 98308
  0.7 9.0 %copy-start.6 = (bf16[4,4096]{1,0:T(4,128)(2,1)S(1)}, bf16[4,4096]{1,0:T(4,128)(2,1)}, u32[]{:S(2)}) copy-start(bf16[4,4096]{1,0:T(4,128)(2,1)} %refs_0_.3) | copy-start | bytes 98308
  2.1 7.6 %collective-permute-start = (bf16[16,4096]{1,0:T(8,128)(2,1)S(1)}, bf16[16,4096]{1,0:T(8,128)(2,1)S(1)}, u32[]{:S(2)}, u32[]{:S(2)}) collective-permute-start(bf16[16,4096]{1,0:T(8,128)(2,1)S(1)} %get-tuple-element.42), channel_id=1, source_target_pairs={{0,1},{1,2},{2,3},{3,4},{4,5},{5,6},{6,7},{7,8},{8,9},{9,10},{10,1... | collective-permute-start | bytes 393224 | tf_op jit(solution)/shard_map/ppermute | solution.py:420
  6.9 11.7 %copy-start.13 = (s32[2]{0:T(128)S(1)}, s32[2]{0:T(128)}, u32[]{:S(2)}) copy-start(s32[2]{0:T(128)} %constant.29.clone) | copy-start | bytes 28
  7.0 11.7 %copy-start.14 = (s32[2]{0:T(128)S(1)}, s32[2]{0:T(128)}, u32[]{:S(2)}) copy-start(s32[2]{0:T(128)} %constant.28.clone) | copy-start | bytes 28
  13.3 15.7 %collective-permute-start.2 = (bf16[4,2,128,128]{3,2,1,0:T(8,128)(2,1)S(1)}, bf16[4,2,128,128]{3,2,1,0:T(8,128)(2,1)S(1)}, u32[]{:S(2)}, u32[]{:S(2)}) collective-permute-start(bf16[4,2,128,128]{3,2,1,0:T(8,128)(2,1)S(1)} %get-tuple-element.47), channel_id=1, source_target_pairs={{0,1},{1,0},{2,3},{3,2},{4,5},{5,4},{6,7},{7,6},{8,9},{9,8},{10,11... | collective-permute-start | bytes 786440 | tf_op jit(solution)/shard_map/ppermute | solution.py:417
  15.9 15.9 %collective-permute-start.3 = (bf16[4,2,128,128]{3,2,1,0:T(8,128)(2,1)S(1)}, bf16[4,2,128,128]{3,2,1,0:T(8,128)(2,1)S(1)}, u32[]{:S(2)}, u32[]{:S(2)}) collective-permute-start(bf16[4,2,128,128]{3,2,1,0:T(8,128)(2,1)S(1)} %get-tuple-element.49), channel_id=1, source_target_pairs={{0,2},{1,3},{2,0},{3,1},{4,6},{5,7},{6,4},{7,5},{8,10},{9,11},{10,... | collective-permute-start | bytes 786440 | tf_op jit(solution)/shard_map/ppermute | solution.py:417
  17.4 11.2 %collective-permute-start.1 = (bf16[16,4096]{1,0:T(8,128)(2,1)S(1)}, bf16[16,4096]{1,0:T(8,128)(2,1)S(1)}, u32[]{:S(2)}, u32[]{:S(2)}) collective-permute-start(bf16[16,4096]{1,0:T(8,128)(2,1)S(1)} %get-tuple-element.46), channel_id=1, source_target_pairs={{1,0},{2,1},{3,2},{4,3},{5,4},{6,5},{7,6},{8,7},{9,8},{10,9},{11,1... | collective-permute-start | bytes 393224 | tf_op jit(solution)/shard_map/ppermute | solution.py:421
  18.7 20.4 %collective-permute-start.4 = (bf16[4,2,128,128]{3,2,1,0:T(8,128)(2,1)S(1)}, bf16[4,2,128,128]{3,2,1,0:T(8,128)(2,1)S(1)}, u32[]{:S(2)}, u32[]{:S(2)}) collective-permute-start(bf16[4,2,128,128]{3,2,1,0:T(8,128)(2,1)S(1)} %get-tuple-element.50), channel_id=1, source_target_pairs={{0,5},{1,4},{2,7},{3,6},{4,1},{5,0},{6,3},{7,2},{8,13},{9,12},{10,... | collective-permute-start | bytes 786440 | tf_op jit(solution)/shard_map/ppermute | solution.py:417
  19.1 20.0 %collective-permute-start.5 = (bf16[4,2,128,128]{3,2,1,0:T(8,128)(2,1)S(1)}, bf16[4,2,128,128]{3,2,1,0:T(8,128)(2,1)S(1)}, u32[]{:S(2)}, u32[]{:S(2)}) collective-permute-start(bf16[4,2,128,128]{3,2,1,0:T(8,128)(2,1)S(1)} %get-tuple-element.51), channel_id=1, source_target_pairs={{0,6},{1,7},{2,4},{3,5},{4,2},{5,3},{6,0},{7,1},{8,14},{9,15},{10,... | collective-permute-start | bytes 786440 | tf_op jit(solution)/shard_map/ppermute | solution.py:417
  25.2 6.5 %copy-start.16 = (s32[8]{0:T(128)S(1)}, s32[8]{0:T(128)}, u32[]{:S(2)}) copy-start(s32[8]{0:T(128)} %constant.26.clone) | copy-start | bytes 100
  28.6 10.6 %collective-permute-start.6 = (bf16[4,2,128,128]{3,2,1,0:T(8,128)(2,1)}, bf16[4,2,128,128]{3,2,1,0:T(8,128)(2,1)S(1)}, u32[]{:S(2)}, u32[]{:S(2)}) collective-permute-start(bf16[4,2,128,128]{3,2,1,0:T(8,128)(2,1)} %get-tuple-element.52), channel_id=1, source_target_pairs={{0,3},{1,2},{2,1},{3,0},{4,7},{5,6},{6,5},{7,4},{8,11},{9,10},{10,... | collective-permute-start | bytes 786440 | tf_op jit(solution)/shard_map/ppermute | solution.py:417
  29.0 2.8 %copy-start.1 = (bf16[4,2,128,128]{3,2,1,0:T(8,128)(2,1)}, bf16[4,2,128,128]{3,2,1,0:T(8,128)(2,1)S(1)}, u32[]{:S(2)}) copy-start(bf16[4,2,128,128]{3,2,1,0:T(8,128)(2,1)S(1)} %collective-permute-done.2.refs_10_.refs_1_) | copy-start | bytes 786436
  29.0 15.3 %collective-permute-start.7 = (bf16[4,2,128,128]{3,2,1,0:T(8,128)(2,1)S(1)}, bf16[4,2,128,128]{3,2,1,0:T(8,128)(2,1)S(1)}, u32[]{:S(2)}, u32[]{:S(2)}) collective-permute-start(bf16[4,2,128,128]{3,2,1,0:T(8,128)(2,1)S(1)} %get-tuple-element.53), channel_id=1, source_target_pairs={{0,7},{1,6},{2,5},{3,4},{4,3},{5,2},{6,1},{7,0},{8,15},{9,14},{10,... | collective-permute-start | bytes 786440 | tf_op jit(solution)/shard_map/ppermute | solution.py:417
  31.7 12.6 %collective-permute-start.8 = (bf16[4,2,128,128]{3,2,1,0:T(8,128)(2,1)S(1)}, bf16[4,2,128,128]{3,2,1,0:T(8,128)(2,1)S(1)}, u32[]{:S(2)}, u32[]{:S(2)}) collective-permute-start(bf16[4,2,128,128]{3,2,1,0:T(8,128)(2,1)S(1)} %get-tuple-element.54), channel_id=1, source_target_pairs={{0,4},{1,5},{2,6},{3,7},{4,0},{5,1},{6,2},{7,3},{8,12},{9,13},{10,... | collective-permute-start | bytes 786440 | tf_op jit(solution)/shard_map/ppermute | solution.py:417
  39.1 12.2 %copy-start.15 = (s32[4]{0:T(128)S(1)}, s32[4]{0:T(128)}, u32[]{:S(2)}) copy-start(s32[4]{0:T(128)} %constant.30.clone) | copy-start | bytes 52
  44.3 1.0 copy-start.2
  46.9 12.4 %collective-permute-start.11 = (bf16[4,128,128]{2,1,0:T(8,128)(2,1)S(1)}, bf16[4,128,128]{2,1,0:T(8,128)(2,1)S(1)}, u32[]{:S(2)}, u32[]{:S(2)}) collective-permute-start(bf16[4,128,128]{2,1,0:T(8,128)(2,1)S(1)} %get-tuple-element.62), channel_id=1, source_target_pairs={{0,24},{8,16},{16,8},{24,0},{1,25},{9,17},{17,9},{25,1},{2,26},{10... | collective-permute-start | bytes 393224 | tf_op jit(solution)/shard_map/ppermute | solution.py:417
  50.5 11.3 %collective-permute-start.10 = (bf16[4,128,128]{2,1,0:T(8,128)(2,1)S(1)}, bf16[4,128,128]{2,1,0:T(8,128)(2,1)S(1)}, u32[]{:S(2)}, u32[]{:S(2)}) collective-permute-start(bf16[4,128,128]{2,1,0:T(8,128)(2,1)S(1)} %get-tuple-element.62), channel_id=1, source_target_pairs={{0,16},{8,24},{16,0},{24,8},{1,17},{9,25},{17,1},{25,9},{2,18},{10... | collective-permute-start | bytes 393224 | tf_op jit(solution)/shard_map/ppermute | solution.py:417
  50.5 8.7 %collective-permute-start.9 = (bf16[4,128,128]{2,1,0:T(8,128)(2,1)S(1)}, bf16[4,128,128]{2,1,0:T(8,128)(2,1)S(1)}, u32[]{:S(2)}, u32[]{:S(2)}) collective-permute-start(bf16[4,128,128]{2,1,0:T(8,128)(2,1)S(1)} %get-tuple-element.61), channel_id=1, source_target_pairs={{0,8},{8,0},{16,24},{24,16},{1,9},{9,1},{17,25},{25,17},{2,10},{10... | collective-permute-start | bytes 393224 | tf_op jit(solution)/shard_map/ppermute | solution.py:417
  51.3 10.5 %copy-start.3 = (bf16[4,2,128,128]{3,2,1,0:T(8,128)(2,1)S(1)}, bf16[4,2,128,128]{3,2,1,0:T(8,128)(2,1)}, u32[]{:S(2)}) copy-start(bf16[4,2,128,128]{3,2,1,0:T(8,128)(2,1)} %copy-done.1) | copy-start | bytes 786436
  61.9 26.9 %copy-start.5 = (bf16[4,4,3,144,128]{4,3,2,1,0:T(8,128)(2,1)S(1)}, bf16[4,4,3,144,128]{4,3,2,1,0:T(8,128)(2,1)}, u32[]{:S(2)}) copy-start(bf16[4,4,3,144,128]{4,3,2,1,0:T(8,128)(2,1)} %get-tuple-element.68.refs_3_) | copy-start | bytes 5308420
  64.5 24.2 %copy-start = (bf16[128,4096]{1,0:T(8,128)(2,1)S(1)}, bf16[128,4096]{1,0:T(8,128)(2,1)}, u32[]{:S(2)}) copy-start(bf16[128,4096]{1,0:T(8,128)(2,1)} %refs_6_.13) | copy-start | bytes 3145732
  64.5 24.2 %copy-start.10 = (bf16[4,2,128,512]{3,2,1,0:T(8,128)(2,1)S(1)}, bf16[4,2,128,512]{3,2,1,0:T(8,128)(2,1)}, u32[]{:S(2)}) copy-start(bf16[4,2,128,512]{3,2,1,0:T(8,128)(2,1)} %get-tuple-element.70.refs_5_) | copy-start | bytes 3145732
  64.6 24.2 %copy-start.11 = (bf16[4,3,16,512]{3,2,1,0:T(8,128)(2,1)S(1)}, bf16[4,3,16,512]{3,2,1,0:T(8,128)(2,1)}, u32[]{:S(2)}) copy-start(bf16[4,3,16,512]{3,2,1,0:T(8,128)(2,1)} %get-tuple-element.69.refs_4_) | copy-start | bytes 589828
  64.6 9.3 %collective-permute-start.15 = (bf16[4,2,128,128]{3,2,1,0:T(8,128)(2,1)S(1)}, bf16[4,2,128,128]{3,2,1,0:T(8,128)(2,1)S(1)}, u32[]{:S(2)}, u32[]{:S(2)}) collective-permute-start(bf16[4,2,128,128]{3,2,1,0:T(8,128)(2,1)S(1)} %get-tuple-element.71), channel_id=1, source_target_pairs={{0,1},{1,0},{2,3},{3,2},{4,5},{5,4},{6,7},{7,6},{8,9},{9,8},{10,11... | collective-permute-start | bytes 786440 | tf_op jit(solution)/shard_map/ppermute | solution.py:417
  64.6 10.9 %collective-permute-start.16 = (bf16[4,2,128,128]{3,2,1,0:T(8,128)(2,1)S(1)}, bf16[4,2,128,128]{3,2,1,0:T(8,128)(2,1)S(1)}, u32[]{:S(2)}, u32[]{:S(2)}) collective-permute-start(bf16[4,2,128,128]{3,2,1,0:T(8,128)(2,1)S(1)} %get-tuple-element.72), channel_id=1, source_target_pairs={{0,2},{1,3},{2,0},{3,1},{4,6},{5,7},{6,4},{7,5},{8,10},{9,11},{10,... | collective-permute-start | bytes 786440 | tf_op jit(solution)/shard_map/ppermute | solution.py:417
  66.8 10.2 %collective-permute-start.17 = (bf16[4,2,128,128]{3,2,1,0:T(8,128)(2,1)S(1)}, bf16[4,2,128,128]{3,2,1,0:T(8,128)(2,1)S(1)}, u32[]{:S(2)}, u32[]{:S(2)}) collective-permute-start(bf16[4,2,128,128]{3,2,1,0:T(8,128)(2,1)S(1)} %get-tuple-element.73), channel_id=1, source_target_pairs={{0,5},{1,4},{2,7},{3,6},{4,1},{5,0},{6,3},{7,2},{8,13},{9,12},{10,... | collective-permute-start | bytes 786440 | tf_op jit(solution)/shard_map/ppermute | solution.py:417
  66.8 21.9 %collective-permute-start.18 = (bf16[4,2,128,128]{3,2,1,0:T(8,128)(2,1)S(1)}, bf16[4,2,128,128]{3,2,1,0:T(8,128)(2,1)S(1)}, u32[]{:S(2)}, u32[]{:S(2)}) collective-permute-start(bf16[4,2,128,128]{3,2,1,0:T(8,128)(2,1)S(1)} %get-tuple-element.74), channel_id=1, source_target_pairs={{0,6},{1,7},{2,4},{3,5},{4,2},{5,3},{6,0},{7,1},{8,14},{9,15},{10,... | collective-permute-start | bytes 786440 | tf_op jit(solution)/shard_map/ppermute | solution.py:417
  71.0 21.6 %collective-permute-start.12 = (bf16[4,2,128,128]{3,2,1,0:T(8,128)(2,1)S(1)}, bf16[4,2,128,128]{3,2,1,0:T(8,128)(2,1)S(1)}, u32[]{:S(2)}, u32[]{:S(2)}) collective-permute-start(bf16[4,2,128,128]{3,2,1,0:T(8,128)(2,1)S(1)} %get-tuple-element.64), channel_id=1, source_target_pairs={{0,4},{1,5},{2,6},{3,7},{4,0},{5,1},{6,2},{7,3},{8,12},{9,13},{10,... | collective-permute-start | bytes 786440 | tf_op jit(solution)/shard_map/ppermute | solution.py:417
  73.9 18.7 %collective-permute-start.13 = (bf16[4,2,128,128]{3,2,1,0:T(8,128)(2,1)S(1)}, bf16[4,2,128,128]{3,2,1,0:T(8,128)(2,1)S(1)}, u32[]{:S(2)}, u32[]{:S(2)}) collective-permute-start(bf16[4,2,128,128]{3,2,1,0:T(8,128)(2,1)S(1)} %get-tuple-element.66), channel_id=1, source_target_pairs={{0,3},{1,2},{2,1},{3,0},{4,7},{5,6},{6,5},{7,4},{8,11},{9,10},{10,... | collective-permute-start | bytes 786440 | tf_op jit(solution)/shard_map/ppermute | solution.py:417
  75.5 17.1 %collective-permute-start.14 = (bf16[4,2,128,128]{3,2,1,0:T(8,128)(2,1)S(1)}, bf16[4,2,128,128]{3,2,1,0:T(8,128)(2,1)S(1)}, u32[]{:S(2)}, u32[]{:S(2)}) collective-permute-start(bf16[4,2,128,128]{3,2,1,0:T(8,128)(2,1)S(1)} %get-tuple-element.67), channel_id=1, source_target_pairs={{0,7},{1,6},{2,5},{3,4},{4,3},{5,2},{6,1},{7,0},{8,15},{9,14},{10,... | collective-permute-start | bytes 786440 | tf_op jit(solution)/shard_map/ppermute | solution.py:417
  88.7 3.9 %copy-start.4 = (bf16[4,4,3,144,128]{4,3,2,1,0:T(8,128)(2,1)S(1)}, bf16[4,4,3,144,128]{4,3,2,1,0:T(8,128)(2,1)}, u32[]{:S(2)}) copy-start(bf16[4,4,3,144,128]{4,3,2,1,0:T(8,128)(2,1)} %get-tuple-element.57.refs_3_) | copy-start | bytes 5308420
  88.8 3.9 %copy-start.9 = (bf16[4,2,128,512]{3,2,1,0:T(8,128)(2,1)S(1)}, bf16[4,2,128,512]{3,2,1,0:T(8,128)(2,1)}, u32[]{:S(2)}) copy-start(bf16[4,2,128,512]{3,2,1,0:T(8,128)(2,1)} %get-tuple-element.59.refs_5_) | copy-start | bytes 3145732
  88.8 3.9 %copy-start.12 = (bf16[4,3,16,512]{3,2,1,0:T(8,128)(2,1)S(1)}, bf16[4,3,16,512]{3,2,1,0:T(8,128)(2,1)}, u32[]{:S(2)}) copy-start(bf16[4,3,16,512]{3,2,1,0:T(8,128)(2,1)} %get-tuple-element.58.refs_4_) | copy-start | bytes 589828

commit v4 on v3

--- a/solution.py
+++ b/solution.py
@@ -104,9 +104,11 @@
 SMEM = pl.BlockSpec(memory_space=pltpu.SMEM)
 
 
-def marked_call(kernel, name, cols, near, remote, outs, scratch=(), flops=0, behind=(), aliases=()):
+def marked_call(
+    kernel, name, cols, near, remote, outs, scratch=(), flops=0, behind=(), arrived=(), aliases=()
+):
     args = [*near, *remote]
-    hidden = len(behind)
+    hidden = len(behind) + len(arrived)
     total = len(args) + len(outs)
 
     def body(cols, *refs):
@@ -119,7 +121,10 @@
     moved = sum(math.prod(x.shape) * jnp.dtype(x.dtype).itemsize for x in [*args, *outs])
     *results, mark = pl.pallas_call(
         body,
-        in_specs=[SMEM] * (1 + hidden) + [VMEM] * len(near) + [HBM] * len(remote),
+        in_specs=[SMEM] * (1 + len(behind))
+        + [pl.BlockSpec(memory_space=pl.ANY)] * len(arrived)
+        + [VMEM] * len(near)
+        + [HBM] * len(remote),
         out_specs=[out_spec(x) for x in outs] + [SMEM],
         out_shape=[*outs, shape((1,), jnp.int32)],
         scratch_shapes=scratch,
@@ -127,7 +132,7 @@
         compiler_params=params(),
         cost_estimate=cost(flops, moved),
         name=name,
-    )(cols, *behind, *near, *[far(x) for x in remote])
+    )(cols, *behind, *arrived, *near, *[far(x) for x in remote])
     return results, mark
 
 
@@ -169,7 +174,7 @@
             s_refs[p][h, 1] = dot(raw_ref[p, 3, :, own], qf, 0, 0).astype(BF16)
 
 
-def states_call(peers, heads, cols, raws, prev, taps, behind):
+def states_call(peers, heads, cols, raws, prev, taps, behind, arrived):
     rows = raws[0].shape[0]
     return marked_call(
         functools.partial(states_kernel, peers, heads),
@@ -185,11 +190,12 @@
         ],
         4 * peers * heads * rows * HEAD * HEAD,
         behind,
+        arrived,
     )
 
 
 def intra_kernel(
-    peers, heads, cols, prev_ref, next_ref, tq, tk, tv, q_hbm, k_hbm, v_hbm, g_hbm, _,
+    peers, heads, cols, prev_ref, next_ref, tq, tk, tv, q_hbm, k_hbm, v_hbm, g_hbm,
     d_hbm, e_hbm, f_hbm, raw_ref, d_ref, e_ref, f_ref, x_ref, sems,
 ):
     rows, width = raw_ref.shape[2:]
@@ -264,7 +270,7 @@
     wait(saves)
 
 
-def intra_call(peers, heads, cols, raws, prev, after, taps, arrived, behind):
+def intra_call(peers, heads, cols, raws, prev, after, taps, behind):
     rows = raws[0].shape[0]
     ext = rows + EDGE
     width = heads * HEAD
@@ -274,7 +280,7 @@
         "intra",
         cols,
         [prev, after, *taps],
-        [*raws, arrived],
+        raws,
         [pltpu.HBM(dims, BF16) for dims in outs],
         [pltpu.VMEM((peers, 4, rows, width), BF16)]
         + [pltpu.VMEM(dims, BF16) for dims in outs]
@@ -299,34 +305,32 @@
             out[h] = jnp.where(low, total[0], total[1]).astype(BF16)
 
 
-def members_kernel(count, planes, places, idx, *refs):
+def members_kernel(order, planes, targets, idx, *refs):
+    count = len(order)
     s_refs, z_refs = refs[:count], refs[count : count + planes - 1]
     outs = refs[count + planes - 1 :]
+    bits = count.bit_length() - 1
 
     def share(condition):
         return jnp.where(condition, 1.0, 0.0)
 
     lower = [share((idx[0] ^ d) < idx[0]) for d in range(1, planes)]
-    weights = [
-        [
-            (share(idx[1 + e] < idx[1 + place]), share(idx[1 + e] > idx[1 + place]))
-            for e in range(count)
-        ]
-        for place in places
-    ]
+    late = [[share(((idx[1] ^ d) >> b) & 1 == 1) for b in range(bits)] for d in targets]
     for h in range(z_refs[0].shape[0]):
         for top in range(0, HEAD, TILE):
             r = slice(top, top + TILE)
-            base = [0.0, 0.0]
-            for z_ref, low in zip(z_refs, lower):
-                got = z_ref[h, r].astype(F32)
-                base = [base[0] + got * low, base[1] + got * (1.0 - low)]
-            states = [[s_ref[h, i, r].astype(F32) for i in range(2)] for s_ref in s_refs]
-            for out, shares in zip(outs, weights):
-                for i in range(2):
-                    total = base[i]
-                    for state, weight in zip(states, shares):
-                        total = total + state[i] * weight[i]
+            for i in range(2):
+                base = 0.0
+                for z_ref, low in zip(z_refs, lower):
+                    base = base + z_ref[h, r].astype(F32) * (1.0 - low if i else low)
+                sums = [[s_refs[order.index(d)][h, i, r].astype(F32) for d in range(count)]]
+                for b in range(bits - 1):
+                    sums.append([x + y for x, y in zip(sums[b][::2], sums[b][1::2])])
+                for out, d, shares in zip(outs, targets, late):
+                    total = base
+                    for b in range(bits):
+                        weight = 1.0 - shares[b] if i else shares[b]
+                        total = total + sums[b][(d >> b) ^ 1] * weight
                     out[h, i, r] = total.astype(BF16)
 
 
@@ -411,7 +415,7 @@
     def numbers(ds):
         return (me ^ jnp.array(ds, jnp.int32)).astype(jnp.int32)
 
-    idx = jnp.concatenate([z[None].astype(jnp.int32), numbers(order)])
+    idx = jnp.stack([z, me]).astype(jnp.int32)
 
     def swap(field, axes, count, d):
         return lax.ppermute(field, axes, [(i, i ^ d) for i in range(count)]) if d else field
@@ -422,23 +426,24 @@
 
     states, mark = {}, []
 
-    def make_states(ds, mark):
-        out, mark = states_call(len(ds), heads, numbers(ds), raws, prev, taps, mark)
+    def make_states(ds, mark, arrived):
+        args = (numbers(ds), raws, prev, taps, mark, arrived)
+        out, mark = states_call(len(ds), heads, *args)
         states.update({d: swap(s, plane, members, d) for s, d in zip(out, ds)})
         return [mark]
 
     intra = {}
 
-    def make_intra(ds, arrived, mark):
-        args = (numbers(ds), raws, prev, after, taps, arrived, mark)
+    def make_intra(ds, mark):
+        args = (numbers(ds), raws, prev, after, taps, mark)
         intra[ds[0]], mark = intra_call(len(ds), heads, *args)
         return [mark]
 
     others = [*near, *diagonal]
-    mark = make_states(direct, mark)
-    mark = make_states(diagonal, mark)
-    mark = make_states(near, mark)
-    mark = make_intra(direct, states[direct[0]], mark)
+    mark = make_states(direct, mark, [])
+    mark = make_states(diagonal, mark, [after])
+    mark = make_states(near, mark, [states[direct[0]]])
+    mark = make_intra(direct, mark)
     states = [states[d] for d in order]
     bits = (planes - 1).bit_length()
     levels, mark = marked_call(
@@ -451,17 +456,18 @@
         behind=mark,
     )
     across = [swap(levels[d.bit_length() - 1], "z", planes, d) for d in range(1, planes)]
-    mark = make_intra(others, states[0], [mark])
+    mark = make_intra(others, [mark])
     backs = {}
     for ds in (direct, [*diagonal, *near]):
         sent, mark = marked_call(
-            functools.partial(members_kernel, members, planes, [order.index(d) for d in ds]),
+            functools.partial(members_kernel, order, planes, ds),
             "members",
             idx,
             [*states, *across],
             [],
             [shape((heads, 2, HEAD, HEAD))] * len(ds),
             behind=mark,
+            arrived=[backs[d] for d in direct[:1] if backs],
         )
         mark = [mark]
         backs |= {d: swap(s, plane, members, d) for s, d in zip(sent, ds)}

time: 96.8 us -> 89.5 us (0.925)
  waiting for transfers between devices: 27 us -> 17.8 us
  starting transfers between devices: 26.3 us -> 30.4 us
  Pallas kernels: 40.8 us -> 39.7 us
    ppermute x17, waiting for transfers between devices: 24.4 us -> 16.4 us  [swap(): lax.ppermute(field, axes, [(i, i ^ d) for i in range(count)])]
    ppermute x17, starting transfers between devices: 20.1 us -> 24.2 us  [swap(): lax.ppermute(field, axes, [(i, i ^ d) for i in range(count)])]
    ppermute x1, waiting for transfers between devices: 2.67 us -> 1.37 us  [local(): lax.ppermute(tail, everyone, [(i, i + 1) for i in range(devices - 1)])]
    pallas_call x10, Pallas kernels: 39.4 us -> 38.3 us  [marked_call(): pl.pallas_call(body, in_specs=[SMEM] * (1 + len(behind)) + [pl.BlockSpec(...]
  transfers between devices with their start and end apart: 19 -> 19, of which waited for: 7 -> 7; matrix products, arithmetic and copies ran while one was open for 0% -> 0% of each run, Pallas kernels for 29% -> 35%
where the time goes in v4:
time: 89.5 us; the launch traced here: 89.1 us
  Pallas kernels  39.7 us (44%)
  starting transfers between devices  30.4 us (34%)
  waiting for transfers between devices  17.8 us (20%)
  between operations  1.13 us (1%)
    pallas_call x10, Pallas kernels, marked_call(): pl.pallas_call(body, in_specs=[SMEM] * (1 + len(behind)) + [pl.BlockSpec(...  38.3 us
    ppermute x17, starting transfers between devices, swap(): lax.ppermute(field, axes, [(i, i ^ d) for i in range(count)])  24.2 us
    ppermute x17, waiting for transfers between devices, swap(): lax.ppermute(field, axes, [(i, i ^ d) for i in range(count)])  16.4 us
    ppermute x1, starting transfers between devices, local(): lax.ppermute(tail, everyone, [(i, i + 1) for i in range(devices - 1)])  4.85 us
  transfers between devices with their start and end apart: 19, of which 7 were waited for; matrix products, arithmetic and copies ran while one was open for 0% of the time, Pallas kernels for 35%

profile of v4, /device:TPU:0, one launch (start us, length us, event | category | flops | bytes accessed | tf_op | source)
XLA Modules:
  0.0 89.1 jit_solution(5952973437523213608)
XLA Ops:
  0.6 0.0 copy-start.13
  0.7 1.4 %pack.1 = (bf16[16,4096]{1,0:T(8,128)(2,1)S(1)}, bf16[16,4096]{1,0:T(8,128)(2,1)S(1)}) custom-call(bf16[128,4096]{1,0:T(8,128)(2,1)} %refs_6_.11, bf16[128,4096]{1,0:T(8,128)(2,1)} %refs_7_.9, bf16[128,4096]{1,0:T(8,128)(2,1)} %refs_8_.7, bf16[128,4096]{1,0:T(8,128)(2,1)} %refs_6_.13), custom_call_target="tpu_custom_call" | custom-call | bytes 1179648 | tf_op jit(solution)/shard_map/pack/pallas_call | solution.py:70
  2.1 4.8 %collective-permute-start = (bf16[16,4096]{1,0:T(8,128)(2,1)S(1)}, bf16[16,4096]{1,0:T(8,128)(2,1)S(1)}, u32[]{:S(2)}, u32[]{:S(2)}) collective-permute-start(bf16[16,4096]{1,0:T(8,128)(2,1)S(1)} %get-tuple-element.42), channel_id=1, source_target_pairs={{0,1},{1,2},{2,3},{3,4},{4,5},{5,6},{6,7},{7,8},{8,9},{9,10},{10,1... | collective-permute-start | bytes 393224 | tf_op jit(solution)/shard_map/ppermute | solution.py:424
  6.9 1.3 %collective-permute-start.1 = (bf16[16,4096]{1,0:T(8,128)(2,1)S(1)}, bf16[16,4096]{1,0:T(8,128)(2,1)S(1)}, u32[]{:S(2)}, u32[]{:S(2)}) collective-permute-start(bf16[16,4096]{1,0:T(8,128)(2,1)S(1)} %get-tuple-element.44), channel_id=1, source_target_pairs={{1,0},{2,1},{3,2},{4,3},{5,4},{6,5},{7,6},{8,7},{9,8},{10,9},{11,1... | collective-permute-start | bytes 393224 | tf_op jit(solution)/shard_map/ppermute | solution.py:425
  8.2 0.0 copy-start.12
  8.3 0.0 copy-start.11
  8.3 1.4 %collective-permute-done.refs_0_.refs_2_.refs_1_ = bf16[16,4096]{1,0:T(8,128)(2,1)S(1)} collective-permute-done((bf16[16,4096]{1,0:T(8,128)(2,1)S(1)}, bf16[16,4096]{1,0:T(8,128)(2,1)S(1)}, u32[]{:S(2)}, u32[]{:S(2)}) %collective-permute-start) | collective-permute-done | bytes 131104 | tf_op jit(solution)/shard_map/ppermute | solution.py:424
  9.7 3.6 %states.3 = (bf16[4,2,128,128]{3,2,1,0:T(8,128)(2,1)S(1)}, bf16[4,2,128,128]{3,2,1,0:T(8,128)(2,1)S(1)}, bf16[4,2,128,128]{3,2,1,0:T(8,128)(2,1)S(1)}, bf16[4,2,128,128]{3,2,1,0:T(8,128)(2,1)S(1)}, s32[1]{0:T(128)}) custom-call(s32[4]{0:T(128)S(1)} %broadcast_xor_fusion.2.cols, bf16[16,4096]{1,0:T(8,128)(2,1)S(1)} %collective-permute-done.refs_0_.refs_2_.refs_1_, ...), custom_call_target="tpu_custom_call" | custom-call | flops 134217728 | bytes 5472256 | tf_op jit(solution)/shard_map/states/pallas_call | solution.py:122
  13.3 2.6 %collective-permute-start.2 = (bf16[4,2,128,128]{3,2,1,0:T(8,128)(2,1)S(1)}, bf16[4,2,128,128]{3,2,1,0:T(8,128)(2,1)S(1)}, u32[]{:S(2)}, u32[]{:S(2)}) collective-permute-start(bf16[4,2,128,128]{3,2,1,0:T(8,128)(2,1)S(1)} %get-tuple-element.46), channel_id=1, source_target_pairs={{0,1},{1,0},{2,3},{3,2},{4,5},{5,4},{6,7},{7,6},{8,9},{9,8},{10,11... | collective-permute-start | bytes 786440 | tf_op jit(solution)/shard_map/ppermute | solution.py:421
  15.9 1.6 %collective-permute-start.3 = (bf16[4,2,128,128]{3,2,1,0:T(8,128)(2,1)S(1)}, bf16[4,2,128,128]{3,2,1,0:T(8,128)(2,1)S(1)}, u32[]{:S(2)}, u32[]{:S(2)}) collective-permute-start(bf16[4,2,128,128]{3,2,1,0:T(8,128)(2,1)S(1)} %get-tuple-element.49), channel_id=1, source_target_pairs={{0,2},{1,3},{2,0},{3,1},{4,6},{5,7},{6,4},{7,5},{8,10},{9,11},{10,... | collective-permute-start | bytes 786440 | tf_op jit(solution)/shard_map/ppermute | solution.py:421
  17.5 0.1 collective-permute-start.4
  17.6 1.7 %collective-permute-start.5 = (bf16[4,2,128,128]{3,2,1,0:T(8,128)(2,1)S(1)}, bf16[4,2,128,128]{3,2,1,0:T(8,128)(2,1)S(1)}, u32[]{:S(2)}, u32[]{:S(2)}) collective-permute-start(bf16[4,2,128,128]{3,2,1,0:T(8,128)(2,1)S(1)} %get-tuple-element.51), channel_id=1, source_target_pairs={{0,6},{1,7},{2,4},{3,5},{4,2},{5,3},{6,0},{7,1},{8,14},{9,15},{10,... | collective-permute-start | bytes 786440 | tf_op jit(solution)/shard_map/ppermute | solution.py:421
  19.3 0.0 collective-permute-done.1.refs_1_.refs_2_
  19.3 3.3 %states.4 = (bf16[4,2,128,128]{3,2,1,0:T(8,128)(2,1)S(1)}, bf16[4,2,128,128]{3,2,1,0:T(8,128)(2,1)S(1)}, s32[1]{0:T(128)}) custom-call(s32[2]{0:T(128)S(1)} %broadcast_xor_fusion.cols, s32[1]{0:T(128)} %get-tuple-element.43.refs_0_, bf16[16,4096]{1,0:T(8,128)(2,1)S(1)} %collective-permute-done.1.refs_1_.refs_2_, ...), custom_call_target="tpu_custom_call" | custom-call | flops 67108864 | bytes 4947968 | tf_op jit(solution)/shard_map/states/pallas_call | solution.py:122
  22.6 1.6 %collective-permute-start.6 = (bf16[4,2,128,128]{3,2,1,0:T(8,128)(2,1)S(1)}, bf16[4,2,128,128]{3,2,1,0:T(8,128)(2,1)S(1)}, u32[]{:S(2)}, u32[]{:S(2)}) collective-permute-start(bf16[4,2,128,128]{3,2,1,0:T(8,128)(2,1)S(1)} %get-tuple-element.52), channel_id=1, source_target_pairs={{0,3},{1,2},{2,1},{3,0},{4,7},{5,6},{6,5},{7,4},{8,11},{9,10},{10,... | collective-permute-start | bytes 786440 | tf_op jit(solution)/shard_map/ppermute | solution.py:421
  24.2 1.1 %collective-permute-start.7 = (bf16[4,2,128,128]{3,2,1,0:T(8,128)(2,1)S(1)}, bf16[4,2,128,128]{3,2,1,0:T(8,128)(2,1)S(1)}, u32[]{:S(2)}, u32[]{:S(2)}) collective-permute-start(bf16[4,2,128,128]{3,2,1,0:T(8,128)(2,1)S(1)} %get-tuple-element.53), channel_id=1, source_target_pairs={{0,7},{1,6},{2,5},{3,4},{4,3},{5,2},{6,1},{7,0},{8,15},{9,14},{10,... | collective-permute-start | bytes 786440 | tf_op jit(solution)/shard_map/ppermute | solution.py:421
  25.3 3.5 %states.5 = (bf16[4,2,128,128]{3,2,1,0:T(8,128)(2,1)}, bf16[4,2,128,128]{3,2,1,0:T(8,128)(2,1)S(1)}, s32[1]{0:T(128)}) custom-call(s32[2]{0:T(128)S(1)} %broadcast_xor_fusion.1.cols, s32[1]{0:T(128)} %get-tuple-element.45.refs_0_, bf16[4,2,128,128]{3,2,1,0:T(8,128)(2,1)S(1)} %collective-permute-done.2.refs_1_.refs_2_, ...), custom_call_target="tpu_custom_call" | custom-call | flops 67108864 | bytes 4947968 | tf_op jit(solution)/shard_map/states/pallas_call | solution.py:122
  28.9 0.0 collective-permute-done.3.refs_2_.refs_3_
  28.9 0.8 collective-permute-start.8
  29.7 0.1 pad_add_fusion.cols
  29.7 7.3 %intra.2 = (bf16[4,4,3,144,128]{4,3,2,1,0:T(8,128)(2,1)}, bf16[4,3,16,512]{3,2,1,0:T(8,128)(2,1)}, bf16[4,2,128,512]{3,2,1,0:T(8,128)(2,1)}, s32[1]{0:T(128)}) custom-call(s32[4]{0:T(128)S(1)} %broadcast_xor_fusion.2.cols, s32[1]{0:T(128)} %get-tuple-element.47.refs_0_, bf16[16,4096]{1,0:T(8,128)(2,1)S(1)} %collective-permute-done.refs_0_.refs_2_.refs_1_, ...), custom_call_target="tpu_custom_call" | custom-call | flops 402653184 | bytes 7569408 | tf_op jit(solution)/shard_map/intra/pallas_call | solution.py:122
  37.1 0.0 copy-start.10
  37.1 0.0 collective-permute-done.5.refs_4_.refs_5_
  37.1 0.7 collective-permute-done.7.refs_6_.refs_7_
  37.9 0.0 collective-permute-done.8.refs_7_.refs_8_
  37.9 1.7 %sums.1 = (bf16[4,128,128]{2,1,0:T(8,128)(2,1)S(1)}, bf16[4,128,128]{2,1,0:T(8,128)(2,1)S(1)}, s32[1]{0:T(128)}) custom-call(s32[2]{0:T(128)S(1)} %pad_add_fusion.cols, s32[1]{0:T(128)} %get-tuple-element.48.refs_0_, bf16[4,2,128,128]{3,2,1,0:T(8,128)(2,1)S(1)} %collective-permute-done.2.refs_1_.refs_2_, ...), custom_call_target="tpu_custom_call" | custom-call | bytes 2359296 | tf_op jit(solution)/shard_map/sums/pallas_call | solution.py:122
  39.6 6.2 %collective-permute-start.11 = (bf16[4,128,128]{2,1,0:T(8,128)(2,1)S(1)}, bf16[4,128,128]{2,1,0:T(8,128)(2,1)S(1)}, u32[]{:S(2)}, u32[]{:S(2)}) collective-permute-start(bf16[4,128,128]{2,1,0:T(8,128)(2,1)S(1)} %get-tuple-element.62), channel_id=1, source_target_pairs={{0,24},{8,16},{16,8},{24,0},{1,25},{9,17},{17,9},{25,1},{2,26},{10... | collective-permute-start | bytes 393224 | tf_op jit(solution)/shard_map/ppermute | solution.py:421
  45.8 0.6 collective-permute-start.9
  46.4 7.3 %intra.3 = (bf16[4,4,3,144,128]{4,3,2,1,0:T(8,128)(2,1)}, bf16[4,3,16,512]{3,2,1,0:T(8,128)(2,1)}, bf16[4,2,128,512]{3,2,1,0:T(8,128)(2,1)}, s32[1]{0:T(128)}) custom-call(s32[4]{0:T(128)S(1)} %broadcast_xor_fusion.3.cols, s32[1]{0:T(128)} %get-tuple-element.56.refs_0_, bf16[16,4096]{1,0:T(8,128)(2,1)S(1)} %collective-permute-done.refs_0_.refs_2_.refs_1_, ...), custom_call_target="tpu_custom_call" | custom-call | flops 402653184 | bytes 7569408 | tf_op jit(solution)/shard_map/intra/pallas_call | solution.py:122
  53.8 1.2 %collective-permute-done.9.refs_9_.refs_10_ = bf16[4,128,128]{2,1,0:T(8,128)(2,1)S(1)} collective-permute-done((bf16[4,128,128]{2,1,0:T(8,128)(2,1)S(1)}, bf16[4,128,128]{2,1,0:T(8,128)(2,1)S(1)}, u32[]{:S(2)}, u32[]{:S(2)}) %collective-permute-start.9) | collective-permute-done | bytes 131104 | tf_op jit(solution)/shard_map/ppermute | solution.py:421
  55.0 0.8 collective-permute-done.10.refs_10_.refs_11_
  55.8 2.0 %members.2 = (bf16[4,2,128,128]{3,2,1,0:T(8,128)(2,1)S(1)}, bf16[4,2,128,128]{3,2,1,0:T(8,128)(2,1)S(1)}, bf16[4,2,128,128]{3,2,1,0:T(8,128)(2,1)S(1)}, bf16[4,2,128,128]{3,2,1,0:T(8,128)(2,1)S(1)}, s32[1]{0:T(128)}) custom-call(s32[2]{0:T(128)S(1)} %pad_add_fusion.cols, s32[1]{0:T(128)} %get-tuple-element.60.refs_0_, ...), custom_call_target="tpu_custom_call" | custom-call | bytes 3538944 | tf_op jit(solution)/shard_map/members/pallas_call | solution.py:122
  57.8 0.0 copy-start
  57.8 0.0 copy-start.7
  57.9 0.0 copy-start.8
  57.9 3.3 %collective-permute-start.12 = (bf16[4,2,128,128]{3,2,1,0:T(8,128)(2,1)S(1)}, bf16[4,2,128,128]{3,2,1,0:T(8,128)(2,1)S(1)}, u32[]{:S(2)}, u32[]{:S(2)}) collective-permute-start(bf16[4,2,128,128]{3,2,1,0:T(8,128)(2,1)S(1)} %get-tuple-element.64), channel_id=1, source_target_pairs={{0,1},{1,0},{2,3},{3,2},{4,5},{5,4},{6,7},{7,6},{8,9},{9,8},{10,11... | collective-permute-start | bytes 786440 | tf_op jit(solution)/shard_map/ppermute | solution.py:421
  61.2 0.3 collective-permute-start.16
  61.4 0.2 collective-permute-start.17
  61.6 1.4 %collective-permute-start.18 = (bf16[4,2,128,128]{3,2,1,0:T(8,128)(2,1)S(1)}, bf16[4,2,128,128]{3,2,1,0:T(8,128)(2,1)S(1)}, u32[]{:S(2)}, u32[]{:S(2)}) collective-permute-start(bf16[4,2,128,128]{3,2,1,0:T(8,128)(2,1)S(1)} %get-tuple-element.74), channel_id=1, source_target_pairs={{0,6},{1,7},{2,4},{3,5},{4,2},{5,3},{6,0},{7,1},{8,14},{9,15},{10,... | collective-permute-start | bytes 786440 | tf_op jit(solution)/shard_map/ppermute | solution.py:421
  63.0 5.3 %collective-permute-done.12.refs_1_.refs_7_ = bf16[4,2,128,128]{3,2,1,0:T(8,128)(2,1)S(1)} collective-permute-done((bf16[4,2,128,128]{3,2,1,0:T(8,128)(2,1)S(1)}, bf16[4,2,128,128]{3,2,1,0:T(8,128)(2,1)S(1)}, u32[]{:S(2)}, u32[]{:S(2)}) %collective-permute-start.12) | collective-permute-done | bytes 262176 | tf_op jit(solution)/shard_map/ppermute | solution.py:421
  68.3 2.2 %members.3 = (bf16[4,2,128,128]{3,2,1,0:T(8,128)(2,1)S(1)}, bf16[4,2,128,128]{3,2,1,0:T(8,128)(2,1)S(1)}, bf16[4,2,128,128]{3,2,1,0:T(8,128)(2,1)S(1)}, bf16[4,2,128,128]{3,2,1,0:T(8,128)(2,1)S(1)}, s32[1]{0:T(128)}) custom-call(s32[2]{0:T(128)S(1)} %pad_add_fusion.cols, s32[1]{0:T(128)} %get-tuple-element.63.refs_0_, ...), custom_call_target="tpu_custom_call" | custom-call | bytes 3538944 | tf_op jit(solution)/shard_map/members/pallas_call | solution.py:122
  70.5 0.1 collective-permute-start.13
  70.6 1.9 %collective-permute-start.14 = (bf16[4,2,128,128]{3,2,1,0:T(8,128)(2,1)S(1)}, bf16[4,2,128,128]{3,2,1,0:T(8,128)(2,1)S(1)}, u32[]{:S(2)}, u32[]{:S(2)}) collective-permute-start(bf16[4,2,128,128]{3,2,1,0:T(8,128)(2,1)S(1)} %get-tuple-element.67), channel_id=1, source_target_pairs={{0,3},{1,2},{2,1},{3,0},{4,7},{5,6},{6,5},{7,4},{8,11},{9,10},{10,... | collective-permute-start | bytes 786440 | tf_op jit(solution)/shard_map/ppermute | solution.py:421
  72.4 0.9 %collective-permute-start.15 = (bf16[4,2,128,128]{3,2,1,0:T(8,128)(2,1)S(1)}, bf16[4,2,128,128]{3,2,1,0:T(8,128)(2,1)S(1)}, u32[]{:S(2)}, u32[]{:S(2)}) collective-permute-start(bf16[4,2,128,128]{3,2,1,0:T(8,128)(2,1)S(1)} %get-tuple-element.68), channel_id=1, source_target_pairs={{0,7},{1,6},{2,5},{3,4},{4,3},{5,2},{6,1},{7,0},{8,15},{9,14},{10,... | collective-permute-start | bytes 786440 | tf_op jit(solution)/shard_map/ppermute | solution.py:421
  73.4 3.6 %grads.2 = (bf16[128,4096]{1,0:T(8,128)(2,1)}, bf16[128,4096]{1,0:T(8,128)(2,1)}, bf16[128,4096]{1,0:T(8,128)(2,1)}, s32[1]{0:T(128)}) custom-call(s32[4]{0:T(128)S(1)} %broadcast_xor_fusion.2.cols, bf16[4,4096]{1,0:T(4,128)(2,1)S(1)} %copy-done.3, bf16[4,4096]{1,0:T(4,128)(2,1)S(1)} %copy-done.4, bf16[4,4096]{1,0:T(4,128)(2,1)S(1)} %copy-done.5, ...), custom_call_target="tpu_custom_call" | custom-call | flops 226492416 | bytes 8355840 | tf_op jit(solution)/shard_map/grads/pallas_call | solution.py:122
  77.1 3.6 %collective-permute-done.14.refs_9_ = bf16[4,2,128,128]{3,2,1,0:T(8,128)(2,1)S(1)} collective-permute-done((bf16[4,2,128,128]{3,2,1,0:T(8,128)(2,1)S(1)}, bf16[4,2,128,128]{3,2,1,0:T(8,128)(2,1)S(1)}, u32[]{:S(2)}, u32[]{:S(2)}) %collective-permute-start.14) | collective-permute-done | bytes 262176 | tf_op jit(solution)/shard_map/ppermute | solution.py:421
  80.7 4.7 %collective-permute-done.15.refs_10_ = bf16[4,2,128,128]{3,2,1,0:T(8,128)(2,1)S(1)} collective-permute-done((bf16[4,2,128,128]{3,2,1,0:T(8,128)(2,1)S(1)}, bf16[4,2,128,128]{3,2,1,0:T(8,128)(2,1)S(1)}, u32[]{:S(2)}, u32[]{:S(2)}) %collective-permute-start.15) | collective-permute-done | bytes 262176 | tf_op jit(solution)/shard_map/ppermute | solution.py:421
  85.4 3.6 %grads.3 = (bf16[128,4096]{1,0:T(8,128)(2,1)}, bf16[128,4096]{1,0:T(8,128)(2,1)}, bf16[128,4096]{1,0:T(8,128)(2,1)}, s32[1]{0:T(128)}) custom-call(s32[4]{0:T(128)S(1)} %broadcast_xor_fusion.3.cols, bf16[4,4096]{1,0:T(4,128)(2,1)S(1)} %copy-done.3, bf16[4,4096]{1,0:T(4,128)(2,1)S(1)} %copy-done.4, ...), custom_call_target="tpu_custom_call", output_to_operand_aliasing={{0}: (12, {}), {1}: (13, {}), {2}: (14, {})} | custom-call | flops 226492416 | bytes 11501568 | tf_op jit(solution)/shard_map/grads/pallas_call | solution.py:122
  (34 shorter events, 0.1 us)
Async XLA Ops:
  0.6 7.6 %copy-start.13 = (s32[4]{0:T(128)S(1)}, s32[4]{0:T(128)}, u32[]{:S(2)}) copy-start(s32[4]{0:T(128)} %constant.24.clone) | copy-start | bytes 52
  0.6 9.0 %copy-start.5 = (bf16[4,4096]{1,0:T(4,128)(2,1)S(1)}, bf16[4,4096]{1,0:T(4,128)(2,1)}, u32[]{:S(2)}) copy-start(bf16[4,4096]{1,0:T(4,128)(2,1)} %refs_2_.5) | copy-start | bytes 98308
  0.7 9.0 %copy-start.4 = (bf16[4,4096]{1,0:T(4,128)(2,1)S(1)}, bf16[4,4096]{1,0:T(4,128)(2,1)}, u32[]{:S(2)}) copy-start(bf16[4,4096]{1,0:T(4,128)(2,1)} %refs_1_.5) | copy-start | bytes 98308
  0.7 9.0 %copy-start.3 = (bf16[4,4096]{1,0:T(4,128)(2,1)S(1)}, bf16[4,4096]{1,0:T(4,128)(2,1)}, u32[]{:S(2)}) copy-start(bf16[4,4096]{1,0:T(4,128)(2,1)} %refs_0_.3) | copy-start | bytes 98308
  2.1 7.6 %collective-permute-start = (bf16[16,4096]{1,0:T(8,128)(2,1)S(1)}, bf16[16,4096]{1,0:T(8,128)(2,1)S(1)}, u32[]{:S(2)}, u32[]{:S(2)}) collective-permute-start(bf16[16,4096]{1,0:T(8,128)(2,1)S(1)} %get-tuple-element.42), channel_id=1, source_target_pairs={{0,1},{1,2},{2,3},{3,4},{4,5},{5,6},{6,7},{7,8},{8,9},{9,10},{10,1... | collective-permute-start | bytes 393224 | tf_op jit(solution)/shard_map/ppermute | solution.py:424
  6.9 12.4 %collective-permute-start.1 = (bf16[16,4096]{1,0:T(8,128)(2,1)S(1)}, bf16[16,4096]{1,0:T(8,128)(2,1)S(1)}, u32[]{:S(2)}, u32[]{:S(2)}) collective-permute-start(bf16[16,4096]{1,0:T(8,128)(2,1)S(1)} %get-tuple-element.44), channel_id=1, source_target_pairs={{1,0},{2,1},{3,2},{4,3},{5,4},{6,5},{7,6},{8,7},{9,8},{10,9},{11,1... | collective-permute-start | bytes 393224 | tf_op jit(solution)/shard_map/ppermute | solution.py:425
  8.2 9.3 %copy-start.12 = (s32[2]{0:T(128)S(1)}, s32[2]{0:T(128)}, u32[]{:S(2)}) copy-start(s32[2]{0:T(128)} %constant.25.clone) | copy-start | bytes 28
  8.3 9.3 %copy-start.11 = (s32[2]{0:T(128)S(1)}, s32[2]{0:T(128)}, u32[]{:S(2)}) copy-start(s32[2]{0:T(128)} %constant.26.clone) | copy-start | bytes 28
  13.3 10.9 %collective-permute-start.2 = (bf16[4,2,128,128]{3,2,1,0:T(8,128)(2,1)S(1)}, bf16[4,2,128,128]{3,2,1,0:T(8,128)(2,1)S(1)}, u32[]{:S(2)}, u32[]{:S(2)}) collective-permute-start(bf16[4,2,128,128]{3,2,1,0:T(8,128)(2,1)S(1)} %get-tuple-element.46), channel_id=1, source_target_pairs={{0,1},{1,0},{2,3},{3,2},{4,5},{5,4},{6,7},{7,6},{8,9},{9,8},{10,11... | collective-permute-start | bytes 786440 | tf_op jit(solution)/shard_map/ppermute | solution.py:421
  15.9 13.0 %collective-permute-start.3 = (bf16[4,2,128,128]{3,2,1,0:T(8,128)(2,1)S(1)}, bf16[4,2,128,128]{3,2,1,0:T(8,128)(2,1)S(1)}, u32[]{:S(2)}, u32[]{:S(2)}) collective-permute-start(bf16[4,2,128,128]{3,2,1,0:T(8,128)(2,1)S(1)} %get-tuple-element.49), channel_id=1, source_target_pairs={{0,2},{1,3},{2,0},{3,1},{4,6},{5,7},{6,4},{7,5},{8,10},{9,11},{10,... | collective-permute-start | bytes 786440 | tf_op jit(solution)/shard_map/ppermute | solution.py:421
  17.5 19.6 %collective-permute-start.4 = (bf16[4,2,128,128]{3,2,1,0:T(8,128)(2,1)S(1)}, bf16[4,2,128,128]{3,2,1,0:T(8,128)(2,1)S(1)}, u32[]{:S(2)}, u32[]{:S(2)}) collective-permute-start(bf16[4,2,128,128]{3,2,1,0:T(8,128)(2,1)S(1)} %get-tuple-element.50), channel_id=1, source_target_pairs={{0,5},{1,4},{2,7},{3,6},{4,1},{5,0},{6,3},{7,2},{8,13},{9,12},{10,... | collective-permute-start | bytes 786440 | tf_op jit(solution)/shard_map/ppermute | solution.py:421
  17.6 19.5 %collective-permute-start.5 = (bf16[4,2,128,128]{3,2,1,0:T(8,128)(2,1)S(1)}, bf16[4,2,128,128]{3,2,1,0:T(8,128)(2,1)S(1)}, u32[]{:S(2)}, u32[]{:S(2)}) collective-permute-start(bf16[4,2,128,128]{3,2,1,0:T(8,128)(2,1)S(1)} %get-tuple-element.51), channel_id=1, source_target_pairs={{0,6},{1,7},{2,4},{3,5},{4,2},{5,3},{6,0},{7,1},{8,14},{9,15},{10,... | collective-permute-start | bytes 786440 | tf_op jit(solution)/shard_map/ppermute | solution.py:421
  22.6 14.5 %collective-permute-start.6 = (bf16[4,2,128,128]{3,2,1,0:T(8,128)(2,1)S(1)}, bf16[4,2,128,128]{3,2,1,0:T(8,128)(2,1)S(1)}, u32[]{:S(2)}, u32[]{:S(2)}) collective-permute-start(bf16[4,2,128,128]{3,2,1,0:T(8,128)(2,1)S(1)} %get-tuple-element.52), channel_id=1, source_target_pairs={{0,3},{1,2},{2,1},{3,0},{4,7},{5,6},{6,5},{7,4},{8,11},{9,10},{10,... | collective-permute-start | bytes 786440 | tf_op jit(solution)/shard_map/ppermute | solution.py:421
  24.2 13.6 %collective-permute-start.7 = (bf16[4,2,128,128]{3,2,1,0:T(8,128)(2,1)S(1)}, bf16[4,2,128,128]{3,2,1,0:T(8,128)(2,1)S(1)}, u32[]{:S(2)}, u32[]{:S(2)}) collective-permute-start(bf16[4,2,128,128]{3,2,1,0:T(8,128)(2,1)S(1)} %get-tuple-element.53), channel_id=1, source_target_pairs={{0,7},{1,6},{2,5},{3,4},{4,3},{5,2},{6,1},{7,0},{8,15},{9,14},{10,... | collective-permute-start | bytes 786440 | tf_op jit(solution)/shard_map/ppermute | solution.py:421
  28.9 9.0 %collective-permute-start.8 = (bf16[4,2,128,128]{3,2,1,0:T(8,128)(2,1)}, bf16[4,2,128,128]{3,2,1,0:T(8,128)(2,1)S(1)}, u32[]{:S(2)}, u32[]{:S(2)}) collective-permute-start(bf16[4,2,128,128]{3,2,1,0:T(8,128)(2,1)} %get-tuple-element.54), channel_id=1, source_target_pairs={{0,4},{1,5},{2,6},{3,7},{4,0},{5,1},{6,2},{7,3},{8,12},{9,13},{10,... | collective-permute-start | bytes 786440 | tf_op jit(solution)/shard_map/ppermute | solution.py:421
  37.1 9.3 %copy-start.10 = (s32[4]{0:T(128)S(1)}, s32[4]{0:T(128)}, u32[]{:S(2)}) copy-start(s32[4]{0:T(128)} %constant.27.clone) | copy-start | bytes 52
  39.6 15.4 %collective-permute-start.11 = (bf16[4,128,128]{2,1,0:T(8,128)(2,1)S(1)}, bf16[4,128,128]{2,1,0:T(8,128)(2,1)S(1)}, u32[]{:S(2)}, u32[]{:S(2)}) collective-permute-start(bf16[4,128,128]{2,1,0:T(8,128)(2,1)S(1)} %get-tuple-element.62), channel_id=1, source_target_pairs={{0,24},{8,16},{16,8},{24,0},{1,25},{9,17},{17,9},{25,1},{2,26},{10... | collective-permute-start | bytes 393224 | tf_op jit(solution)/shard_map/ppermute | solution.py:421
  45.8 10.0 %collective-permute-start.10 = (bf16[4,128,128]{2,1,0:T(8,128)(2,1)S(1)}, bf16[4,128,128]{2,1,0:T(8,128)(2,1)S(1)}, u32[]{:S(2)}, u32[]{:S(2)}) collective-permute-start(bf16[4,128,128]{2,1,0:T(8,128)(2,1)S(1)} %get-tuple-element.62), channel_id=1, source_target_pairs={{0,16},{8,24},{16,0},{24,8},{1,17},{9,25},{17,1},{25,9},{2,18},{10... | collective-permute-start | bytes 393224 | tf_op jit(solution)/shard_map/ppermute | solution.py:421
  45.8 9.2 %collective-permute-start.9 = (bf16[4,128,128]{2,1,0:T(8,128)(2,1)S(1)}, bf16[4,128,128]{2,1,0:T(8,128)(2,1)S(1)}, u32[]{:S(2)}, u32[]{:S(2)}) collective-permute-start(bf16[4,128,128]{2,1,0:T(8,128)(2,1)S(1)} %get-tuple-element.61), channel_id=1, source_target_pairs={{0,8},{8,0},{16,24},{24,16},{1,9},{9,1},{17,25},{25,17},{2,10},{10... | collective-permute-start | bytes 393224 | tf_op jit(solution)/shard_map/ppermute | solution.py:421
  55.8 17.6 %copy-start.2 = (bf16[4,4,3,144,128]{4,3,2,1,0:T(8,128)(2,1)S(1)}, bf16[4,4,3,144,128]{4,3,2,1,0:T(8,128)(2,1)}, u32[]{:S(2)}) copy-start(bf16[4,4,3,144,128]{4,3,2,1,0:T(8,128)(2,1)} %get-tuple-element.69.refs_3_) | copy-start | bytes 5308420
  57.8 15.5 %copy-start = (bf16[128,4096]{1,0:T(8,128)(2,1)S(1)}, bf16[128,4096]{1,0:T(8,128)(2,1)}, u32[]{:S(2)}) copy-start(bf16[128,4096]{1,0:T(8,128)(2,1)} %refs_6_.13) | copy-start | bytes 3145732
  57.8 15.5 %copy-start.7 = (bf16[4,2,128,512]{3,2,1,0:T(8,128)(2,1)S(1)}, bf16[4,2,128,512]{3,2,1,0:T(8,128)(2,1)}, u32[]{:S(2)}) copy-start(bf16[4,2,128,512]{3,2,1,0:T(8,128)(2,1)} %get-tuple-element.71.refs_5_) | copy-start | bytes 3145732
  57.9 15.5 %copy-start.8 = (bf16[4,3,16,512]{3,2,1,0:T(8,128)(2,1)S(1)}, bf16[4,3,16,512]{3,2,1,0:T(8,128)(2,1)}, u32[]{:S(2)}) copy-start(bf16[4,3,16,512]{3,2,1,0:T(8,128)(2,1)} %get-tuple-element.70.refs_4_) | copy-start | bytes 589828
  57.9 10.4 %collective-permute-start.12 = (bf16[4,2,128,128]{3,2,1,0:T(8,128)(2,1)S(1)}, bf16[4,2,128,128]{3,2,1,0:T(8,128)(2,1)S(1)}, u32[]{:S(2)}, u32[]{:S(2)}) collective-permute-start(bf16[4,2,128,128]{3,2,1,0:T(8,128)(2,1)S(1)} %get-tuple-element.64), channel_id=1, source_target_pairs={{0,1},{1,0},{2,3},{3,2},{4,5},{5,4},{6,7},{7,6},{8,9},{9,8},{10,11... | collective-permute-start | bytes 786440 | tf_op jit(solution)/shard_map/ppermute | solution.py:421
  61.2 11.3 %collective-permute-start.16 = (bf16[4,2,128,128]{3,2,1,0:T(8,128)(2,1)S(1)}, bf16[4,2,128,128]{3,2,1,0:T(8,128)(2,1)S(1)}, u32[]{:S(2)}, u32[]{:S(2)}) collective-permute-start(bf16[4,2,128,128]{3,2,1,0:T(8,128)(2,1)S(1)} %get-tuple-element.72), channel_id=1, source_target_pairs={{0,2},{1,3},{2,0},{3,1},{4,6},{5,7},{6,4},{7,5},{8,10},{9,11},{10,... | collective-permute-start | bytes 786440 | tf_op jit(solution)/shard_map/ppermute | solution.py:421
  61.4 11.9 %collective-permute-start.17 = (bf16[4,2,128,128]{3,2,1,0:T(8,128)(2,1)S(1)}, bf16[4,2,128,128]{3,2,1,0:T(8,128)(2,1)S(1)}, u32[]{:S(2)}, u32[]{:S(2)}) collective-permute-start(bf16[4,2,128,128]{3,2,1,0:T(8,128)(2,1)S(1)} %get-tuple-element.73), channel_id=1, source_target_pairs={{0,5},{1,4},{2,7},{3,6},{4,1},{5,0},{6,3},{7,2},{8,13},{9,12},{10,... | collective-permute-start | bytes 786440 | tf_op jit(solution)/shard_map/ppermute | solution.py:421
  61.6 11.8 %collective-permute-start.18 = (bf16[4,2,128,128]{3,2,1,0:T(8,128)(2,1)S(1)}, bf16[4,2,128,128]{3,2,1,0:T(8,128)(2,1)S(1)}, u32[]{:S(2)}, u32[]{:S(2)}) collective-permute-start(bf16[4,2,128,128]{3,2,1,0:T(8,128)(2,1)S(1)} %get-tuple-element.74), channel_id=1, source_target_pairs={{0,6},{1,7},{2,4},{3,5},{4,2},{5,3},{6,0},{7,1},{8,14},{9,15},{10,... | collective-permute-start | bytes 786440 | tf_op jit(solution)/shard_map/ppermute | solution.py:421
  70.5 6.5 %collective-permute-start.13 = (bf16[4,2,128,128]{3,2,1,0:T(8,128)(2,1)S(1)}, bf16[4,2,128,128]{3,2,1,0:T(8,128)(2,1)S(1)}, u32[]{:S(2)}, u32[]{:S(2)}) collective-permute-start(bf16[4,2,128,128]{3,2,1,0:T(8,128)(2,1)S(1)} %get-tuple-element.65), channel_id=1, source_target_pairs={{0,4},{1,5},{2,6},{3,7},{4,0},{5,1},{6,2},{7,3},{8,12},{9,13},{10,... | collective-permute-start | bytes 786440 | tf_op jit(solution)/shard_map/ppermute | solution.py:421
  70.6 10.1 %collective-permute-start.14 = (bf16[4,2,128,128]{3,2,1,0:T(8,128)(2,1)S(1)}, bf16[4,2,128,128]{3,2,1,0:T(8,128)(2,1)S(1)}, u32[]{:S(2)}, u32[]{:S(2)}) collective-permute-start(bf16[4,2,128,128]{3,2,1,0:T(8,128)(2,1)S(1)} %get-tuple-element.67), channel_id=1, source_target_pairs={{0,3},{1,2},{2,1},{3,0},{4,7},{5,6},{6,5},{7,4},{8,11},{9,10},{10,... | collective-permute-start | bytes 786440 | tf_op jit(solution)/shard_map/ppermute | solution.py:421
  72.4 12.9 %collective-permute-start.15 = (bf16[4,2,128,128]{3,2,1,0:T(8,128)(2,1)S(1)}, bf16[4,2,128,128]{3,2,1,0:T(8,128)(2,1)S(1)}, u32[]{:S(2)}, u32[]{:S(2)}) collective-permute-start(bf16[4,2,128,128]{3,2,1,0:T(8,128)(2,1)S(1)} %get-tuple-element.68), channel_id=1, source_target_pairs={{0,7},{1,6},{2,5},{3,4},{4,3},{5,2},{6,1},{7,0},{8,15},{9,14},{10,... | collective-permute-start | bytes 786440 | tf_op jit(solution)/shard_map/ppermute | solution.py:421
  73.4 12.0 %copy-start.1 = (bf16[4,4,3,144,128]{4,3,2,1,0:T(8,128)(2,1)S(1)}, bf16[4,4,3,144,128]{4,3,2,1,0:T(8,128)(2,1)}, u32[]{:S(2)}) copy-start(bf16[4,4,3,144,128]{4,3,2,1,0:T(8,128)(2,1)} %get-tuple-element.57.refs_3_) | copy-start | bytes 5308420
  73.4 12.0 %copy-start.6 = (bf16[4,2,128,512]{3,2,1,0:T(8,128)(2,1)S(1)}, bf16[4,2,128,512]{3,2,1,0:T(8,128)(2,1)}, u32[]{:S(2)}) copy-start(bf16[4,2,128,512]{3,2,1,0:T(8,128)(2,1)} %get-tuple-element.59.refs_5_) | copy-start | bytes 3145732
  73.4 12.0 %copy-start.9 = (bf16[4,3,16,512]{3,2,1,0:T(8,128)(2,1)S(1)}, bf16[4,3,16,512]{3,2,1,0:T(8,128)(2,1)}, u32[]{:S(2)}) copy-start(bf16[4,3,16,512]{3,2,1,0:T(8,128)(2,1)} %get-tuple-element.58.refs_4_) | copy-start | bytes 589828

commit v5 on v4

--- a/solution.py
+++ b/solution.py
@@ -41,40 +41,33 @@
     return pl.CostEstimate(flops=int(flops), bytes_accessed=int(moved), transcendentals=0)
 
 
-def pack_kernel(q_ref, k_ref, v_ref, g_ref, tail_ref, lead_ref, x_ref, sems):
-    rows = q_ref.shape[0]
+def pack_kernel(start, *refs):
+    count = len(refs) - 3
+    out_ref, x_ref, sems = refs[count:]
     copies = []
-    for i, ref in enumerate((q_ref, k_ref, v_ref)):
-        copies.append((ref.at[pl.ds(rows - EDGE, EDGE)], x_ref.at[i]))
-    for i, ref in enumerate((q_ref, k_ref, v_ref, g_ref)):
-        copies.append((ref.at[pl.ds(0, EDGE)], x_ref.at[3 + i]))
-    copies = [pltpu.make_async_copy(a, b, sems.at[i]) for i, (a, b) in enumerate(copies)]
+    for i, ref in enumerate(refs[:count]):
+        first = ref.shape[0] - EDGE if start else 0
+        copy = pltpu.make_async_copy(ref.at[pl.ds(first, EDGE)], x_ref.at[i], sems.at[i])
+        copy.start()
+        copies.append(copy)
     for copy in copies:
-        copy.start()
-
-    def rows_of(first, count, start):
-        parts = [x_ref[first + i].astype(F32)[start : start + REACH] for i in range(count)]
-        fill = jnp.zeros((EDGE - REACH * count, parts[0].shape[1]), F32)
-        return jnp.concatenate(parts + [fill], 0).astype(BF16)
-
-    for copy in copies[:3]:
         copy.wait()
-    tail_ref[...] = rows_of(0, 3, EDGE - REACH)
-    for copy in copies[3:]:
-        copy.wait()
-    lead_ref[...] = rows_of(3, 4, 0)
-
-
-def pack(raws):
+    parts = [x_ref[i].astype(F32)[start : start + REACH] for i in range(count)]
+    fill = jnp.zeros((EDGE - REACH * count, parts[0].shape[1]), F32)
+    out_ref[...] = jnp.concatenate(parts + [fill], 0).astype(BF16)
+
+
+def pack(raws, start):
     width = raws[0].shape[1]
+    count = len(raws)
     return pl.pallas_call(
-        pack_kernel,
-        in_specs=[pl.BlockSpec(memory_space=pltpu.HBM)] * 4,
-        out_specs=[pl.BlockSpec(memory_space=pltpu.VMEM)] * 2,
-        out_shape=[shape((EDGE, width))] * 2,
-        scratch_shapes=[pltpu.VMEM((7, EDGE, width), BF16), pltpu.SemaphoreType.DMA((7,))],
+        functools.partial(pack_kernel, start),
+        in_specs=[pl.BlockSpec(memory_space=pltpu.HBM)] * count,
+        out_specs=pl.BlockSpec(memory_space=pltpu.VMEM),
+        out_shape=shape((EDGE, width)),
+        scratch_shapes=[pltpu.VMEM((count, EDGE, width), BF16), pltpu.SemaphoreType.DMA((count,))],
         compiler_params=params(),
-        cost_estimate=cost(0, 9 * 2 * EDGE * width),
+        cost_estimate=cost(0, 5 * 2 * EDGE * width),
         name="pack",
     )(*[far(x) for x in raws])
 
@@ -334,7 +327,7 @@
                     out[h, i, r] = total.astype(BF16)
 
 
-def grads_kernel(scale, peers, heads, alias, cols, *refs):
+def grads_kernel(scale, peers, heads, first, cols, *refs):
     tq, tk, tv, d_ref, e_ref, f_ref, g_ref = refs[:7]
     p_refs = refs[7 : 7 + peers]
     outs, (out_ref, x_ref, sems) = refs[-6:-3], refs[-3:]
@@ -347,13 +340,15 @@
             own = slice(h * HEAD, (h + 1) * HEAD)
             vk, gq = p_refs[p][h, 0], p_refs[p][h, 1]
             kx, vx, gx = [
-                jnp.concatenate([field, e_ref[p, i, :, own]], 0)
-                for i, field in enumerate((f_ref[p, 0, :, own], f_ref[p, 1, :, own], g_ref[:, c]))
+                jnp.concatenate([field, e_ref[first + p, i, :, own]], 0)
+                for i, field in enumerate(
+                    (f_ref[first + p, 0, :, own], f_ref[first + p, 1, :, own], g_ref[:, c])
+                )
             ]
             d = x_ref.at[h]
-            d[0] = d_ref[p, h, 0].astype(F32) + dot(gx, vk, 1, 0)
-            d[1] = d_ref[p, h, 1].astype(F32) + dot(vx, gq, 1, 0)
-            d[2] = d_ref[p, h, 2].astype(F32) + dot(kx, gq, 1, 1)
+            d[0] = d_ref[first + p, h, 0].astype(F32) + dot(gx, vk, 1, 0)
+            d[1] = d_ref[first + p, h, 1].astype(F32) + dot(vx, gq, 1, 0)
+            d[2] = d_ref[first + p, h, 2].astype(F32) + dot(kx, gq, 1, 1)
             for i, tap_ref in enumerate((tq, tk, tv)):
                 taps = tap_ref[:, c].astype(F32) * scale
                 total = taps[0:1] * d[i, 0:rows]
@@ -365,7 +360,7 @@
     wait(saves)
 
 
-def grads_call(peers, heads, scale, cols, g, intra, states, taps, outs):
+def grads_call(peers, heads, scale, cols, g, intra, first, states, taps, outs):
     rows, total_width = g.shape
     ext = rows + EDGE
     near = [*taps, *intra, g, *states]
@@ -375,7 +370,7 @@
         aliases = [(len(near) + i, i) for i in range(3)]
         remote = outs
     results, _ = marked_call(
-        functools.partial(grads_kernel, scale, peers, heads, outs is not None),
+        functools.partial(grads_kernel, scale, peers, heads, first),
         "grads",
         cols,
         near,
@@ -420,7 +415,7 @@
     def swap(field, axes, count, d):
         return lax.ppermute(field, axes, [(i, i ^ d) for i in range(count)]) if d else field
 
-    tail, lead = pack(raws)
+    tail, lead = pack(raws[:3], EDGE - REACH), pack(raws, 0)
     prev = lax.ppermute(tail, everyone, [(i, i + 1) for i in range(devices - 1)])
     after = lax.ppermute(lead, everyone, [(i + 1, i) for i in range(devices - 1)])
 
@@ -472,9 +467,10 @@
         mark = [mark]
         backs |= {d: swap(s, plane, members, d) for s, d in zip(sent, ds)}
     outs = None
-    for ds in (direct, others):
+    for ds, group in ((direct, direct), (near, others), (diagonal, others)):
         got = [backs[d] for d in ds]
-        outs = grads_call(len(ds), heads, scale, numbers(ds), grad_out, intra[ds[0]], got, taps, outs)
+        args = (grad_out, intra[group[0]], group.index(ds[0]), got, taps, outs)
+        outs = grads_call(len(ds), heads, scale, numbers(ds), *args)
     return tuple(outs)
 
 

time: 89.5 us -> 88.3 us (0.987)
  Pallas kernels: 39.7 us -> 42.5 us
  waiting for transfers between devices: 17.8 us -> 15.5 us
  starting transfers between devices: 30.4 us -> 28.5 us
    ppermute x17, starting transfers between devices: 24.2 us -> 22.2 us  [swap(): lax.ppermute(field, axes, [(i, i ^ d) for i in range(count)])]
    pallas_call x10 -> x11, Pallas kernels: 38.3 us -> 40.2 us  [marked_call(): pl.pallas_call(body, in_specs=[SMEM] * (1 + len(behind)) + [pl.BlockSpec(...]
    ppermute x1, waiting for transfers between devices: 1.37 us -> 0.18 us  [local(): lax.ppermute(tail, everyone, [(i, i + 1) for i in range(devices - 1)])]
    ppermute x17, waiting for transfers between devices: 16.4 us -> 15.3 us  [swap(): lax.ppermute(field, axes, [(i, i ^ d) for i in range(count)])]
    pallas_call x1 -> x2, Pallas kernels: 1.37 us -> 2.29 us  [pack(): pl.pallas_call(functools.partial(pack_kernel, start), in_specs=[pl.BlockS...]
  transfers between devices with their start and end apart: 19 -> 19, of which waited for: 7 -> 8; matrix products, arithmetic and copies ran while one was open for 0% -> 0% of each run, Pallas kernels for 35% -> 40%
where the time goes in v5:
time: 88.3 us; the launch traced here: 87.8 us
  Pallas kernels  42.5 us (48%)
  starting transfers between devices  28.5 us (32%)
  waiting for transfers between devices  15.5 us (18%)
  between operations  1.13 us (1%)
    pallas_call x11, Pallas kernels, marked_call(): pl.pallas_call(body, in_specs=[SMEM] * (1 + len(behind)) + [pl.BlockSpec(...  40.2 us
    ppermute x17, starting transfers between devices, swap(): lax.ppermute(field, axes, [(i, i ^ d) for i in range(count)])  22.2 us
    ppermute x17, waiting for transfers between devices, swap(): lax.ppermute(field, axes, [(i, i ^ d) for i in range(count)])  15.3 us
    ppermute x1, starting transfers between devices, local(): lax.ppermute(tail, everyone, [(i, i + 1) for i in range(devices - 1)])  4.98 us
    pallas_call x2, Pallas kernels, pack(): pl.pallas_call(functools.partial(pack_kernel, start), in_specs=[pl.BlockS...  2.29 us
  transfers between devices with their start and end apart: 19, of which 8 were waited for; matrix products, arithmetic and copies ran while one was open for 0% of the time, Pallas kernels for 40%

profile of v5, /device:TPU:0, one launch (start us, length us, event | category | flops | bytes accessed | tf_op | source)
XLA Modules:
  0.0 87.8 jit_solution(12947624085828359444)
XLA Ops:
  0.6 1.1 %pack.2 = bf16[16,4096]{1,0:T(8,128)(2,1)S(1)} custom-call(bf16[128,4096]{1,0:T(8,128)(2,1)} %refs_6_.12, bf16[128,4096]{1,0:T(8,128)(2,1)} %refs_7_.9, bf16[128,4096]{1,0:T(8,128)(2,1)} %refs_8_.7), custom_call_target="tpu_custom_call" | custom-call | bytes 655360 | tf_op jit(solution)/shard_map/pack/pallas_call | solution.py:63
  1.7 0.0 copy-start.13
  1.8 0.0 copy-start.3
  1.8 0.0 copy-start.4
  1.8 0.0 copy-start.5
  1.8 5.0 %collective-permute-start = (bf16[16,4096]{1,0:T(8,128)(2,1)S(1)}, bf16[16,4096]{1,0:T(8,128)(2,1)S(1)}, u32[]{:S(2)}, u32[]{:S(2)}) collective-permute-start(bf16[16,4096]{1,0:T(8,128)(2,1)S(1)} %pack.2), channel_id=1, source_target_pairs={{0,1},{1,2},{2,3},{3,4},{4,5},{5,6},{6,7},{7,8},{8,9},{9,10},{10,1... | collective-permute-start | bytes 393224 | tf_op jit(solution)/shard_map/ppermute | solution.py:419
  6.8 1.2 %pack.3 = bf16[16,4096]{1,0:T(8,128)(2,1)S(1)} custom-call(bf16[128,4096]{1,0:T(8,128)(2,1)} %refs_6_.12, bf16[128,4096]{1,0:T(8,128)(2,1)} %refs_7_.9, bf16[128,4096]{1,0:T(8,128)(2,1)} %refs_8_.7, bf16[128,4096]{1,0:T(8,128)(2,1)} %refs_6_.15), custom_call_target="tpu_custom_call" | custom-call | bytes 655360 | tf_op jit(solution)/shard_map/pack/pallas_call | solution.py:63
  8.0 1.3 %collective-permute-start.1 = (bf16[16,4096]{1,0:T(8,128)(2,1)S(1)}, bf16[16,4096]{1,0:T(8,128)(2,1)S(1)}, u32[]{:S(2)}, u32[]{:S(2)}) collective-permute-start(bf16[16,4096]{1,0:T(8,128)(2,1)S(1)} %pack.3), channel_id=1, source_target_pairs={{1,0},{2,1},{3,2},{4,3},{5,4},{6,5},{7,6},{8,7},{9,8},{10,9},{11,1... | collective-permute-start | bytes 393224 | tf_op jit(solution)/shard_map/ppermute | solution.py:420
  9.3 0.0 copy-start.12
  9.3 0.0 copy-start.11
  9.3 0.2 collective-permute-done.refs_0_.refs_2_.refs_1_
  9.5 3.6 %states.3 = (bf16[4,2,128,128]{3,2,1,0:T(8,128)(2,1)S(1)}, bf16[4,2,128,128]{3,2,1,0:T(8,128)(2,1)S(1)}, bf16[4,2,128,128]{3,2,1,0:T(8,128)(2,1)S(1)}, bf16[4,2,128,128]{3,2,1,0:T(8,128)(2,1)S(1)}, s32[1]{0:T(128)}) custom-call(s32[4]{0:T(128)S(1)} %broadcast_xor_fusion.cols, bf16[16,4096]{1,0:T(8,128)(2,1)S(1)} %collective-permute-done.refs_0_.refs_2_.refs_1_, ...), custom_call_target="tpu_custom_call" | custom-call | flops 134217728 | bytes 5472256 | tf_op jit(solution)/shard_map/states/pallas_call | solution.py:115
  13.2 2.6 %collective-permute-start.2 = (bf16[4,2,128,128]{3,2,1,0:T(8,128)(2,1)S(1)}, bf16[4,2,128,128]{3,2,1,0:T(8,128)(2,1)S(1)}, u32[]{:S(2)}, u32[]{:S(2)}) collective-permute-start(bf16[4,2,128,128]{3,2,1,0:T(8,128)(2,1)S(1)} %get-tuple-element.45), channel_id=1, source_target_pairs={{0,1},{1,0},{2,3},{3,2},{4,5},{5,4},{6,7},{7,6},{8,9},{9,8},{10,11... | collective-permute-start | bytes 786440 | tf_op jit(solution)/shard_map/ppermute | solution.py:416
  15.7 1.5 %collective-permute-start.3 = (bf16[4,2,128,128]{3,2,1,0:T(8,128)(2,1)S(1)}, bf16[4,2,128,128]{3,2,1,0:T(8,128)(2,1)S(1)}, u32[]{:S(2)}, u32[]{:S(2)}) collective-permute-start(bf16[4,2,128,128]{3,2,1,0:T(8,128)(2,1)S(1)} %get-tuple-element.48), channel_id=1, source_target_pairs={{0,2},{1,3},{2,0},{3,1},{4,6},{5,7},{6,4},{7,5},{8,10},{9,11},{10,... | collective-permute-start | bytes 786440 | tf_op jit(solution)/shard_map/ppermute | solution.py:416
  17.3 0.1 collective-permute-start.4
  17.3 1.2 %collective-permute-start.5 = (bf16[4,2,128,128]{3,2,1,0:T(8,128)(2,1)S(1)}, bf16[4,2,128,128]{3,2,1,0:T(8,128)(2,1)S(1)}, u32[]{:S(2)}, u32[]{:S(2)}) collective-permute-start(bf16[4,2,128,128]{3,2,1,0:T(8,128)(2,1)S(1)} %get-tuple-element.50), channel_id=1, source_target_pairs={{0,6},{1,7},{2,4},{3,5},{4,2},{5,3},{6,0},{7,1},{8,14},{9,15},{10,... | collective-permute-start | bytes 786440 | tf_op jit(solution)/shard_map/ppermute | solution.py:416
  18.5 3.3 %states.4 = (bf16[4,2,128,128]{3,2,1,0:T(8,128)(2,1)S(1)}, bf16[4,2,128,128]{3,2,1,0:T(8,128)(2,1)S(1)}, s32[1]{0:T(128)}) custom-call(s32[2]{0:T(128)S(1)} %broadcast_xor_fusion.3.cols, s32[1]{0:T(128)} %get-tuple-element.43.refs_0_, bf16[16,4096]{1,0:T(8,128)(2,1)S(1)} %collective-permute-done.1.refs_1_.refs_2_, ...), custom_call_target="tpu_custom_call" | custom-call | flops 67108864 | bytes 4947968 | tf_op jit(solution)/shard_map/states/pallas_call | solution.py:115
  21.9 2.1 %collective-permute-start.6 = (bf16[4,2,128,128]{3,2,1,0:T(8,128)(2,1)S(1)}, bf16[4,2,128,128]{3,2,1,0:T(8,128)(2,1)S(1)}, u32[]{:S(2)}, u32[]{:S(2)}) collective-permute-start(bf16[4,2,128,128]{3,2,1,0:T(8,128)(2,1)S(1)} %get-tuple-element.51), channel_id=1, source_target_pairs={{0,3},{1,2},{2,1},{3,0},{4,7},{5,6},{6,5},{7,4},{8,11},{9,10},{10,... | collective-permute-start | bytes 786440 | tf_op jit(solution)/shard_map/ppermute | solution.py:416
  24.0 0.6 collective-permute-start.7
  24.6 3.5 %states.5 = (bf16[4,2,128,128]{3,2,1,0:T(8,128)(2,1)}, bf16[4,2,128,128]{3,2,1,0:T(8,128)(2,1)S(1)}, s32[1]{0:T(128)}) custom-call(s32[2]{0:T(128)S(1)} %broadcast_xor_fusion.2.cols, s32[1]{0:T(128)} %get-tuple-element.44.refs_0_, bf16[4,2,128,128]{3,2,1,0:T(8,128)(2,1)S(1)} %collective-permute-done.2.refs_1_.refs_2_, ...), custom_call_target="tpu_custom_call" | custom-call | flops 67108864 | bytes 4947968 | tf_op jit(solution)/shard_map/states/pallas_call | solution.py:115
  28.1 1.5 %collective-permute-start.8 = (bf16[4,2,128,128]{3,2,1,0:T(8,128)(2,1)}, bf16[4,2,128,128]{3,2,1,0:T(8,128)(2,1)S(1)}, u32[]{:S(2)}, u32[]{:S(2)}) collective-permute-start(bf16[4,2,128,128]{3,2,1,0:T(8,128)(2,1)} %get-tuple-element.53), channel_id=1, source_target_pairs={{0,4},{1,5},{2,6},{3,7},{4,0},{5,1},{6,2},{7,3},{8,12},{9,13},{10,... | collective-permute-start | bytes 786440 | tf_op jit(solution)/shard_map/ppermute | solution.py:416
  29.7 0.1 pad_add_fusion.cols
  29.7 7.3 %intra.2 = (bf16[4,4,3,144,128]{4,3,2,1,0:T(8,128)(2,1)}, bf16[4,3,16,512]{3,2,1,0:T(8,128)(2,1)}, bf16[4,2,128,512]{3,2,1,0:T(8,128)(2,1)}, s32[1]{0:T(128)}) custom-call(s32[4]{0:T(128)S(1)} %broadcast_xor_fusion.cols, s32[1]{0:T(128)} %get-tuple-element.46.refs_0_, bf16[16,4096]{1,0:T(8,128)(2,1)S(1)} %collective-permute-done.refs_0_.refs_2_.refs_1_, ...), custom_call_target="tpu_custom_call" | custom-call | flops 402653184 | bytes 7569408 | tf_op jit(solution)/shard_map/intra/pallas_call | solution.py:115
  37.1 0.0 copy-start.10
  37.1 2.1 %collective-permute-done.5.refs_4_.refs_5_ = bf16[4,2,128,128]{3,2,1,0:T(8,128)(2,1)S(1)} collective-permute-done((bf16[4,2,128,128]{3,2,1,0:T(8,128)(2,1)S(1)}, bf16[4,2,128,128]{3,2,1,0:T(8,128)(2,1)S(1)}, u32[]{:S(2)}, u32[]{:S(2)}) %collective-permute-start.5) | collective-permute-done | bytes 262176 | tf_op jit(solution)/shard_map/ppermute | solution.py:416
  39.2 1.7 %sums.1 = (bf16[4,128,128]{2,1,0:T(8,128)(2,1)S(1)}, bf16[4,128,128]{2,1,0:T(8,128)(2,1)S(1)}, s32[1]{0:T(128)}) custom-call(s32[2]{0:T(128)S(1)} %pad_add_fusion.cols, s32[1]{0:T(128)} %get-tuple-element.47.refs_0_, bf16[4,2,128,128]{3,2,1,0:T(8,128)(2,1)S(1)} %collective-permute-done.2.refs_1_.refs_2_, ...), custom_call_target="tpu_custom_call" | custom-call | bytes 2359296 | tf_op jit(solution)/shard_map/sums/pallas_call | solution.py:115
  40.9 3.3 %collective-permute-start.11 = (bf16[4,128,128]{2,1,0:T(8,128)(2,1)S(1)}, bf16[4,128,128]{2,1,0:T(8,128)(2,1)S(1)}, u32[]{:S(2)}, u32[]{:S(2)}) collective-permute-start(bf16[4,128,128]{2,1,0:T(8,128)(2,1)S(1)} %get-tuple-element.61), channel_id=1, source_target_pairs={{0,24},{8,16},{16,8},{24,0},{1,25},{9,17},{17,9},{25,1},{2,26},{10... | collective-permute-start | bytes 393224 | tf_op jit(solution)/shard_map/ppermute | solution.py:416
  44.1 1.2 %collective-permute-start.9 = (bf16[4,128,128]{2,1,0:T(8,128)(2,1)S(1)}, bf16[4,128,128]{2,1,0:T(8,128)(2,1)S(1)}, u32[]{:S(2)}, u32[]{:S(2)}) collective-permute-start(bf16[4,128,128]{2,1,0:T(8,128)(2,1)S(1)} %get-tuple-element.60), channel_id=1, source_target_pairs={{0,8},{8,0},{16,24},{24,16},{1,9},{9,1},{17,25},{25,17},{2,10},{10... | collective-permute-start | bytes 393224 | tf_op jit(solution)/shard_map/ppermute | solution.py:416
  45.4 7.3 %intra.3 = (bf16[4,4,3,144,128]{4,3,2,1,0:T(8,128)(2,1)}, bf16[4,3,16,512]{3,2,1,0:T(8,128)(2,1)}, bf16[4,2,128,512]{3,2,1,0:T(8,128)(2,1)}, s32[1]{0:T(128)}) custom-call(s32[4]{0:T(128)S(1)} %broadcast_xor_fusion.1.cols, s32[1]{0:T(128)} %get-tuple-element.55.refs_0_, bf16[16,4096]{1,0:T(8,128)(2,1)S(1)} %collective-permute-done.refs_0_.refs_2_.refs_1_, ...), custom_call_target="tpu_custom_call" | custom-call | flops 402653184 | bytes 7569408 | tf_op jit(solution)/shard_map/intra/pallas_call | solution.py:115
  52.7 0.2 collective-permute-done.9.refs_9_.refs_10_
  52.9 2.6 %collective-permute-done.10.refs_10_.refs_11_ = bf16[4,128,128]{2,1,0:T(8,128)(2,1)S(1)} collective-permute-done((bf16[4,128,128]{2,1,0:T(8,128)(2,1)S(1)}, bf16[4,128,128]{2,1,0:T(8,128)(2,1)S(1)}, u32[]{:S(2)}, u32[]{:S(2)}) %collective-permute-start.10) | collective-permute-done | bytes 131104 | tf_op jit(solution)/shard_map/ppermute | solution.py:416
  55.5 2.0 %members.2 = (bf16[4,2,128,128]{3,2,1,0:T(8,128)(2,1)S(1)}, bf16[4,2,128,128]{3,2,1,0:T(8,128)(2,1)S(1)}, bf16[4,2,128,128]{3,2,1,0:T(8,128)(2,1)S(1)}, bf16[4,2,128,128]{3,2,1,0:T(8,128)(2,1)S(1)}, s32[1]{0:T(128)}) custom-call(s32[2]{0:T(128)S(1)} %pad_add_fusion.cols, s32[1]{0:T(128)} %get-tuple-element.59.refs_0_, ...), custom_call_target="tpu_custom_call" | custom-call | bytes 3538944 | tf_op jit(solution)/shard_map/members/pallas_call | solution.py:115
  57.6 0.0 copy-start
  57.6 1.6 %collective-permute-start.12 = (bf16[4,2,128,128]{3,2,1,0:T(8,128)(2,1)S(1)}, bf16[4,2,128,128]{3,2,1,0:T(8,128)(2,1)S(1)}, u32[]{:S(2)}, u32[]{:S(2)}) collective-permute-start(bf16[4,2,128,128]{3,2,1,0:T(8,128)(2,1)S(1)} %get-tuple-element.63), channel_id=1, source_target_pairs={{0,1},{1,0},{2,3},{3,2},{4,5},{5,4},{6,7},{7,6},{8,9},{9,8},{10,11... | collective-permute-start | bytes 786440 | tf_op jit(solution)/shard_map/ppermute | solution.py:416
  59.2 2.1 %collective-permute-start.16 = (bf16[4,2,128,128]{3,2,1,0:T(8,128)(2,1)S(1)}, bf16[4,2,128,128]{3,2,1,0:T(8,128)(2,1)S(1)}, u32[]{:S(2)}, u32[]{:S(2)}) collective-permute-start(bf16[4,2,128,128]{3,2,1,0:T(8,128)(2,1)S(1)} %get-tuple-element.71), channel_id=1, source_target_pairs={{0,2},{1,3},{2,0},{3,1},{4,6},{5,7},{6,4},{7,5},{8,10},{9,11},{10,... | collective-permute-start | bytes 786440 | tf_op jit(solution)/shard_map/ppermute | solution.py:416
  61.3 0.5 collective-permute-start.17
  61.9 0.6 collective-permute-start.18
  62.5 4.4 %collective-permute-done.12.refs_1_.refs_7_ = bf16[4,2,128,128]{3,2,1,0:T(8,128)(2,1)S(1)} collective-permute-done((bf16[4,2,128,128]{3,2,1,0:T(8,128)(2,1)S(1)}, bf16[4,2,128,128]{3,2,1,0:T(8,128)(2,1)S(1)}, u32[]{:S(2)}, u32[]{:S(2)}) %collective-permute-start.12) | collective-permute-done | bytes 262176 | tf_op jit(solution)/shard_map/ppermute | solution.py:416
  66.9 2.2 %members.3 = (bf16[4,2,128,128]{3,2,1,0:T(8,128)(2,1)S(1)}, bf16[4,2,128,128]{3,2,1,0:T(8,128)(2,1)S(1)}, bf16[4,2,128,128]{3,2,1,0:T(8,128)(2,1)S(1)}, bf16[4,2,128,128]{3,2,1,0:T(8,128)(2,1)S(1)}, s32[1]{0:T(128)}) custom-call(s32[2]{0:T(128)S(1)} %pad_add_fusion.cols, s32[1]{0:T(128)} %get-tuple-element.62.refs_0_, ...), custom_call_target="tpu_custom_call" | custom-call | bytes 3538944 | tf_op jit(solution)/shard_map/members/pallas_call | solution.py:115
  69.1 0.1 collective-permute-start.15
  69.1 3.2 %collective-permute-start.13 = (bf16[4,2,128,128]{3,2,1,0:T(8,128)(2,1)S(1)}, bf16[4,2,128,128]{3,2,1,0:T(8,128)(2,1)S(1)}, u32[]{:S(2)}, u32[]{:S(2)}) collective-permute-start(bf16[4,2,128,128]{3,2,1,0:T(8,128)(2,1)S(1)} %get-tuple-element.64), channel_id=1, source_target_pairs={{0,3},{1,2},{2,1},{3,0},{4,7},{5,6},{6,5},{7,4},{8,11},{9,10},{10,... | collective-permute-start | bytes 786440 | tf_op jit(solution)/shard_map/ppermute | solution.py:416
  72.3 0.1 collective-permute-start.14
  72.4 0.3 collective-permute-done.18.refs_10_
  72.8 3.6 %grads.3 = (bf16[128,4096]{1,0:T(8,128)(2,1)}, bf16[128,4096]{1,0:T(8,128)(2,1)}, bf16[128,4096]{1,0:T(8,128)(2,1)}, s32[1]{0:T(128)}) custom-call(s32[4]{0:T(128)S(1)} %broadcast_xor_fusion.cols, bf16[4,4096]{1,0:T(4,128)(2,1)S(1)} %copy-done.3, bf16[4,4096]{1,0:T(4,128)(2,1)S(1)} %copy-done.4, bf16[4,4096]{1,0:T(4,128)(2,1)S(1)} %copy-done.5, ...), custom_call_target="tpu_custom_call" | custom-call | flops 226492416 | bytes 8355840 | tf_op jit(solution)/shard_map/grads/pallas_call | solution.py:115
  76.5 2.8 %grads.4 = (bf16[128,4096]{1,0:T(8,128)(2,1)}, bf16[128,4096]{1,0:T(8,128)(2,1)}, bf16[128,4096]{1,0:T(8,128)(2,1)}, s32[1]{0:T(128)}) custom-call(s32[2]{0:T(128)S(1)} %broadcast_xor_fusion.2.cols, bf16[4,4096]{1,0:T(4,128)(2,1)S(1)} %copy-done.3, bf16[4,4096]{1,0:T(4,128)(2,1)S(1)} %copy-done.4, ...), custom_call_target="tpu_custom_call", output_to_operand_aliasing={{0}: (10, {}), {1}: (11, {}), {2}: (12, {})} | custom-call | flops 113246208 | bytes 10977280 | tf_op jit(solution)/shard_map/grads/pallas_call | solution.py:115
  79.2 0.9 collective-permute-done.13.refs_7_
  80.1 4.8 %collective-permute-done.14.refs_8_ = bf16[4,2,128,128]{3,2,1,0:T(8,128)(2,1)S(1)} collective-permute-done((bf16[4,2,128,128]{3,2,1,0:T(8,128)(2,1)S(1)}, bf16[4,2,128,128]{3,2,1,0:T(8,128)(2,1)S(1)}, u32[]{:S(2)}, u32[]{:S(2)}) %collective-permute-start.14) | collective-permute-done | bytes 262176 | tf_op jit(solution)/shard_map/ppermute | solution.py:416
  84.9 2.7 %grads.5 = (bf16[128,4096]{1,0:T(8,128)(2,1)}, bf16[128,4096]{1,0:T(8,128)(2,1)}, bf16[128,4096]{1,0:T(8,128)(2,1)}, s32[1]{0:T(128)}) custom-call(s32[2]{0:T(128)S(1)} %broadcast_xor_fusion.3.cols, bf16[4,4096]{1,0:T(4,128)(2,1)S(1)} %copy-done.3, bf16[4,4096]{1,0:T(4,128)(2,1)S(1)} %copy-done.4, ...), custom_call_target="tpu_custom_call", output_to_operand_aliasing={{0}: (10, {}), {1}: (11, {}), {2}: (12, {})} | custom-call | flops 113246208 | bytes 10977280 | tf_op jit(solution)/shard_map/grads/pallas_call | solution.py:115
  (36 shorter events, 0.1 us)
Async XLA Ops:
  1.7 7.5 %copy-start.13 = (s32[4]{0:T(128)S(1)}, s32[4]{0:T(128)}, u32[]{:S(2)}) copy-start(s32[4]{0:T(128)} %constant.24.clone) | copy-start | bytes 52
  1.8 7.8 %copy-start.3 = (bf16[4,4096]{1,0:T(4,128)(2,1)S(1)}, bf16[4,4096]{1,0:T(4,128)(2,1)}, u32[]{:S(2)}) copy-start(bf16[4,4096]{1,0:T(4,128)(2,1)} %refs_0_.9) | copy-start | bytes 98308
  1.8 7.7 %copy-start.4 = (bf16[4,4096]{1,0:T(4,128)(2,1)S(1)}, bf16[4,4096]{1,0:T(4,128)(2,1)}, u32[]{:S(2)}) copy-start(bf16[4,4096]{1,0:T(4,128)(2,1)} %refs_1_.11) | copy-start | bytes 98308
  1.8 7.7 %copy-start.5 = (bf16[4,4096]{1,0:T(4,128)(2,1)S(1)}, bf16[4,4096]{1,0:T(4,128)(2,1)}, u32[]{:S(2)}) copy-start(bf16[4,4096]{1,0:T(4,128)(2,1)} %refs_2_.11) | copy-start | bytes 98308
  1.8 7.7 %collective-permute-start = (bf16[16,4096]{1,0:T(8,128)(2,1)S(1)}, bf16[16,4096]{1,0:T(8,128)(2,1)S(1)}, u32[]{:S(2)}, u32[]{:S(2)}) collective-permute-start(bf16[16,4096]{1,0:T(8,128)(2,1)S(1)} %pack.2), channel_id=1, source_target_pairs={{0,1},{1,2},{2,3},{3,4},{4,5},{5,6},{6,7},{7,8},{8,9},{9,10},{10,1... | collective-permute-start | bytes 393224 | tf_op jit(solution)/shard_map/ppermute | solution.py:419
  8.0 10.5 %collective-permute-start.1 = (bf16[16,4096]{1,0:T(8,128)(2,1)S(1)}, bf16[16,4096]{1,0:T(8,128)(2,1)S(1)}, u32[]{:S(2)}, u32[]{:S(2)}) collective-permute-start(bf16[16,4096]{1,0:T(8,128)(2,1)S(1)} %pack.3), channel_id=1, source_target_pairs={{1,0},{2,1},{3,2},{4,3},{5,4},{6,5},{7,6},{8,7},{9,8},{10,9},{11,1... | collective-permute-start | bytes 393224 | tf_op jit(solution)/shard_map/ppermute | solution.py:420
  9.3 8.0 %copy-start.12 = (s32[2]{0:T(128)S(1)}, s32[2]{0:T(128)}, u32[]{:S(2)}) copy-start(s32[2]{0:T(128)} %constant.25.clone) | copy-start | bytes 28
  9.3 7.9 %copy-start.11 = (s32[2]{0:T(128)S(1)}, s32[2]{0:T(128)}, u32[]{:S(2)}) copy-start(s32[2]{0:T(128)} %constant.26.clone) | copy-start | bytes 28
  13.2 10.8 %collective-permute-start.2 = (bf16[4,2,128,128]{3,2,1,0:T(8,128)(2,1)S(1)}, bf16[4,2,128,128]{3,2,1,0:T(8,128)(2,1)S(1)}, u32[]{:S(2)}, u32[]{:S(2)}) collective-permute-start(bf16[4,2,128,128]{3,2,1,0:T(8,128)(2,1)S(1)} %get-tuple-element.45), channel_id=1, source_target_pairs={{0,1},{1,0},{2,3},{3,2},{4,5},{5,4},{6,7},{7,6},{8,9},{9,8},{10,11... | collective-permute-start | bytes 786440 | tf_op jit(solution)/shard_map/ppermute | solution.py:416
  15.7 12.4 %collective-permute-start.3 = (bf16[4,2,128,128]{3,2,1,0:T(8,128)(2,1)S(1)}, bf16[4,2,128,128]{3,2,1,0:T(8,128)(2,1)S(1)}, u32[]{:S(2)}, u32[]{:S(2)}) collective-permute-start(bf16[4,2,128,128]{3,2,1,0:T(8,128)(2,1)S(1)} %get-tuple-element.48), channel_id=1, source_target_pairs={{0,2},{1,3},{2,0},{3,1},{4,6},{5,7},{6,4},{7,5},{8,10},{9,11},{10,... | collective-permute-start | bytes 786440 | tf_op jit(solution)/shard_map/ppermute | solution.py:416
  17.3 19.8 %collective-permute-start.4 = (bf16[4,2,128,128]{3,2,1,0:T(8,128)(2,1)S(1)}, bf16[4,2,128,128]{3,2,1,0:T(8,128)(2,1)S(1)}, u32[]{:S(2)}, u32[]{:S(2)}) collective-permute-start(bf16[4,2,128,128]{3,2,1,0:T(8,128)(2,1)S(1)} %get-tuple-element.49), channel_id=1, source_target_pairs={{0,5},{1,4},{2,7},{3,6},{4,1},{5,0},{6,3},{7,2},{8,13},{9,12},{10,... | collective-permute-start | bytes 786440 | tf_op jit(solution)/shard_map/ppermute | solution.py:416
  17.3 21.8 %collective-permute-start.5 = (bf16[4,2,128,128]{3,2,1,0:T(8,128)(2,1)S(1)}, bf16[4,2,128,128]{3,2,1,0:T(8,128)(2,1)S(1)}, u32[]{:S(2)}, u32[]{:S(2)}) collective-permute-start(bf16[4,2,128,128]{3,2,1,0:T(8,128)(2,1)S(1)} %get-tuple-element.50), channel_id=1, source_target_pairs={{0,6},{1,7},{2,4},{3,5},{4,2},{5,3},{6,0},{7,1},{8,14},{9,15},{10,... | collective-permute-start | bytes 786440 | tf_op jit(solution)/shard_map/ppermute | solution.py:416
  21.9 17.3 %collective-permute-start.6 = (bf16[4,2,128,128]{3,2,1,0:T(8,128)(2,1)S(1)}, bf16[4,2,128,128]{3,2,1,0:T(8,128)(2,1)S(1)}, u32[]{:S(2)}, u32[]{:S(2)}) collective-permute-start(bf16[4,2,128,128]{3,2,1,0:T(8,128)(2,1)S(1)} %get-tuple-element.51), channel_id=1, source_target_pairs={{0,3},{1,2},{2,1},{3,0},{4,7},{5,6},{6,5},{7,4},{8,11},{9,10},{10,... | collective-permute-start | bytes 786440 | tf_op jit(solution)/shard_map/ppermute | solution.py:416
  24.0 15.2 %collective-permute-start.7 = (bf16[4,2,128,128]{3,2,1,0:T(8,128)(2,1)S(1)}, bf16[4,2,128,128]{3,2,1,0:T(8,128)(2,1)S(1)}, u32[]{:S(2)}, u32[]{:S(2)}) collective-permute-start(bf16[4,2,128,128]{3,2,1,0:T(8,128)(2,1)S(1)} %get-tuple-element.52), channel_id=1, source_target_pairs={{0,7},{1,6},{2,5},{3,4},{4,3},{5,2},{6,1},{7,0},{8,15},{9,14},{10,... | collective-permute-start | bytes 786440 | tf_op jit(solution)/shard_map/ppermute | solution.py:416
  28.1 11.1 %collective-permute-start.8 = (bf16[4,2,128,128]{3,2,1,0:T(8,128)(2,1)}, bf16[4,2,128,128]{3,2,1,0:T(8,128)(2,1)S(1)}, u32[]{:S(2)}, u32[]{:S(2)}) collective-permute-start(bf16[4,2,128,128]{3,2,1,0:T(8,128)(2,1)} %get-tuple-element.53), channel_id=1, source_target_pairs={{0,4},{1,5},{2,6},{3,7},{4,0},{5,1},{6,2},{7,3},{8,12},{9,13},{10,... | collective-permute-start | bytes 786440 | tf_op jit(solution)/shard_map/ppermute | solution.py:416
  37.1 8.3 %copy-start.10 = (s32[4]{0:T(128)S(1)}, s32[4]{0:T(128)}, u32[]{:S(2)}) copy-start(s32[4]{0:T(128)} %constant.27.clone) | copy-start | bytes 52
  40.9 12.0 %collective-permute-start.11 = (bf16[4,128,128]{2,1,0:T(8,128)(2,1)S(1)}, bf16[4,128,128]{2,1,0:T(8,128)(2,1)S(1)}, u32[]{:S(2)}, u32[]{:S(2)}) collective-permute-start(bf16[4,128,128]{2,1,0:T(8,128)(2,1)S(1)} %get-tuple-element.61), channel_id=1, source_target_pairs={{0,24},{8,16},{16,8},{24,0},{1,25},{9,17},{17,9},{25,1},{2,26},{10... | collective-permute-start | bytes 393224 | tf_op jit(solution)/shard_map/ppermute | solution.py:416
  44.1 11.4 %collective-permute-start.10 = (bf16[4,128,128]{2,1,0:T(8,128)(2,1)S(1)}, bf16[4,128,128]{2,1,0:T(8,128)(2,1)S(1)}, u32[]{:S(2)}, u32[]{:S(2)}) collective-permute-start(bf16[4,128,128]{2,1,0:T(8,128)(2,1)S(1)} %get-tuple-element.61), channel_id=1, source_target_pairs={{0,16},{8,24},{16,0},{24,8},{1,17},{9,25},{17,1},{25,9},{2,18},{10... | collective-permute-start | bytes 393224 | tf_op jit(solution)/shard_map/ppermute | solution.py:416
  44.1 8.7 %collective-permute-start.9 = (bf16[4,128,128]{2,1,0:T(8,128)(2,1)S(1)}, bf16[4,128,128]{2,1,0:T(8,128)(2,1)S(1)}, u32[]{:S(2)}, u32[]{:S(2)}) collective-permute-start(bf16[4,128,128]{2,1,0:T(8,128)(2,1)S(1)} %get-tuple-element.60), channel_id=1, source_target_pairs={{0,8},{8,0},{16,24},{24,16},{1,9},{9,1},{17,25},{25,17},{2,10},{10... | collective-permute-start | bytes 393224 | tf_op jit(solution)/shard_map/ppermute | solution.py:416
  55.5 17.2 %copy-start.6 = (bf16[4,4,3,144,128]{4,3,2,1,0:T(8,128)(2,1)S(1)}, bf16[4,4,3,144,128]{4,3,2,1,0:T(8,128)(2,1)}, u32[]{:S(2)}) copy-start(bf16[4,4,3,144,128]{4,3,2,1,0:T(8,128)(2,1)} %get-tuple-element.68.refs_3_) | copy-start | bytes 5308420
  57.6 15.2 %copy-start = (bf16[128,4096]{1,0:T(8,128)(2,1)S(1)}, bf16[128,4096]{1,0:T(8,128)(2,1)}, u32[]{:S(2)}) copy-start(bf16[128,4096]{1,0:T(8,128)(2,1)} %refs_6_.15) | copy-start | bytes 3145732
  57.6 15.2 %copy-start.7 = (bf16[4,2,128,512]{3,2,1,0:T(8,128)(2,1)S(1)}, bf16[4,2,128,512]{3,2,1,0:T(8,128)(2,1)}, u32[]{:S(2)}) copy-start(bf16[4,2,128,512]{3,2,1,0:T(8,128)(2,1)} %get-tuple-element.70.refs_5_) | copy-start | bytes 3145732
  57.6 15.2 %copy-start.9 = (bf16[4,3,16,512]{3,2,1,0:T(8,128)(2,1)S(1)}, bf16[4,3,16,512]{3,2,1,0:T(8,128)(2,1)}, u32[]{:S(2)}) copy-start(bf16[4,3,16,512]{3,2,1,0:T(8,128)(2,1)} %get-tuple-element.69.refs_4_) | copy-start | bytes 589828
  57.6 9.2 %collective-permute-start.12 = (bf16[4,2,128,128]{3,2,1,0:T(8,128)(2,1)S(1)}, bf16[4,2,128,128]{3,2,1,0:T(8,128)(2,1)S(1)}, u32[]{:S(2)}, u32[]{:S(2)}) collective-permute-start(bf16[4,2,128,128]{3,2,1,0:T(8,128)(2,1)S(1)} %get-tuple-element.63), channel_id=1, source_target_pairs={{0,1},{1,0},{2,3},{3,2},{4,5},{5,4},{6,7},{7,6},{8,9},{9,8},{10,11... | collective-permute-start | bytes 786440 | tf_op jit(solution)/shard_map/ppermute | solution.py:416
  59.2 13.1 %collective-permute-start.16 = (bf16[4,2,128,128]{3,2,1,0:T(8,128)(2,1)S(1)}, bf16[4,2,128,128]{3,2,1,0:T(8,128)(2,1)S(1)}, u32[]{:S(2)}, u32[]{:S(2)}) collective-permute-start(bf16[4,2,128,128]{3,2,1,0:T(8,128)(2,1)S(1)} %get-tuple-element.71), channel_id=1, source_target_pairs={{0,2},{1,3},{2,0},{3,1},{4,6},{5,7},{6,4},{7,5},{8,10},{9,11},{10,... | collective-permute-start | bytes 786440 | tf_op jit(solution)/shard_map/ppermute | solution.py:416
  61.3 11.1 %collective-permute-start.17 = (bf16[4,2,128,128]{3,2,1,0:T(8,128)(2,1)S(1)}, bf16[4,2,128,128]{3,2,1,0:T(8,128)(2,1)S(1)}, u32[]{:S(2)}, u32[]{:S(2)}) collective-permute-start(bf16[4,2,128,128]{3,2,1,0:T(8,128)(2,1)S(1)} %get-tuple-element.72), channel_id=1, source_target_pairs={{0,5},{1,4},{2,7},{3,6},{4,1},{5,0},{6,3},{7,2},{8,13},{9,12},{10,... | collective-permute-start | bytes 786440 | tf_op jit(solution)/shard_map/ppermute | solution.py:416
  61.9 10.9 %collective-permute-start.18 = (bf16[4,2,128,128]{3,2,1,0:T(8,128)(2,1)S(1)}, bf16[4,2,128,128]{3,2,1,0:T(8,128)(2,1)S(1)}, u32[]{:S(2)}, u32[]{:S(2)}) collective-permute-start(bf16[4,2,128,128]{3,2,1,0:T(8,128)(2,1)S(1)} %get-tuple-element.73), channel_id=1, source_target_pairs={{0,6},{1,7},{2,4},{3,5},{4,2},{5,3},{6,0},{7,1},{8,14},{9,15},{10,... | collective-permute-start | bytes 786440 | tf_op jit(solution)/shard_map/ppermute | solution.py:416
  69.1 7.3 %collective-permute-start.15 = (bf16[4,2,128,128]{3,2,1,0:T(8,128)(2,1)S(1)}, bf16[4,2,128,128]{3,2,1,0:T(8,128)(2,1)S(1)}, u32[]{:S(2)}, u32[]{:S(2)}) collective-permute-start(bf16[4,2,128,128]{3,2,1,0:T(8,128)(2,1)S(1)} %get-tuple-element.66), channel_id=1, source_target_pairs={{0,4},{1,5},{2,6},{3,7},{4,0},{5,1},{6,2},{7,3},{8,12},{9,13},{10,... | collective-permute-start | bytes 786440 | tf_op jit(solution)/shard_map/ppermute | solution.py:416
  69.1 10.9 %collective-permute-start.13 = (bf16[4,2,128,128]{3,2,1,0:T(8,128)(2,1)S(1)}, bf16[4,2,128,128]{3,2,1,0:T(8,128)(2,1)S(1)}, u32[]{:S(2)}, u32[]{:S(2)}) collective-permute-start(bf16[4,2,128,128]{3,2,1,0:T(8,128)(2,1)S(1)} %get-tuple-element.64), channel_id=1, source_target_pairs={{0,3},{1,2},{2,1},{3,0},{4,7},{5,6},{6,5},{7,4},{8,11},{9,10},{10,... | collective-permute-start | bytes 786440 | tf_op jit(solution)/shard_map/ppermute | solution.py:416
  72.3 12.6 %collective-permute-start.14 = (bf16[4,2,128,128]{3,2,1,0:T(8,128)(2,1)S(1)}, bf16[4,2,128,128]{3,2,1,0:T(8,128)(2,1)S(1)}, u32[]{:S(2)}, u32[]{:S(2)}) collective-permute-start(bf16[4,2,128,128]{3,2,1,0:T(8,128)(2,1)S(1)} %get-tuple-element.65), channel_id=1, source_target_pairs={{0,7},{1,6},{2,5},{3,4},{4,3},{5,2},{6,1},{7,0},{8,15},{9,14},{10,... | collective-permute-start | bytes 786440 | tf_op jit(solution)/shard_map/ppermute | solution.py:416
  72.8 3.7 %copy-start.1 = (bf16[4,4,3,144,128]{4,3,2,1,0:T(8,128)(2,1)S(1)}, bf16[4,4,3,144,128]{4,3,2,1,0:T(8,128)(2,1)}, u32[]{:S(2)}) copy-start(bf16[4,4,3,144,128]{4,3,2,1,0:T(8,128)(2,1)} %get-tuple-element.56.refs_3_) | copy-start | bytes 5308420
  72.8 3.7 %copy-start.2 = (bf16[4,2,128,512]{3,2,1,0:T(8,128)(2,1)S(1)}, bf16[4,2,128,512]{3,2,1,0:T(8,128)(2,1)}, u32[]{:S(2)}) copy-start(bf16[4,2,128,512]{3,2,1,0:T(8,128)(2,1)} %get-tuple-element.58.refs_5_) | copy-start | bytes 3145732
  72.8 3.7 %copy-start.8 = (bf16[4,3,16,512]{3,2,1,0:T(8,128)(2,1)S(1)}, bf16[4,3,16,512]{3,2,1,0:T(8,128)(2,1)}, u32[]{:S(2)}) copy-start(bf16[4,3,16,512]{3,2,1,0:T(8,128)(2,1)} %get-tuple-element.57.refs_4_) | copy-start | bytes 589828

commit v6 on v5

--- a/solution.py
+++ b/solution.py
@@ -331,7 +331,7 @@
     tq, tk, tv, d_ref, e_ref, f_ref, g_ref = refs[:7]
     p_refs = refs[7 : 7 + peers]
     outs, (out_ref, x_ref, sems) = refs[-6:-3], refs[-3:]
-    rows, width = out_ref.shape[2:]
+    rows = out_ref.shape[2]
     copies = Copies(sems)
     saves = []
     for p in range(peers):
@@ -355,8 +355,7 @@
                 for j in range(1, KERNEL):
                     total = total + taps[j : j + 1] * d[i, j : j + rows]
                 out_ref[p, i, :, own] = total.astype(BF16)
-        c = lanes(cols[p] * width, width)
-        saves += [copies.start(out_ref.at[p, i], outs[i].at[:, c]) for i in range(3)]
+                saves.append(copies.start(out_ref.at[p, i, :, own], outs[i].at[:, c]))
     wait(saves)
 
 
@@ -379,7 +378,7 @@
         [
             pltpu.VMEM((peers, 3, rows, heads * HEAD), BF16),
             pltpu.VMEM((heads, 3, ext, HEAD), F32),
-            pltpu.SemaphoreType.DMA((peers * 3,)),
+            pltpu.SemaphoreType.DMA((peers * heads * 3,)),
         ],
         6 * heads * peers * ext * HEAD * HEAD,
         aliases=aliases,

time: 88.3 us -> 88.3 us (level)
  no operation moved by 1% of the time
where the time goes in v6:
time: 88.3 us; the launch traced here: 87.9 us
  Pallas kernels  42.9 us (49%)
  starting transfers between devices  28.5 us (32%)
  waiting for transfers between devices  15.2 us (17%)
  between operations  1.13 us (1%)
    pallas_call x11, Pallas kernels, marked_call(): pl.pallas_call(body, in_specs=[SMEM] * (1 + len(behind)) + [pl.BlockSpec(...  40.6 us
    ppermute x17, starting transfers between devices, swap(): lax.ppermute(field, axes, [(i, i ^ d) for i in range(count)])  22.2 us
    ppermute x17, waiting for transfers between devices, swap(): lax.ppermute(field, axes, [(i, i ^ d) for i in range(count)])  15 us
    ppermute x1, starting transfers between devices, local(): lax.ppermute(tail, everyone, [(i, i + 1) for i in range(devices - 1)])  4.98 us
    pallas_call x2, Pallas kernels, pack(): pl.pallas_call(functools.partial(pack_kernel, start), in_specs=[pl.BlockS...  2.29 us
  transfers between devices with their start and end apart: 19, of which 8 were waited for; matrix products, arithmetic and copies ran while one was open for 0% of the time, Pallas kernels for 40%

profile of v6, /device:TPU:0, one launch (start us, length us, event | category | flops | bytes accessed | tf_op | source)
XLA Modules:
  0.0 87.9 jit_solution(8599999317385021499)
XLA Ops:
  0.6 1.1 %pack.2 = bf16[16,4096]{1,0:T(8,128)(2,1)S(1)} custom-call(bf16[128,4096]{1,0:T(8,128)(2,1)} %refs_6_.12, bf16[128,4096]{1,0:T(8,128)(2,1)} %refs_7_.9, bf16[128,4096]{1,0:T(8,128)(2,1)} %refs_8_.7), custom_call_target="tpu_custom_call" | custom-call | bytes 655360 | tf_op jit(solution)/shard_map/pack/pallas_call | solution.py:63
  1.7 0.0 copy-start.13
  1.8 0.0 copy-start.3
  1.8 0.0 copy-start.4
  1.8 0.0 copy-start.5
  1.8 5.0 %collective-permute-start = (bf16[16,4096]{1,0:T(8,128)(2,1)S(1)}, bf16[16,4096]{1,0:T(8,128)(2,1)S(1)}, u32[]{:S(2)}, u32[]{:S(2)}) collective-permute-start(bf16[16,4096]{1,0:T(8,128)(2,1)S(1)} %pack.2), channel_id=1, source_target_pairs={{0,1},{1,2},{2,3},{3,4},{4,5},{5,6},{6,7},{7,8},{8,9},{9,10},{10,1... | collective-permute-start | bytes 393224 | tf_op jit(solution)/shard_map/ppermute | solution.py:418
  6.8 1.2 %pack.3 = bf16[16,4096]{1,0:T(8,128)(2,1)S(1)} custom-call(bf16[128,4096]{1,0:T(8,128)(2,1)} %refs_6_.12, bf16[128,4096]{1,0:T(8,128)(2,1)} %refs_7_.9, bf16[128,4096]{1,0:T(8,128)(2,1)} %refs_8_.7, bf16[128,4096]{1,0:T(8,128)(2,1)} %refs_6_.15), custom_call_target="tpu_custom_call" | custom-call | bytes 655360 | tf_op jit(solution)/shard_map/pack/pallas_call | solution.py:63
  8.0 1.3 %collective-permute-start.1 = (bf16[16,4096]{1,0:T(8,128)(2,1)S(1)}, bf16[16,4096]{1,0:T(8,128)(2,1)S(1)}, u32[]{:S(2)}, u32[]{:S(2)}) collective-permute-start(bf16[16,4096]{1,0:T(8,128)(2,1)S(1)} %pack.3), channel_id=1, source_target_pairs={{1,0},{2,1},{3,2},{4,3},{5,4},{6,5},{7,6},{8,7},{9,8},{10,9},{11,1... | collective-permute-start | bytes 393224 | tf_op jit(solution)/shard_map/ppermute | solution.py:419
  9.3 0.0 copy-start.12
  9.3 0.0 copy-start.11
  9.3 0.2 collective-permute-done.refs_0_.refs_2_.refs_1_
  9.5 3.6 %states.3 = (bf16[4,2,128,128]{3,2,1,0:T(8,128)(2,1)S(1)}, bf16[4,2,128,128]{3,2,1,0:T(8,128)(2,1)S(1)}, bf16[4,2,128,128]{3,2,1,0:T(8,128)(2,1)S(1)}, bf16[4,2,128,128]{3,2,1,0:T(8,128)(2,1)S(1)}, s32[1]{0:T(128)}) custom-call(s32[4]{0:T(128)S(1)} %broadcast_xor_fusion.cols, bf16[16,4096]{1,0:T(8,128)(2,1)S(1)} %collective-permute-done.refs_0_.refs_2_.refs_1_, ...), custom_call_target="tpu_custom_call" | custom-call | flops 134217728 | bytes 5472256 | tf_op jit(solution)/shard_map/states/pallas_call | solution.py:115
  13.2 2.6 %collective-permute-start.2 = (bf16[4,2,128,128]{3,2,1,0:T(8,128)(2,1)S(1)}, bf16[4,2,128,128]{3,2,1,0:T(8,128)(2,1)S(1)}, u32[]{:S(2)}, u32[]{:S(2)}) collective-permute-start(bf16[4,2,128,128]{3,2,1,0:T(8,128)(2,1)S(1)} %get-tuple-element.45), channel_id=1, source_target_pairs={{0,1},{1,0},{2,3},{3,2},{4,5},{5,4},{6,7},{7,6},{8,9},{9,8},{10,11... | collective-permute-start | bytes 786440 | tf_op jit(solution)/shard_map/ppermute | solution.py:415
  15.7 1.5 %collective-permute-start.3 = (bf16[4,2,128,128]{3,2,1,0:T(8,128)(2,1)S(1)}, bf16[4,2,128,128]{3,2,1,0:T(8,128)(2,1)S(1)}, u32[]{:S(2)}, u32[]{:S(2)}) collective-permute-start(bf16[4,2,128,128]{3,2,1,0:T(8,128)(2,1)S(1)} %get-tuple-element.48), channel_id=1, source_target_pairs={{0,2},{1,3},{2,0},{3,1},{4,6},{5,7},{6,4},{7,5},{8,10},{9,11},{10,... | collective-permute-start | bytes 786440 | tf_op jit(solution)/shard_map/ppermute | solution.py:415
  17.3 0.1 collective-permute-start.4
  17.3 1.2 %collective-permute-start.5 = (bf16[4,2,128,128]{3,2,1,0:T(8,128)(2,1)S(1)}, bf16[4,2,128,128]{3,2,1,0:T(8,128)(2,1)S(1)}, u32[]{:S(2)}, u32[]{:S(2)}) collective-permute-start(bf16[4,2,128,128]{3,2,1,0:T(8,128)(2,1)S(1)} %get-tuple-element.50), channel_id=1, source_target_pairs={{0,6},{1,7},{2,4},{3,5},{4,2},{5,3},{6,0},{7,1},{8,14},{9,15},{10,... | collective-permute-start | bytes 786440 | tf_op jit(solution)/shard_map/ppermute | solution.py:415
  18.5 3.3 %states.4 = (bf16[4,2,128,128]{3,2,1,0:T(8,128)(2,1)S(1)}, bf16[4,2,128,128]{3,2,1,0:T(8,128)(2,1)S(1)}, s32[1]{0:T(128)}) custom-call(s32[2]{0:T(128)S(1)} %broadcast_xor_fusion.3.cols, s32[1]{0:T(128)} %get-tuple-element.43.refs_0_, bf16[16,4096]{1,0:T(8,128)(2,1)S(1)} %collective-permute-done.1.refs_1_.refs_2_, ...), custom_call_target="tpu_custom_call" | custom-call | flops 67108864 | bytes 4947968 | tf_op jit(solution)/shard_map/states/pallas_call | solution.py:115
  21.9 2.1 %collective-permute-start.6 = (bf16[4,2,128,128]{3,2,1,0:T(8,128)(2,1)S(1)}, bf16[4,2,128,128]{3,2,1,0:T(8,128)(2,1)S(1)}, u32[]{:S(2)}, u32[]{:S(2)}) collective-permute-start(bf16[4,2,128,128]{3,2,1,0:T(8,128)(2,1)S(1)} %get-tuple-element.51), channel_id=1, source_target_pairs={{0,3},{1,2},{2,1},{3,0},{4,7},{5,6},{6,5},{7,4},{8,11},{9,10},{10,... | collective-permute-start | bytes 786440 | tf_op jit(solution)/shard_map/ppermute | solution.py:415
  24.0 0.6 collective-permute-start.7
  24.6 3.5 %states.5 = (bf16[4,2,128,128]{3,2,1,0:T(8,128)(2,1)}, bf16[4,2,128,128]{3,2,1,0:T(8,128)(2,1)S(1)}, s32[1]{0:T(128)}) custom-call(s32[2]{0:T(128)S(1)} %broadcast_xor_fusion.2.cols, s32[1]{0:T(128)} %get-tuple-element.44.refs_0_, bf16[4,2,128,128]{3,2,1,0:T(8,128)(2,1)S(1)} %collective-permute-done.2.refs_1_.refs_2_, ...), custom_call_target="tpu_custom_call" | custom-call | flops 67108864 | bytes 4947968 | tf_op jit(solution)/shard_map/states/pallas_call | solution.py:115
  28.1 1.5 %collective-permute-start.8 = (bf16[4,2,128,128]{3,2,1,0:T(8,128)(2,1)}, bf16[4,2,128,128]{3,2,1,0:T(8,128)(2,1)S(1)}, u32[]{:S(2)}, u32[]{:S(2)}) collective-permute-start(bf16[4,2,128,128]{3,2,1,0:T(8,128)(2,1)} %get-tuple-element.53), channel_id=1, source_target_pairs={{0,4},{1,5},{2,6},{3,7},{4,0},{5,1},{6,2},{7,3},{8,12},{9,13},{10,... | collective-permute-start | bytes 786440 | tf_op jit(solution)/shard_map/ppermute | solution.py:415
  29.7 0.1 pad_add_fusion.cols
  29.7 7.3 %intra.2 = (bf16[4,4,3,144,128]{4,3,2,1,0:T(8,128)(2,1)}, bf16[4,3,16,512]{3,2,1,0:T(8,128)(2,1)}, bf16[4,2,128,512]{3,2,1,0:T(8,128)(2,1)}, s32[1]{0:T(128)}) custom-call(s32[4]{0:T(128)S(1)} %broadcast_xor_fusion.cols, s32[1]{0:T(128)} %get-tuple-element.46.refs_0_, bf16[16,4096]{1,0:T(8,128)(2,1)S(1)} %collective-permute-done.refs_0_.refs_2_.refs_1_, ...), custom_call_target="tpu_custom_call" | custom-call | flops 402653184 | bytes 7569408 | tf_op jit(solution)/shard_map/intra/pallas_call | solution.py:115
  37.1 0.0 copy-start.10
  37.1 2.1 %collective-permute-done.5.refs_4_.refs_5_ = bf16[4,2,128,128]{3,2,1,0:T(8,128)(2,1)S(1)} collective-permute-done((bf16[4,2,128,128]{3,2,1,0:T(8,128)(2,1)S(1)}, bf16[4,2,128,128]{3,2,1,0:T(8,128)(2,1)S(1)}, u32[]{:S(2)}, u32[]{:S(2)}) %collective-permute-start.5) | collective-permute-done | bytes 262176 | tf_op jit(solution)/shard_map/ppermute | solution.py:415
  39.2 1.7 %sums.1 = (bf16[4,128,128]{2,1,0:T(8,128)(2,1)S(1)}, bf16[4,128,128]{2,1,0:T(8,128)(2,1)S(1)}, s32[1]{0:T(128)}) custom-call(s32[2]{0:T(128)S(1)} %pad_add_fusion.cols, s32[1]{0:T(128)} %get-tuple-element.47.refs_0_, bf16[4,2,128,128]{3,2,1,0:T(8,128)(2,1)S(1)} %collective-permute-done.2.refs_1_.refs_2_, ...), custom_call_target="tpu_custom_call" | custom-call | bytes 2359296 | tf_op jit(solution)/shard_map/sums/pallas_call | solution.py:115
  40.9 3.3 %collective-permute-start.11 = (bf16[4,128,128]{2,1,0:T(8,128)(2,1)S(1)}, bf16[4,128,128]{2,1,0:T(8,128)(2,1)S(1)}, u32[]{:S(2)}, u32[]{:S(2)}) collective-permute-start(bf16[4,128,128]{2,1,0:T(8,128)(2,1)S(1)} %get-tuple-element.61), channel_id=1, source_target_pairs={{0,24},{8,16},{16,8},{24,0},{1,25},{9,17},{17,9},{25,1},{2,26},{10... | collective-permute-start | bytes 393224 | tf_op jit(solution)/shard_map/ppermute | solution.py:415
  44.1 1.2 %collective-permute-start.9 = (bf16[4,128,128]{2,1,0:T(8,128)(2,1)S(1)}, bf16[4,128,128]{2,1,0:T(8,128)(2,1)S(1)}, u32[]{:S(2)}, u32[]{:S(2)}) collective-permute-start(bf16[4,128,128]{2,1,0:T(8,128)(2,1)S(1)} %get-tuple-element.60), channel_id=1, source_target_pairs={{0,8},{8,0},{16,24},{24,16},{1,9},{9,1},{17,25},{25,17},{2,10},{10... | collective-permute-start | bytes 393224 | tf_op jit(solution)/shard_map/ppermute | solution.py:415
  45.4 7.3 %intra.3 = (bf16[4,4,3,144,128]{4,3,2,1,0:T(8,128)(2,1)}, bf16[4,3,16,512]{3,2,1,0:T(8,128)(2,1)}, bf16[4,2,128,512]{3,2,1,0:T(8,128)(2,1)}, s32[1]{0:T(128)}) custom-call(s32[4]{0:T(128)S(1)} %broadcast_xor_fusion.1.cols, s32[1]{0:T(128)} %get-tuple-element.55.refs_0_, bf16[16,4096]{1,0:T(8,128)(2,1)S(1)} %collective-permute-done.refs_0_.refs_2_.refs_1_, ...), custom_call_target="tpu_custom_call" | custom-call | flops 402653184 | bytes 7569408 | tf_op jit(solution)/shard_map/intra/pallas_call | solution.py:115
  52.7 0.2 collective-permute-done.9.refs_9_.refs_10_
  52.9 2.6 %collective-permute-done.10.refs_10_.refs_11_ = bf16[4,128,128]{2,1,0:T(8,128)(2,1)S(1)} collective-permute-done((bf16[4,128,128]{2,1,0:T(8,128)(2,1)S(1)}, bf16[4,128,128]{2,1,0:T(8,128)(2,1)S(1)}, u32[]{:S(2)}, u32[]{:S(2)}) %collective-permute-start.10) | collective-permute-done | bytes 131104 | tf_op jit(solution)/shard_map/ppermute | solution.py:415
  55.5 2.0 %members.2 = (bf16[4,2,128,128]{3,2,1,0:T(8,128)(2,1)S(1)}, bf16[4,2,128,128]{3,2,1,0:T(8,128)(2,1)S(1)}, bf16[4,2,128,128]{3,2,1,0:T(8,128)(2,1)S(1)}, bf16[4,2,128,128]{3,2,1,0:T(8,128)(2,1)S(1)}, s32[1]{0:T(128)}) custom-call(s32[2]{0:T(128)S(1)} %pad_add_fusion.cols, s32[1]{0:T(128)} %get-tuple-element.59.refs_0_, ...), custom_call_target="tpu_custom_call" | custom-call | bytes 3538944 | tf_op jit(solution)/shard_map/members/pallas_call | solution.py:115
  57.6 0.0 copy-start
  57.6 1.6 %collective-permute-start.12 = (bf16[4,2,128,128]{3,2,1,0:T(8,128)(2,1)S(1)}, bf16[4,2,128,128]{3,2,1,0:T(8,128)(2,1)S(1)}, u32[]{:S(2)}, u32[]{:S(2)}) collective-permute-start(bf16[4,2,128,128]{3,2,1,0:T(8,128)(2,1)S(1)} %get-tuple-element.63), channel_id=1, source_target_pairs={{0,1},{1,0},{2,3},{3,2},{4,5},{5,4},{6,7},{7,6},{8,9},{9,8},{10,11... | collective-permute-start | bytes 786440 | tf_op jit(solution)/shard_map/ppermute | solution.py:415
  59.2 2.1 %collective-permute-start.16 = (bf16[4,2,128,128]{3,2,1,0:T(8,128)(2,1)S(1)}, bf16[4,2,128,128]{3,2,1,0:T(8,128)(2,1)S(1)}, u32[]{:S(2)}, u32[]{:S(2)}) collective-permute-start(bf16[4,2,128,128]{3,2,1,0:T(8,128)(2,1)S(1)} %get-tuple-element.71), channel_id=1, source_target_pairs={{0,2},{1,3},{2,0},{3,1},{4,6},{5,7},{6,4},{7,5},{8,10},{9,11},{10,... | collective-permute-start | bytes 786440 | tf_op jit(solution)/shard_map/ppermute | solution.py:415
  61.3 0.5 collective-permute-start.17
  61.9 0.6 collective-permute-start.18
  62.5 4.4 %collective-permute-done.12.refs_1_.refs_7_ = bf16[4,2,128,128]{3,2,1,0:T(8,128)(2,1)S(1)} collective-permute-done((bf16[4,2,128,128]{3,2,1,0:T(8,128)(2,1)S(1)}, bf16[4,2,128,128]{3,2,1,0:T(8,128)(2,1)S(1)}, u32[]{:S(2)}, u32[]{:S(2)}) %collective-permute-start.12) | collective-permute-done | bytes 262176 | tf_op jit(solution)/shard_map/ppermute | solution.py:415
  66.9 2.2 %members.3 = (bf16[4,2,128,128]{3,2,1,0:T(8,128)(2,1)S(1)}, bf16[4,2,128,128]{3,2,1,0:T(8,128)(2,1)S(1)}, bf16[4,2,128,128]{3,2,1,0:T(8,128)(2,1)S(1)}, bf16[4,2,128,128]{3,2,1,0:T(8,128)(2,1)S(1)}, s32[1]{0:T(128)}) custom-call(s32[2]{0:T(128)S(1)} %pad_add_fusion.cols, s32[1]{0:T(128)} %get-tuple-element.62.refs_0_, ...), custom_call_target="tpu_custom_call" | custom-call | bytes 3538944 | tf_op jit(solution)/shard_map/members/pallas_call | solution.py:115
  69.1 0.1 collective-permute-start.15
  69.1 3.2 %collective-permute-start.13 = (bf16[4,2,128,128]{3,2,1,0:T(8,128)(2,1)S(1)}, bf16[4,2,128,128]{3,2,1,0:T(8,128)(2,1)S(1)}, u32[]{:S(2)}, u32[]{:S(2)}) collective-permute-start(bf16[4,2,128,128]{3,2,1,0:T(8,128)(2,1)S(1)} %get-tuple-element.64), channel_id=1, source_target_pairs={{0,3},{1,2},{2,1},{3,0},{4,7},{5,6},{6,5},{7,4},{8,11},{9,10},{10,... | collective-permute-start | bytes 786440 | tf_op jit(solution)/shard_map/ppermute | solution.py:415
  72.3 0.1 collective-permute-start.14
  72.4 0.3 collective-permute-done.18.refs_10_
  72.8 3.9 %grads.3 = (bf16[128,4096]{1,0:T(8,128)(2,1)}, bf16[128,4096]{1,0:T(8,128)(2,1)}, bf16[128,4096]{1,0:T(8,128)(2,1)}, s32[1]{0:T(128)}) custom-call(s32[4]{0:T(128)S(1)} %broadcast_xor_fusion.cols, bf16[4,4096]{1,0:T(4,128)(2,1)S(1)} %copy-done.3, bf16[4,4096]{1,0:T(4,128)(2,1)S(1)} %copy-done.4, bf16[4,4096]{1,0:T(4,128)(2,1)S(1)} %copy-done.5, ...), custom_call_target="tpu_custom_call" | custom-call | flops 226492416 | bytes 8355840 | tf_op jit(solution)/shard_map/grads/pallas_call | solution.py:115
  76.7 2.8 %grads.4 = (bf16[128,4096]{1,0:T(8,128)(2,1)}, bf16[128,4096]{1,0:T(8,128)(2,1)}, bf16[128,4096]{1,0:T(8,128)(2,1)}, s32[1]{0:T(128)}) custom-call(s32[2]{0:T(128)S(1)} %broadcast_xor_fusion.2.cols, bf16[4,4096]{1,0:T(4,128)(2,1)S(1)} %copy-done.3, bf16[4,4096]{1,0:T(4,128)(2,1)S(1)} %copy-done.4, ...), custom_call_target="tpu_custom_call", output_to_operand_aliasing={{0}: (10, {}), {1}: (11, {}), {2}: (12, {})} | custom-call | flops 113246208 | bytes 10977280 | tf_op jit(solution)/shard_map/grads/pallas_call | solution.py:115
  79.5 0.6 collective-permute-done.13.refs_7_
  80.1 4.8 %collective-permute-done.14.refs_8_ = bf16[4,2,128,128]{3,2,1,0:T(8,128)(2,1)S(1)} collective-permute-done((bf16[4,2,128,128]{3,2,1,0:T(8,128)(2,1)S(1)}, bf16[4,2,128,128]{3,2,1,0:T(8,128)(2,1)S(1)}, u32[]{:S(2)}, u32[]{:S(2)}) %collective-permute-start.14) | collective-permute-done | bytes 262176 | tf_op jit(solution)/shard_map/ppermute | solution.py:415
  84.9 2.8 %grads.5 = (bf16[128,4096]{1,0:T(8,128)(2,1)}, bf16[128,4096]{1,0:T(8,128)(2,1)}, bf16[128,4096]{1,0:T(8,128)(2,1)}, s32[1]{0:T(128)}) custom-call(s32[2]{0:T(128)S(1)} %broadcast_xor_fusion.3.cols, bf16[4,4096]{1,0:T(4,128)(2,1)S(1)} %copy-done.3, bf16[4,4096]{1,0:T(4,128)(2,1)S(1)} %copy-done.4, ...), custom_call_target="tpu_custom_call", output_to_operand_aliasing={{0}: (10, {}), {1}: (11, {}), {2}: (12, {})} | custom-call | flops 113246208 | bytes 10977280 | tf_op jit(solution)/shard_map/grads/pallas_call | solution.py:115
  (36 shorter events, 0.1 us)
Async XLA Ops:
  1.7 7.5 %copy-start.13 = (s32[4]{0:T(128)S(1)}, s32[4]{0:T(128)}, u32[]{:S(2)}) copy-start(s32[4]{0:T(128)} %constant.24.clone) | copy-start | bytes 52
  1.8 7.8 %copy-start.3 = (bf16[4,4096]{1,0:T(4,128)(2,1)S(1)}, bf16[4,4096]{1,0:T(4,128)(2,1)}, u32[]{:S(2)}) copy-start(bf16[4,4096]{1,0:T(4,128)(2,1)} %refs_0_.9) | copy-start | bytes 98308
  1.8 7.7 %copy-start.4 = (bf16[4,4096]{1,0:T(4,128)(2,1)S(1)}, bf16[4,4096]{1,0:T(4,128)(2,1)}, u32[]{:S(2)}) copy-start(bf16[4,4096]{1,0:T(4,128)(2,1)} %refs_1_.11) | copy-start | bytes 98308
  1.8 7.7 %copy-start.5 = (bf16[4,4096]{1,0:T(4,128)(2,1)S(1)}, bf16[4,4096]{1,0:T(4,128)(2,1)}, u32[]{:S(2)}) copy-start(bf16[4,4096]{1,0:T(4,128)(2,1)} %refs_2_.11) | copy-start | bytes 98308
  1.8 7.7 %collective-permute-start = (bf16[16,4096]{1,0:T(8,128)(2,1)S(1)}, bf16[16,4096]{1,0:T(8,128)(2,1)S(1)}, u32[]{:S(2)}, u32[]{:S(2)}) collective-permute-start(bf16[16,4096]{1,0:T(8,128)(2,1)S(1)} %pack.2), channel_id=1, source_target_pairs={{0,1},{1,2},{2,3},{3,4},{4,5},{5,6},{6,7},{7,8},{8,9},{9,10},{10,1... | collective-permute-start | bytes 393224 | tf_op jit(solution)/shard_map/ppermute | solution.py:418
  8.0 10.5 %collective-permute-start.1 = (bf16[16,4096]{1,0:T(8,128)(2,1)S(1)}, bf16[16,4096]{1,0:T(8,128)(2,1)S(1)}, u32[]{:S(2)}, u32[]{:S(2)}) collective-permute-start(bf16[16,4096]{1,0:T(8,128)(2,1)S(1)} %pack.3), channel_id=1, source_target_pairs={{1,0},{2,1},{3,2},{4,3},{5,4},{6,5},{7,6},{8,7},{9,8},{10,9},{11,1... | collective-permute-start | bytes 393224 | tf_op jit(solution)/shard_map/ppermute | solution.py:419
  9.3 8.0 %copy-start.12 = (s32[2]{0:T(128)S(1)}, s32[2]{0:T(128)}, u32[]{:S(2)}) copy-start(s32[2]{0:T(128)} %constant.25.clone) | copy-start | bytes 28
  9.3 7.9 %copy-start.11 = (s32[2]{0:T(128)S(1)}, s32[2]{0:T(128)}, u32[]{:S(2)}) copy-start(s32[2]{0:T(128)} %constant.26.clone) | copy-start | bytes 28
  13.2 10.8 %collective-permute-start.2 = (bf16[4,2,128,128]{3,2,1,0:T(8,128)(2,1)S(1)}, bf16[4,2,128,128]{3,2,1,0:T(8,128)(2,1)S(1)}, u32[]{:S(2)}, u32[]{:S(2)}) collective-permute-start(bf16[4,2,128,128]{3,2,1,0:T(8,128)(2,1)S(1)} %get-tuple-element.45), channel_id=1, source_target_pairs={{0,1},{1,0},{2,3},{3,2},{4,5},{5,4},{6,7},{7,6},{8,9},{9,8},{10,11... | collective-permute-start | bytes 786440 | tf_op jit(solution)/shard_map/ppermute | solution.py:415
  15.7 12.4 %collective-permute-start.3 = (bf16[4,2,128,128]{3,2,1,0:T(8,128)(2,1)S(1)}, bf16[4,2,128,128]{3,2,1,0:T(8,128)(2,1)S(1)}, u32[]{:S(2)}, u32[]{:S(2)}) collective-permute-start(bf16[4,2,128,128]{3,2,1,0:T(8,128)(2,1)S(1)} %get-tuple-element.48), channel_id=1, source_target_pairs={{0,2},{1,3},{2,0},{3,1},{4,6},{5,7},{6,4},{7,5},{8,10},{9,11},{10,... | collective-permute-start | bytes 786440 | tf_op jit(solution)/shard_map/ppermute | solution.py:415
  17.3 19.8 %collective-permute-start.4 = (bf16[4,2,128,128]{3,2,1,0:T(8,128)(2,1)S(1)}, bf16[4,2,128,128]{3,2,1,0:T(8,128)(2,1)S(1)}, u32[]{:S(2)}, u32[]{:S(2)}) collective-permute-start(bf16[4,2,128,128]{3,2,1,0:T(8,128)(2,1)S(1)} %get-tuple-element.49), channel_id=1, source_target_pairs={{0,5},{1,4},{2,7},{3,6},{4,1},{5,0},{6,3},{7,2},{8,13},{9,12},{10,... | collective-permute-start | bytes 786440 | tf_op jit(solution)/shard_map/ppermute | solution.py:415
  17.3 21.8 %collective-permute-start.5 = (bf16[4,2,128,128]{3,2,1,0:T(8,128)(2,1)S(1)}, bf16[4,2,128,128]{3,2,1,0:T(8,128)(2,1)S(1)}, u32[]{:S(2)}, u32[]{:S(2)}) collective-permute-start(bf16[4,2,128,128]{3,2,1,0:T(8,128)(2,1)S(1)} %get-tuple-element.50), channel_id=1, source_target_pairs={{0,6},{1,7},{2,4},{3,5},{4,2},{5,3},{6,0},{7,1},{8,14},{9,15},{10,... | collective-permute-start | bytes 786440 | tf_op jit(solution)/shard_map/ppermute | solution.py:415
  21.9 17.3 %collective-permute-start.6 = (bf16[4,2,128,128]{3,2,1,0:T(8,128)(2,1)S(1)}, bf16[4,2,128,128]{3,2,1,0:T(8,128)(2,1)S(1)}, u32[]{:S(2)}, u32[]{:S(2)}) collective-permute-start(bf16[4,2,128,128]{3,2,1,0:T(8,128)(2,1)S(1)} %get-tuple-element.51), channel_id=1, source_target_pairs={{0,3},{1,2},{2,1},{3,0},{4,7},{5,6},{6,5},{7,4},{8,11},{9,10},{10,... | collective-permute-start | bytes 786440 | tf_op jit(solution)/shard_map/ppermute | solution.py:415
  24.0 15.2 %collective-permute-start.7 = (bf16[4,2,128,128]{3,2,1,0:T(8,128)(2,1)S(1)}, bf16[4,2,128,128]{3,2,1,0:T(8,128)(2,1)S(1)}, u32[]{:S(2)}, u32[]{:S(2)}) collective-permute-start(bf16[4,2,128,128]{3,2,1,0:T(8,128)(2,1)S(1)} %get-tuple-element.52), channel_id=1, source_target_pairs={{0,7},{1,6},{2,5},{3,4},{4,3},{5,2},{6,1},{7,0},{8,15},{9,14},{10,... | collective-permute-start | bytes 786440 | tf_op jit(solution)/shard_map/ppermute | solution.py:415
  28.1 11.1 %collective-permute-start.8 = (bf16[4,2,128,128]{3,2,1,0:T(8,128)(2,1)}, bf16[4,2,128,128]{3,2,1,0:T(8,128)(2,1)S(1)}, u32[]{:S(2)}, u32[]{:S(2)}) collective-permute-start(bf16[4,2,128,128]{3,2,1,0:T(8,128)(2,1)} %get-tuple-element.53), channel_id=1, source_target_pairs={{0,4},{1,5},{2,6},{3,7},{4,0},{5,1},{6,2},{7,3},{8,12},{9,13},{10,... | collective-permute-start | bytes 786440 | tf_op jit(solution)/shard_map/ppermute | solution.py:415
  37.1 8.3 %copy-start.10 = (s32[4]{0:T(128)S(1)}, s32[4]{0:T(128)}, u32[]{:S(2)}) copy-start(s32[4]{0:T(128)} %constant.27.clone) | copy-start | bytes 52
  40.9 12.0 %collective-permute-start.11 = (bf16[4,128,128]{2,1,0:T(8,128)(2,1)S(1)}, bf16[4,128,128]{2,1,0:T(8,128)(2,1)S(1)}, u32[]{:S(2)}, u32[]{:S(2)}) collective-permute-start(bf16[4,128,128]{2,1,0:T(8,128)(2,1)S(1)} %get-tuple-element.61), channel_id=1, source_target_pairs={{0,24},{8,16},{16,8},{24,0},{1,25},{9,17},{17,9},{25,1},{2,26},{10... | collective-permute-start | bytes 393224 | tf_op jit(solution)/shard_map/ppermute | solution.py:415
  44.1 11.4 %collective-permute-start.10 = (bf16[4,128,128]{2,1,0:T(8,128)(2,1)S(1)}, bf16[4,128,128]{2,1,0:T(8,128)(2,1)S(1)}, u32[]{:S(2)}, u32[]{:S(2)}) collective-permute-start(bf16[4,128,128]{2,1,0:T(8,128)(2,1)S(1)} %get-tuple-element.61), channel_id=1, source_target_pairs={{0,16},{8,24},{16,0},{24,8},{1,17},{9,25},{17,1},{25,9},{2,18},{10... | collective-permute-start | bytes 393224 | tf_op jit(solution)/shard_map/ppermute | solution.py:415
  44.1 8.7 %collective-permute-start.9 = (bf16[4,128,128]{2,1,0:T(8,128)(2,1)S(1)}, bf16[4,128,128]{2,1,0:T(8,128)(2,1)S(1)}, u32[]{:S(2)}, u32[]{:S(2)}) collective-permute-start(bf16[4,128,128]{2,1,0:T(8,128)(2,1)S(1)} %get-tuple-element.60), channel_id=1, source_target_pairs={{0,8},{8,0},{16,24},{24,16},{1,9},{9,1},{17,25},{25,17},{2,10},{10... | collective-permute-start | bytes 393224 | tf_op jit(solution)/shard_map/ppermute | solution.py:415
  55.5 17.2 %copy-start.6 = (bf16[4,4,3,144,128]{4,3,2,1,0:T(8,128)(2,1)S(1)}, bf16[4,4,3,144,128]{4,3,2,1,0:T(8,128)(2,1)}, u32[]{:S(2)}) copy-start(bf16[4,4,3,144,128]{4,3,2,1,0:T(8,128)(2,1)} %get-tuple-element.68.refs_3_) | copy-start | bytes 5308420
  57.6 15.2 %copy-start = (bf16[128,4096]{1,0:T(8,128)(2,1)S(1)}, bf16[128,4096]{1,0:T(8,128)(2,1)}, u32[]{:S(2)}) copy-start(bf16[128,4096]{1,0:T(8,128)(2,1)} %refs_6_.15) | copy-start | bytes 3145732
  57.6 15.2 %copy-start.7 = (bf16[4,2,128,512]{3,2,1,0:T(8,128)(2,1)S(1)}, bf16[4,2,128,512]{3,2,1,0:T(8,128)(2,1)}, u32[]{:S(2)}) copy-start(bf16[4,2,128,512]{3,2,1,0:T(8,128)(2,1)} %get-tuple-element.70.refs_5_) | copy-start | bytes 3145732
  57.6 15.2 %copy-start.9 = (bf16[4,3,16,512]{3,2,1,0:T(8,128)(2,1)S(1)}, bf16[4,3,16,512]{3,2,1,0:T(8,128)(2,1)}, u32[]{:S(2)}) copy-start(bf16[4,3,16,512]{3,2,1,0:T(8,128)(2,1)} %get-tuple-element.69.refs_4_) | copy-start | bytes 589828
  57.6 9.2 %collective-permute-start.12 = (bf16[4,2,128,128]{3,2,1,0:T(8,128)(2,1)S(1)}, bf16[4,2,128,128]{3,2,1,0:T(8,128)(2,1)S(1)}, u32[]{:S(2)}, u32[]{:S(2)}) collective-permute-start(bf16[4,2,128,128]{3,2,1,0:T(8,128)(2,1)S(1)} %get-tuple-element.63), channel_id=1, source_target_pairs={{0,1},{1,0},{2,3},{3,2},{4,5},{5,4},{6,7},{7,6},{8,9},{9,8},{10,11... | collective-permute-start | bytes 786440 | tf_op jit(solution)/shard_map/ppermute | solution.py:415
  59.2 13.1 %collective-permute-start.16 = (bf16[4,2,128,128]{3,2,1,0:T(8,128)(2,1)S(1)}, bf16[4,2,128,128]{3,2,1,0:T(8,128)(2,1)S(1)}, u32[]{:S(2)}, u32[]{:S(2)}) collective-permute-start(bf16[4,2,128,128]{3,2,1,0:T(8,128)(2,1)S(1)} %get-tuple-element.71), channel_id=1, source_target_pairs={{0,2},{1,3},{2,0},{3,1},{4,6},{5,7},{6,4},{7,5},{8,10},{9,11},{10,... | collective-permute-start | bytes 786440 | tf_op jit(solution)/shard_map/ppermute | solution.py:415
  61.3 11.1 %collective-permute-start.17 = (bf16[4,2,128,128]{3,2,1,0:T(8,128)(2,1)S(1)}, bf16[4,2,128,128]{3,2,1,0:T(8,128)(2,1)S(1)}, u32[]{:S(2)}, u32[]{:S(2)}) collective-permute-start(bf16[4,2,128,128]{3,2,1,0:T(8,128)(2,1)S(1)} %get-tuple-element.72), channel_id=1, source_target_pairs={{0,5},{1,4},{2,7},{3,6},{4,1},{5,0},{6,3},{7,2},{8,13},{9,12},{10,... | collective-permute-start | bytes 786440 | tf_op jit(solution)/shard_map/ppermute | solution.py:415
  61.9 10.9 %collective-permute-start.18 = (bf16[4,2,128,128]{3,2,1,0:T(8,128)(2,1)S(1)}, bf16[4,2,128,128]{3,2,1,0:T(8,128)(2,1)S(1)}, u32[]{:S(2)}, u32[]{:S(2)}) collective-permute-start(bf16[4,2,128,128]{3,2,1,0:T(8,128)(2,1)S(1)} %get-tuple-element.73), channel_id=1, source_target_pairs={{0,6},{1,7},{2,4},{3,5},{4,2},{5,3},{6,0},{7,1},{8,14},{9,15},{10,... | collective-permute-start | bytes 786440 | tf_op jit(solution)/shard_map/ppermute | solution.py:415
  69.1 7.6 %collective-permute-start.15 = (bf16[4,2,128,128]{3,2,1,0:T(8,128)(2,1)S(1)}, bf16[4,2,128,128]{3,2,1,0:T(8,128)(2,1)S(1)}, u32[]{:S(2)}, u32[]{:S(2)}) collective-permute-start(bf16[4,2,128,128]{3,2,1,0:T(8,128)(2,1)S(1)} %get-tuple-element.66), channel_id=1, source_target_pairs={{0,4},{1,5},{2,6},{3,7},{4,0},{5,1},{6,2},{7,3},{8,12},{9,13},{10,... | collective-permute-start | bytes 786440 | tf_op jit(solution)/shard_map/ppermute | solution.py:415
  69.1 10.9 %collective-permute-start.13 = (bf16[4,2,128,128]{3,2,1,0:T(8,128)(2,1)S(1)}, bf16[4,2,128,128]{3,2,1,0:T(8,128)(2,1)S(1)}, u32[]{:S(2)}, u32[]{:S(2)}) collective-permute-start(bf16[4,2,128,128]{3,2,1,0:T(8,128)(2,1)S(1)} %get-tuple-element.64), channel_id=1, source_target_pairs={{0,3},{1,2},{2,1},{3,0},{4,7},{5,6},{6,5},{7,4},{8,11},{9,10},{10,... | collective-permute-start | bytes 786440 | tf_op jit(solution)/shard_map/ppermute | solution.py:415
  72.3 12.6 %collective-permute-start.14 = (bf16[4,2,128,128]{3,2,1,0:T(8,128)(2,1)S(1)}, bf16[4,2,128,128]{3,2,1,0:T(8,128)(2,1)S(1)}, u32[]{:S(2)}, u32[]{:S(2)}) collective-permute-start(bf16[4,2,128,128]{3,2,1,0:T(8,128)(2,1)S(1)} %get-tuple-element.65), channel_id=1, source_target_pairs={{0,7},{1,6},{2,5},{3,4},{4,3},{5,2},{6,1},{7,0},{8,15},{9,14},{10,... | collective-permute-start | bytes 786440 | tf_op jit(solution)/shard_map/ppermute | solution.py:415
  72.8 3.9 %copy-start.1 = (bf16[4,4,3,144,128]{4,3,2,1,0:T(8,128)(2,1)S(1)}, bf16[4,4,3,144,128]{4,3,2,1,0:T(8,128)(2,1)}, u32[]{:S(2)}) copy-start(bf16[4,4,3,144,128]{4,3,2,1,0:T(8,128)(2,1)} %get-tuple-element.56.refs_3_) | copy-start | bytes 5308420
  72.8 3.9 %copy-start.2 = (bf16[4,2,128,512]{3,2,1,0:T(8,128)(2,1)S(1)}, bf16[4,2,128,512]{3,2,1,0:T(8,128)(2,1)}, u32[]{:S(2)}) copy-start(bf16[4,2,128,512]{3,2,1,0:T(8,128)(2,1)} %get-tuple-element.58.refs_5_) | copy-start | bytes 3145732
  72.8 3.9 %copy-start.8 = (bf16[4,3,16,512]{3,2,1,0:T(8,128)(2,1)S(1)}, bf16[4,3,16,512]{3,2,1,0:T(8,128)(2,1)}, u32[]{:S(2)}) copy-start(bf16[4,3,16,512]{3,2,1,0:T(8,128)(2,1)} %get-tuple-element.57.refs_4_) | copy-start | bytes 589828
